TPU v7x, 1024 devices: a whole 4x8x16 slice. The times are simulated.
1024 devices in a mesh: gx: 32 (over x_lo, z), gy: 8 (over y), dev: 4 (over x_hi, core).
Axes of the slice: x: 4 (x_hi: 2, x_lo: 2; x = x_hi * 2 + x_lo), y: 8, z: 16, core: 2. Of those that a mesh axis runs over, the one named last changes fastest.
Arguments:
- activations: bfloat16 [9216, 512], P(('gy', 'gx'), 'dev'), may hold values from -6 to 6
- weight_in: bfloat16 [9216, 36864], P('gy', 'gx'), may hold values from -0.125 to 0.125
- weight_out: bfloat16 [36864, 9216], P('gx', 'gy'), may hold values from -0.0625 to 0.0625
- cotangent: bfloat16 [9216, 512], P(('gy', 'gx'), 'dev'), may hold values from -6 to 6
Outputs:
- outputs: bfloat16 [9216, 512], P(('gy', 'gx'), 'dev')
- grad_inputs: bfloat16 [9216, 512], P(('gy', 'gx'), 'dev')
- grad_weight_in: bfloat16 [9216, 36864], P(('gy', 'dev'), 'gx')
- grad_weight_out: bfloat16 [36864, 9216], P(('gx', 'dev'), 'gy')
All inputs are finite; a program needn't handle non-finite values.
Results may differ from a plain program's by a relative error of at most 0.0049.
Values may be sent and summed in bfloat16 or wider, within the bound.
No kernel may reach another device: no remote copies, remote signals or barrier semaphores. Data moves between devices by JAX's collectives and lax.ppermute only.
A program may use at most 32 MiB of HBM per device.

v0:
```python
import math

import jax
import jax.numpy as jnp
from jax import lax
from jax.sharding import PartitionSpec as P


def silu_slope(pre):
    sig = jax.nn.sigmoid(pre)
    return sig * (1.0 + pre * (1.0 - sig))


def contract_first(left, right):
    return lax.dot_general(
        left, right, (((0,), (0,)), ((), ())), preferred_element_type=jnp.float32
    )


def contract_last(left, right):
    return lax.dot_general(
        left, right, (((1,), (1,)), ((), ())), preferred_element_type=jnp.float32
    )


def gather_features(local):
    return lax.all_gather(local, "gx", axis=0, tiled=True)


def hidden_section(make_term, total_rows, finish):
    summed = lax.psum(make_term(0, total_rows), "gy")
    return (finish(summed), summed)


def feature_section(make_term, total_rows):
    share_rows = total_rows // lax.axis_size("gx")
    return lax.psum_scatter(
        make_term(jnp.int32(0), lax.axis_size("gx") * share_rows),
        "gx",
        scatter_dimension=0,
        tiled=True,
    ).astype(jnp.bfloat16)


def body(activations, weight_in, weight_out, cotangent):
    feat_rows = weight_in.shape[0]
    unit_rows = weight_in.shape[1]
    input_block = gather_features(activations)

    def pre_term(start, count):
        return contract_first(weight_in, input_block)

    def make_hidden(pre):
        return jax.nn.silu(pre).astype(jnp.bfloat16)

    hidden_block, kept_pre = hidden_section(pre_term, unit_rows, make_hidden)

    def out_term(start, count):
        return contract_first(weight_out, hidden_block)

    outputs = feature_section(out_term, feat_rows)
    grad_block = gather_features(cotangent)

    def back_term(start, count):
        return jnp.dot(weight_out, grad_block, preferred_element_type=jnp.float32)

    def make_grad(grad_hidden):
        return (grad_hidden * silu_slope(kept_pre)).astype(jnp.bfloat16)

    grad_pre_block, unused_sum = hidden_section(back_term, unit_rows, make_grad)

    def input_term(start, count):
        return jnp.dot(weight_in, grad_pre_block, preferred_element_type=jnp.float32)

    grad_inputs = feature_section(input_term, feat_rows)
    groups = lax.axis_size("dev")
    feat_own = feat_rows // groups
    unit_own = unit_rows // groups
    input_all, hidden_all, grad_all, grad_pre_all = (
        lax.all_gather(input_block, "dev", axis=1, tiled=True),
        lax.all_gather(hidden_block, "dev", axis=1, tiled=True),
        lax.all_gather(grad_block, "dev", axis=1, tiled=True),
        lax.all_gather(grad_pre_block, "dev", axis=1, tiled=True),
    )
    owner = lax.axis_index("dev")
    input_own = lax.dynamic_slice_in_dim(input_all, owner * feat_own, feat_own, 0)
    hidden_own = lax.dynamic_slice_in_dim(hidden_all, owner * unit_own, unit_own, 0)
    factor = 1.0 / math.sqrt(grad_all.shape[1])
    grad_weight_in = (contract_last(input_own, grad_pre_all) * factor).astype(jnp.bfloat16)
    grad_weight_out = (contract_last(hidden_own, grad_all) * factor).astype(jnp.bfloat16)
    return (outputs, grad_inputs, grad_weight_in, grad_weight_out)


def solution(mesh):
    return jax.shard_map(
        body,
        mesh=mesh,
        in_specs=(P(("gy", "gx"), "dev"), P("gy", "gx"), P("gx", "gy"), P(("gy", "gx"), "dev")),
        out_specs=(
            P(("gy", "gx"), "dev"),
            P(("gy", "gx"), "dev"),
            P(("gy", "dev"), "gx"),
            P(("gx", "dev"), "gy"),
        ),
        check_vma=False,
    )
```

profile of v0, /device:TPU:6, one launch (start us, length us, event | category | flops | bytes accessed | tf_op | source)
XLA Modules:
  0.0 404.1 jit_solution(17451151043047185206)
XLA Ops:
  8.0 0.0 copy-start
  8.0 0.0 all-reduce.7.cloned.1.call-start
  8.1 77.1 %all-gather = bf16[32,36,128]{2,1,0:T(8,128)(2,1)S(1)} all-gather(bf16[1,36,128]{2,1,0:T(8,128)(2,1)} %bitcast.21), channel_id=1, replica_groups=mesh['gx'=32,'gy'=8,'dev'=4] {'gx'}, dimensions={0}, use_global_device_ids=true | all-gather | bytes 304128 | tf_op jit(solution)/shard_map/all_gather | solution.py:27
  85.1 0.1 reshape.9
  85.2 0.0 copy-start.3
  85.2 65.3 %all-gather.1 = bf16[32,36,128]{2,1,0:T(8,128)(2,1)} all-gather(bf16[1,36,128]{2,1,0:T(8,128)(2,1)} %bitcast.22), channel_id=1, replica_groups=mesh['gx'=32,'gy'=8,'dev'=4] {'gx'}, dimensions={0}, use_global_device_ids=true | all-gather | bytes 304128 | tf_op jit(solution)/shard_map/all_gather | solution.py:27
  150.5 1.0 reshape.11
  151.5 0.0 copy-start.1
  151.5 1.7 fusion.6
  153.3 0.1 copy-done.1
  153.4 1.7 fusion.7
  155.0 0.0 all-reduce.7.cloned.1.call-update
  155.1 0.0 all-gather.7.cloned.1.call-start
  155.1 0.5 all-gather.7.cloned.1.call-update
  155.6 0.0 all-gather.9.cloned.1.call-start
  155.7 84.9 %all-reduce.7.cloned.1.call-done = (f32[1152,128]{1,0:T(8,128)}, f32[1152,128]{1,0:T(8,128)}) async-done(((f32[1152,128]{1,0:T(8,128)}, f32[1152,128]{1,0:T(8,128)}), (f32[1152,128]{1,0:T(8,128)}, f32[1152,128]{1,0:T(8,128)})) %all-reduce.7.cloned.1.call-update) | async-done | bytes 1179664 | tf_op jit(solution)/shard_map/psum | solution.py:31
  240.6 2.4 multiply_convert_fusion
  243.0 0.0 all-gather.9.cloned.1.call-update
  243.0 0.0 all-gather.13.cloned.1.call-start
  243.1 0.5 all-gather.13.cloned.1.call-update
  243.6 0.0 all-gather.11.cloned.1.call-start
  243.6 0.7 all-gather.11.cloned.1.call-update
  244.3 1.3 dynamic-slice
  246.3 0.0 copy-start.2
  246.3 2.0 convolution_bitcast_fusion
  248.4 1.4 convolution_bitcast_fusion.1
  249.8 138.8 %all-reduce.8 = (bf16[1152,128]{0,1:T(8,128)(2,1)S(1)}, bf16[1152,128]{0,1:T(8,128)(2,1)}) all-reduce(f32[1152,128]{0,1:T(8,128)} %convolution_bitcast_fusion.1, f32[1152,128]{0,1:T(8,128)S(1)} %convolution_bitcast_fusion), channel_id=2, replica_groups=mesh['gx'=32,'gy'=8,'dev'=4] {'gx'}, use_global_device_ids=true, to_apply=%region_1.2.clone | all-reduce | flops 294912 | bytes 1769472
  388.6 0.9 dynamic-slice_convert_fusion
  389.5 0.7 copy.12
  390.2 0.7 copy.13
  390.9 2.8 fusion
  393.7 2.8 fusion.1
  (11 shorter events, 0.0 us)
Async XLA Ops:
  8.0 143.5 %copy-start = (bf16[1152,1152]{1,0:T(8,128)(2,1)S(1)}, bf16[1152,1152]{1,0:T(8,128)(2,1)}, u32[]{:S(2)}) copy-start(bf16[1152,1152]{1,0:T(8,128)(2,1)} %param.5) | copy-start | bytes 7962628
  8.0 232.6 %all-reduce.7.cloned.1.call-start = ((), (), s32[]{:S(2)}) async-start(), calls=%async_computation.4 | async-start | bytes 2359296 | tf_op jit(solution)/shard_map/psum | solution.py:31
  85.2 68.1 %copy-start.3 = (bf16[1152,128]{1,0:T(8,128)(2,1)}, bf16[1152,128]{1,0:T(8,128)(2,1)S(1)}, u32[]{:S(2)}) copy-start(bf16[1152,128]{1,0:T(8,128)(2,1)S(1)} %reshape.9) | copy-start | bytes 884740
  151.5 1.8 copy-start.5
  151.5 1.9 copy-start.1
  155.1 235.9 %all-gather.7.cloned.1.call-start = ((), (), s32[]{:S(2)}) async-start(), calls=%async_computation | async-start | bytes 1474560 | tf_op jit(solution)/shard_map/all_gather | solution.py:80
  155.6 235.3 %all-gather.9.cloned.1.call-start = ((), (), s32[]{:S(2)}) async-start(), calls=%async_computation.1 | async-start | bytes 1474560 | tf_op jit(solution)/shard_map/all_gather | solution.py:83
  243.0 150.7 %all-gather.13.cloned.1.call-start = ((), (), s32[]{:S(2)}) async-start(), calls=%async_computation.3 | async-start | bytes 1474560 | tf_op jit(solution)/shard_map/all_gather | solution.py:82
  243.6 150.1 %all-gather.11.cloned.1.call-start = ((), (), s32[]{:S(2)}) async-start(), calls=%async_computation.2 | async-start | bytes 1474560 | tf_op jit(solution)/shard_map/all_gather | solution.py:81
  246.3 2.1 copy-start.2
  246.3 2.1 copy-start.4
Sparse Core Ops, SparseCore 0:
  155.2 85.3 all-reduce.6
Sparse Core Ops, SparseCore 1:
  158.2 23.2 all-gather.6
  243.1 31.4 all-gather.8
  277.1 32.2 all-gather.12
  312.1 31.4 all-gather.10
where the time goes:
time: 405 us; the launch traced here: 404 us
  blocking collectives  281 us (69%)
  waiting for transfers between devices  86.7 us (21%)
  between operations  16.4 us (4%)
  matrix products  12.5 us (3%)
  local copies, waits for them, and re-layouts  4.84 us (1%)
    all_gather x2, blocking collectives, gather_features(): return lax.all_gather(local, 'gx', axis=0, tiled=True)  142 us
    unnamed x1, blocking collectives  139 us
    psum x1, waiting for transfers between devices, hidden_section(): summed = lax.psum(make_term(0, total_rows), 'gy')  84.9 us
  transfers between devices with their start and end apart: 5, of which 1 were waited for; matrix products, arithmetic and copies ran while one was open for 3% of the time, Pallas kernels for 0%

commit v1 on v0

v1 whole, which is shorter than its diff:
```python
import math

import jax
import jax.numpy as jnp
from jax import lax
from jax.sharding import Mesh, PartitionSpec as P

F32 = jnp.float32
BF16 = jnp.bfloat16


def silu_slope(pre):
    sig = jax.nn.sigmoid(pre)
    return sig * (1.0 + pre * (1.0 - sig))


def dot(left, right, contract):
    return lax.dot_general(left, right, (contract, ((), ())), preferred_element_type=F32)


def body(activations, weight_in, weight_out, cotangent):
    own, tokens = activations.shape
    feats, units = weight_in.shape
    n_gx = lax.axis_size("xl") * lax.axis_size("z")
    n_gy = lax.axis_size("gy")
    n_dev = lax.axis_size("xh") * lax.axis_size("core")
    share = units // n_gy

    pair = jnp.concatenate([activations, cotangent], axis=0)
    block = lax.all_gather(pair, "z", axis=0, tiled=False)
    block = lax.all_gather(block, "xl", axis=0, tiled=True)
    acts = block[:, :own].reshape(feats, tokens)
    cots = block[:, own:].reshape(feats, tokens)
    block_all = lax.all_gather(block, ("xh", "core"), axis=0, tiled=False)

    pre_part = dot(weight_in, acts, ((0,), (0,))).astype(BF16).reshape(n_gy, share, tokens)
    grad_part = dot(weight_out, cots, ((1,), (0,))).astype(BF16).reshape(n_gy, share, tokens)
    parts = lax.all_to_all(
        jnp.concatenate([pre_part, grad_part], axis=1), "gy", 0, 0, tiled=True
    )
    total = jnp.sum(parts.astype(F32), axis=0)
    pre, grad_hidden = total[:share], total[share:]
    hidden = jax.nn.silu(pre).astype(BF16)
    grad_pre = (grad_hidden * silu_slope(pre)).astype(BF16)
    both = lax.all_gather(jnp.concatenate([hidden, grad_pre], axis=0), "gy", axis=0, tiled=False)
    both_all = lax.all_gather(both, ("xh", "core"), axis=0, tiled=False)
    hidden_block = both[:, :share].reshape(units, tokens)
    grad_block = both[:, share:].reshape(units, tokens)

    out_part = dot(weight_out, hidden_block, ((0,), (0,))).astype(BF16).reshape(n_gx, own, tokens)
    in_part = dot(weight_in, grad_block, ((1,), (0,))).astype(BF16).reshape(n_gx, own, tokens)
    sums = lax.all_to_all(
        jnp.concatenate([out_part, in_part], axis=1), ("xl", "z"), 0, 0, tiled=True
    )
    sums = jnp.sum(sums.astype(F32), axis=0).astype(BF16)
    outputs, grad_inputs = sums[:own], sums[own:]

    owner = lax.axis_index("xh") * lax.axis_size("core") + lax.axis_index("core")
    rows = n_gx // n_dev
    acts_own = lax.dynamic_slice_in_dim(block_all, owner * rows, rows, 1)[:, :, :own]
    acts_own = acts_own.reshape(n_dev, rows * own, tokens)
    cots_all = block_all[:, :, own:].reshape(n_dev, feats, tokens)
    chunks = n_gy // n_dev
    hidden_own = lax.dynamic_slice_in_dim(both_all, owner * chunks, chunks, 1)[:, :, :share]
    hidden_own = hidden_own.reshape(n_dev, chunks * share, tokens)
    grads_all = both_all[:, :, share:].reshape(n_dev, units, tokens)
    factor = 1.0 / math.sqrt(n_dev * tokens)
    grad_weight_in = dot(acts_own, grads_all, ((0, 2), (0, 2)))
    grad_weight_out = dot(hidden_own, cots_all, ((0, 2), (0, 2)))
    return (
        outputs,
        grad_inputs,
        (grad_weight_in * factor).astype(BF16),
        (grad_weight_out * factor).astype(BF16),
    )


def solution(mesh):
    shape = mesh.devices.shape
    fine = Mesh(
        mesh.devices.reshape(2, shape[0] // 2, shape[1], 2, shape[2] // 2),
        ("xl", "z", "gy", "xh", "core"),
    )
    gx, dev = ("xl", "z"), ("xh", "core")
    return jax.shard_map(
        body,
        mesh=fine,
        in_specs=(P(("gy", *gx), dev), P("gy", gx), P(gx, "gy"), P(("gy", *gx), dev)),
        out_specs=(P(("gy", *gx), dev), P(("gy", *gx), dev), P(("gy", *dev), gx), P((*gx, *dev), "gy")),
        check_vma=False,
    )
```

time: 405 us -> 171 us (0.42)
  blocking collectives: 281 us -> 101 us
  waiting for transfers between devices: 86.7 us -> 23 us
  local copies, waits for them, and re-layouts: 4.84 us -> 14.7 us
  starting transfers between devices: 0.21 us -> 5.6 us
    unnamed x1 -> x0, blocking collectives: 139 us -> none
    psum x1 -> x0, waiting for transfers between devices: 84.9 us -> none  [hidden_section(): summed = lax.psum(make_term(0, total_rows), 'gy')]
    all_gather x2 -> x3, blocking collectives: 142 us -> 78.9 us  [the longest x1 43.8 us: body(): block = lax.all_gather(pair, 'z', axis=0, tiled=False)]
    all_to_all x0 -> x1, waiting for transfers between devices: none -> 23 us  [body(): lax.all_to_all(jnp.concatenate([out_part, in_part], axis=1), ('xl', 'z'),...]
    all_to_all x0 -> x1, blocking collectives: none -> 21.7 us  [body(): lax.all_to_all(jnp.concatenate([pre_part, grad_part], axis=1), 'gy', 0, 0...]
    slice x0 -> x9, local copies, waits for them, and re-layouts: none -> 10.6 us  [the longest x2 3.99 us: body(): cots_all = block_all[:, :, own:].reshape(n_dev, feats, tokens)]
    all_to_all x0 -> x1, starting transfers between devices: none -> 5.52 us  [body(): lax.all_to_all(jnp.concatenate([out_part, in_part], axis=1), ('xl', 'z'),...]
  transfers between devices with their start and end apart: 5 -> 3, of which waited for: 1 -> 1; matrix products, arithmetic and copies ran while one was open for 3% -> 12% of each run, Pallas kernels for 0% -> 0%
where the time goes in v1:
time: 171 us
  blocking collectives  101 us (59%)
  waiting for transfers between devices  23 us (13%)
  local copies, waits for them, and re-layouts  14.7 us (9%)
  between operations  14.2 us (8%)
  matrix products  9.54 us (6%)
  starting transfers between devices  5.6 us (3%)
  other arithmetic  3.07 us (2%)
    all_gather x1, blocking collectives, body(): block = lax.all_gather(pair, 'z', axis=0, tiled=False)  43.8 us
    all_gather x1, blocking collectives, body(): lax.all_gather(jnp.concatenate([hidden, grad_pre], axis=0), 'gy', axis=0,...  27.6 us
    all_to_all x1, waiting for transfers between devices, body(): lax.all_to_all(jnp.concatenate([out_part, in_part], axis=1), ('xl', 'z'),...  23 us
    all_to_all x1, blocking collectives, body(): lax.all_to_all(jnp.concatenate([pre_part, grad_part], axis=1), 'gy', 0, 0...  21.7 us
    dot_general x6, matrix products, dot(): lax.dot_general(left, right, (contract, ((), ())), preferred_element_type...  9.54 us
    all_gather x1, blocking collectives, body(): block = lax.all_gather(block, 'xl', axis=0, tiled=True)  7.49 us
    all_to_all x1, starting transfers between devices, body(): lax.all_to_all(jnp.concatenate([out_part, in_part], axis=1), ('xl', 'z'),...  5.52 us
    slice x2, local copies, waits for them, and re-layouts, body(): cots_all = block_all[:, :, own:].reshape(n_dev, feats, tokens)  3.99 us
  transfers between devices with their start and end apart: 3, of which 1 were waited for; matrix products, arithmetic and copies ran while one was open for 12% of the time, Pallas kernels for 0%

profile of v1, /device:TPU:6, one launch (start us, length us, event | category | flops | bytes accessed | tf_op | source)
XLA Modules:
  0.0 170.7 jit_solution(9280467306299205465)
XLA Ops:
  7.2 0.9 pad_maximum_fusion.3
  8.1 43.8 %all-gather = bf16[1152,128]{1,0:T(8,128)(2,1)S(1)} all-gather(bf16[72,128]{1,0:T(8,128)(2,1)S(1)} %pad_maximum_fusion.3), channel_id=2, replica_groups=mesh['xl'=2,'z'=16,'gy'=8,'xh'=2,'core'=2] {'z'}, dimensions={0}, use_global_device_ids=true | all-gather | bytes 313344 | tf_op jit(solution)/shard_map/all_gather | solution.py:30
  51.9 7.5 %all_gather.29 = bf16[32,72,128]{2,1,0:T(8,128)(2,1)} all-gather(bf16[16,72,128]{2,1,0:T(8,128)(2,1)S(1)} %bitcast.46), channel_id=1, replica_groups=mesh['xl'=2,'z'=16,'gy'=8,'xh'=2,'core'=2] {'xl'}, dimensions={0}, use_global_device_ids=true | all-gather | bytes 884736 | tf_op jit(solution)/shard_map/all_gather | solution.py:31
  59.5 1.2 fusion.12
  60.6 0.8 reshape.44
  61.4 2.5 %fusion.4 = bf16[1152,128]{0,1:T(8,128)(2,1)S(1)} fusion(bf16[1152,128]{1,0:T(8,128)(2,1)} %reshape.44, bf16[1152,1152]{1,0:T(8,128)(2,1)} %param.5), kind=kOutput, calls=%fused_computation.10 | convolution fusion | flops 339886080 | bytes 3244032 | tf_op jit(solution)/shard_map/dot_general | solution.py:18
  63.9 0.9 copy.22
  64.9 0.9 fusion.5
  65.8 0.2 copy.23
  66.0 1.0 pad_maximum_fusion
  67.0 21.7 %all_to_all.10 = bf16[8,288,128]{2,1,0:T(8,128)(2,1)S(1)} all-to-all(bf16[8,288,128]{2,1,0:T(8,128)(2,1)S(1)} %pad_maximum_fusion), channel_id=1, replica_groups=mesh['xl'=2,'z'=16,'gy'=8,'xh'=2,'core'=2] {'gy'}, dimensions={0} | all-to-all | bytes 1179648 | tf_op jit(solution)/shard_map/all_to_all | solution.py:38
  88.7 0.1 convert_reduce_fusion
  88.9 27.6 %all-gather.1 = bf16[2304,128]{1,0:T(8,128)(2,1)} all-gather(bf16[288,128]{1,0:T(8,128)(2,1)S(1)} %pad_maximum_fusion.2), channel_id=3, replica_groups=mesh['xl'=2,'z'=16,'gy'=8,'xh'=2,'core'=2] {'gy'}, dimensions={0}, use_global_device_ids=true | all-gather | bytes 663552 | tf_op jit(solution)/shard_map/all_gather | solution.py:45
  116.5 1.1 fusion.11
  117.6 0.6 fusion.6
  118.2 0.9 copy.24
  119.1 2.7 %fusion.7 = bf16[1152,128]{0,1:T(8,128)(2,1)S(1)} fusion(bf16[1152,128]{1,0:T(8,128)(2,1)S(1)} %bitcast.44, bf16[1152,1152]{1,0:T(8,128)(2,1)} %param.5), kind=kOutput, calls=%fused_computation.13 | convolution fusion | flops 339886080 | bytes 3244032 | tf_op jit(solution)/shard_map/dot_general | solution.py:18
  121.8 0.2 copy.25
  122.1 1.0 reshape.49
  123.1 1.0 pad_maximum_fusion.1
  124.1 5.5 %all-to-all-start.1 = ((bf16[32,72,128]{2,1,0:T(8,128)(2,1)}), bf16[32,72,128]{2,1,0:T(8,128)(2,1)S(1)}, u32[]{:S(2)}, u32[]{:S(2)}) async-start(bf16[32,72,128]{2,1,0:T(8,128)(2,1)} %pad_maximum_fusion.1), calls=%async_computation.1 | async-start | bytes 1179648 | tf_op jit(solution)/shard_map/all_to_all | solution.py:52
  129.6 23.0 %all-to-all-done.1 = bf16[32,72,128]{2,1,0:T(8,128)(2,1)S(1)} async-done(((bf16[32,72,128]{2,1,0:T(8,128)(2,1)}), bf16[32,72,128]{2,1,0:T(8,128)(2,1)S(1)}, u32[]{:S(2)}, u32[]{:S(2)}) %all-to-all-start.1) | async-done | bytes 589856 | tf_op jit(solution)/shard_map/all_to_all | solution.py:52
  152.6 0.1 reduce_sum.22
  152.7 0.6 fusion.13
  153.3 2.0 %slice.57 = bf16[4,32,36,128]{3,2,1,0:T(8,128)(2,1)S(1)} slice(bf16[4,32,72,128]{3,2,1,0:T(8,128)(2,1)} %bitcast.51), slice={[0:4], [0:32], [36:72], [0:128]} | slice | bytes 2359296 | tf_op jit(solution)/shard_map/slice | solution.py:62
  155.3 2.0 %copy.28 = bf16[4,32,36,128]{3,0,2,1:T(4,128)(2,1)} copy(bf16[4,32,36,128]{3,2,1,0:T(8,128)(2,1)S(1)} %slice.57) | data formatting | bytes 2359296 | tf_op jit(solution)/shard_map/slice | solution.py:62
  157.3 1.0 constant_dynamic-slice_fusion.1
  158.3 0.2 copy.26
  158.6 1.4 slice.56
  159.9 1.1 constant_dynamic-slice_fusion
  161.0 1.4 fusion.2
  162.5 1.4 fusion.3
  (14 shorter events, 0.3 us)
Async XLA Ops:
  7.2 57.7 %copy-start = (bf16[1152,1152]{1,0:T(8,128)(2,1)S(1)}, bf16[1152,1152]{1,0:T(8,128)(2,1)}, u32[]{:S(2)}) copy-start(bf16[1152,1152]{1,0:T(8,128)(2,1)} %param.6) | copy-start | bytes 7962628
  7.2 146.1 %all-gather.7.cloned.1.call-start = ((), (), s32[]{:S(2)}) async-start(), calls=%async_computation.2 | async-start | bytes 2949120 | tf_op jit(solution)/shard_map/all_gather | solution.py:34
  59.4 99.1 %all-gather.9.cloned.1.call-start = ((), (), s32[]{:S(2)}) async-start(), calls=%async_computation.3 | async-start | bytes 2949120 | tf_op jit(solution)/shard_map/all_gather | solution.py:46
  124.1 28.5 %all-to-all-start.1 = ((bf16[32,72,128]{2,1,0:T(8,128)(2,1)}), bf16[32,72,128]{2,1,0:T(8,128)(2,1)S(1)}, u32[]{:S(2)}, u32[]{:S(2)}) async-start(bf16[32,72,128]{2,1,0:T(8,128)(2,1)} %pad_maximum_fusion.1), calls=%async_computation.1 | async-start | bytes 1179648 | tf_op jit(solution)/shard_map/all_to_all | solution.py:52
  159.9 2.5 %copy-start.1 = (bf16[4,32,36,128]{3,0,2,1:T(4,128)(2,1)S(1)}, bf16[4,32,36,128]{3,0,2,1:T(4,128)(2,1)}, u32[]{:S(2)}) copy-start(bf16[4,32,36,128]{3,0,2,1:T(4,128)(2,1)} %copy.28) | copy-start | bytes 3538948
Sparse Core Ops, SparseCore 0:
  59.5 30.0 all-gather.6
  116.6 28.8 all-gather.8

commit v2 on v1

v2 whole, which is shorter than its diff:
```python
import functools
import math

import jax
import jax.numpy as jnp
from jax import lax
from jax.experimental import pallas as pl
from jax.experimental.pallas import tpu as pltpu
from jax.sharding import Mesh, PartitionSpec as P

F32 = jnp.float32
BF16 = jnp.bfloat16
GX = ("xl", "z")
DEV = ("xh", "core")
VMEM = pl.BlockSpec(memory_space=pltpu.VMEM)


def silu_slope(pre):
    sig = jax.nn.sigmoid(pre)
    return sig * (1.0 + pre * (1.0 - sig))


def dot(left, right, contract):
    return lax.dot_general(left, right, (contract, ((), ())), preferred_element_type=F32)


def turned(right):
    return right.astype(F32).T.astype(BF16)


class Weights:
    def __init__(self, rows_hbm, columns_hbm, rows_ref, columns_ref, sems):
        self.rows_ref, self.columns_ref = rows_ref, columns_ref
        self.width = rows_ref.shape[0] // sems.shape[1]
        self.parts = [pl.ds(c * self.width, self.width) for c in range(sems.shape[1])]
        self.rows = [
            pltpu.make_async_copy(rows_hbm.at[part], rows_ref.at[part], sems.at[0, c])
            for c, part in enumerate(self.parts)
        ]
        self.columns = [
            pltpu.make_async_copy(columns_hbm.at[:, part], columns_ref.at[:, part], sems.at[1, c])
            for c, part in enumerate(self.parts)
        ]
        for copy in self.rows + self.columns:
            copy.start()

    def rows_dot(self, right, to_ref):
        for part, copy in zip(self.parts, self.rows):
            copy.wait()
            to_ref[part] = dot(self.rows_ref[part], right, ((1,), (0,)))

    def columns_dot(self, left, to_ref):
        for part, copy in zip(self.parts, self.columns):
            copy.wait()
            to_ref[part] = dot(left, self.columns_ref[:, part], ((1,), (0,))).T


def unit_terms(block_ref, in_hbm, out_hbm, parts_ref, out_ref, in_ref, acts_ref, cots_ref, pair_ref, sems):
    weights = Weights(out_hbm, in_hbm, out_ref, in_ref, sems)
    own = block_ref.shape[1] // 2
    for g in range(block_ref.shape[0]):
        pair_ref[...] = block_ref[g].astype(F32)
        acts_ref[g * own : (g + 1) * own] = pair_ref[:own]
        cots_ref[g * own : (g + 1) * own] = pair_ref[own:]
    cots, acts = cots_ref[...].astype(BF16), turned(acts_ref[...])
    grad_ref, pre_ref = cots_ref, acts_ref
    weights.rows_dot(cots, grad_ref)
    weights.columns_dot(acts, pre_ref)
    share = parts_ref.shape[1] // 2
    for k in range(parts_ref.shape[0]):
        at = pl.ds(k * share, share)
        parts_ref[k, :share] = pre_ref[at].astype(BF16)
        parts_ref[k, share:] = grad_ref[at].astype(BF16)


def feature_terms(both_ref, in_hbm, out_hbm, sums_ref, in_ref, out_ref, out_rows_ref, in_rows_ref, pair_ref, sems):
    weights = Weights(in_hbm, out_hbm, in_ref, out_ref, sems)
    share = both_ref.shape[1] // 2
    shares = range(both_ref.shape[0])
    hidden = turned(jnp.concatenate([both_ref[k, :share] for k in shares], axis=0))
    grad = jnp.concatenate([both_ref[k, share:] for k in shares], axis=0)
    weights.rows_dot(grad, in_rows_ref)
    weights.columns_dot(hidden, out_rows_ref)
    own = sums_ref.shape[1] // 2
    for g in range(sums_ref.shape[0]):
        pair_ref[:own] = out_rows_ref[g * own : (g + 1) * own]
        pair_ref[own:] = in_rows_ref[g * own : (g + 1) * own]
        sums_ref[g] = pair_ref[...].astype(BF16)


def unpack(block_hbm, acts_out, cots_out, block_ref, acts_ref, cots_ref, pair_ref, sems):
    groups, members, rows, tokens = block_ref.shape
    own = rows // 2
    copies = [
        pltpu.make_async_copy(block_hbm.at[t], block_ref.at[t], sems.at[t]) for t in range(groups)
    ]
    for copy in copies:
        copy.start()
    owner = lax.axis_index(DEV)
    for t in range(groups):
        copies[t].wait()
        lanes = slice(t * tokens, (t + 1) * tokens)
        for g in range(members):
            pair_ref[...] = block_ref[t, g].astype(F32)
            cots_ref[g * own : (g + 1) * own] = pair_ref[own:]
        cots_out[:, lanes] = cots_ref[...].astype(BF16)
        for g in range(members // groups):
            pair_ref[...] = block_ref[t, owner * (members // groups) + g].astype(F32)
            acts_ref[g * own : (g + 1) * own] = pair_ref[:own]
        acts_out[:, lanes] = acts_ref[...].astype(BF16)


def weight_grads(factor, acts_ref, cots_ref, both_hbm, in_ref, out_ref, grads_ref, hidden_ref, sems):
    groups, _, share, _ = grads_ref.shape
    pieces = hidden_ref.shape[1]
    shares = grads_ref.shape[1]
    first = lax.axis_index(DEV) * pieces
    copies = [
        pltpu.make_async_copy(
            both_hbm.at[:, pl.ds(k, 2), pl.ds(share, share)], grads_ref.at[:, pl.ds(k, 2)], sems.at[k // 2]
        )
        for k in range(0, shares, 2)
    ]
    copies.append(
        pltpu.make_async_copy(
            both_hbm.at[:, pl.ds(first, pieces), pl.ds(0, share)], hidden_ref, sems.at[shares // 2]
        )
    )
    for copy in copies:
        copy.start()

    def beside(ref, at, count):
        return jnp.concatenate(
            [
                jnp.concatenate([ref[t, at + j] for j in range(count)], axis=0)
                for t in range(groups)
            ],
            axis=1,
        )

    acts = acts_ref[...]
    for k in (0, 2, 4, 6):
        copies[k // 2].wait()
    width = 384
    every = beside(grads_ref, 0, shares)
    for at in range(0, in_ref.shape[1], width):
        part = every[at : at + width]
        in_ref[:, at : at + width] = (dot(acts, part, ((1,), (1,))) * factor).astype(BF16)
    copies[-1].wait()
    hidden = beside(hidden_ref, 0, pieces)
    for at in range(0, out_ref.shape[1], width):
        part = cots_ref[at : at + width]
        out_ref[:, at : at + width] = (dot(hidden, part, ((1,), (1,))) * factor).astype(BF16)


def call(kernel, name, outs, scratch, n_sems, args, in_hbm, flops, vmem):
    n_bytes = sum(a.size * a.dtype.itemsize for a in args)
    return pl.pallas_call(
        kernel,
        out_shape=outs,
        in_specs=[pl.BlockSpec(memory_space=pltpu.HBM) if i in in_hbm else VMEM for i in range(len(args))],
        out_specs=jax.tree.map(lambda _: VMEM, outs),
        scratch_shapes=[pltpu.VMEM(*s) for s in scratch] + [pltpu.SemaphoreType.DMA(n_sems)],
        compiler_params=pltpu.CompilerParams(vmem_limit_bytes=vmem * 2**20),
        cost_estimate=pl.CostEstimate(flops=flops, bytes_accessed=n_bytes, transcendentals=0),
        name=name,
    )(*args)


def spread(local, axes):
    copies = jnp.broadcast_to(local[None], (lax.axis_size(axes), *local.shape))
    return lax.all_to_all(copies, axes, 0, 0, tiled=True)


def body(activations, weight_in, weight_out, cotangent):
    own, tokens = activations.shape
    feats, units = weight_in.shape
    n_gx, n_gy, n_dev = (lax.axis_size(a) for a in (GX, "gy", DEV))
    share = units // n_gy
    pair_rows = (2 * own, tokens)
    products = 4 * feats * units * tokens

    pair = jnp.concatenate([activations, cotangent], axis=0)
    block = lax.all_gather(pair, "z", axis=0, tiled=False)
    block = lax.all_gather(block, "xl", axis=0, tiled=True)
    block_all = lax.all_gather(block, DEV, axis=0, tiled=False)

    weight = (weight_in.shape, BF16)
    rows = ((feats, tokens), F32)
    parts = call(
        unit_terms,
        "unit_terms",
        jax.ShapeDtypeStruct((n_gy, 2 * share, tokens), BF16),
        [weight, weight, rows, rows, (pair_rows, F32)],
        (2, 3),
        (block, weight_in, weight_out),
        (1, 2),
        products,
        62,
    )
    parts = lax.all_to_all(parts, "gy", 0, 0, tiled=True)
    total = jnp.sum(parts.astype(F32), axis=0)
    pre, grad_hidden = total[:share], total[share:]
    hidden = jax.nn.silu(pre).astype(BF16)
    grad_pre = (grad_hidden * silu_slope(pre)).astype(BF16)
    both = spread(jnp.concatenate([hidden, grad_pre], axis=0), "gy").reshape(n_gy, 2 * share, tokens)
    both_all = lax.all_gather(both, DEV, axis=0, tiled=False)

    sums = call(
        feature_terms,
        "feature_terms",
        jax.ShapeDtypeStruct((n_gx, *pair_rows), BF16),
        [weight, weight, rows, rows, (pair_rows, F32)],
        (2, 3),
        (both, weight_in, weight_out),
        (1, 2),
        products,
        62,
    )
    sums = lax.all_to_all(sums, GX, 0, 0, tiled=True)
    sums = jnp.sum(sums.astype(F32), axis=0).astype(BF16)

    acts_own, cots_all = call(
        unpack,
        "unpack",
        (
            jax.ShapeDtypeStruct((feats // n_dev, n_dev * tokens), BF16),
            jax.ShapeDtypeStruct((feats, n_dev * tokens), BF16),
        ),
        [
            (block_all.shape, BF16),
            ((feats // n_dev, tokens), F32),
            ((feats, tokens), F32),
            (pair_rows, F32),
        ],
        (n_dev,),
        (block_all,),
        (0,),
        products,
        62,
    )
    grads = call(
        functools.partial(weight_grads, 1.0 / math.sqrt(n_dev * tokens)),
        "weight_grads",
        (
            jax.ShapeDtypeStruct((feats // n_dev, units), BF16),
            jax.ShapeDtypeStruct((units // n_dev, feats), BF16),
        ),
        [
            ((n_dev, n_gy, share, tokens), BF16),
            ((n_dev, n_gy // n_dev, share, tokens), BF16),
        ],
        (n_gy // 2 + 1,),
        (acts_own, cots_all, both_all),
        (2,),
        products,
        60,
    )
    return (sums[:own], sums[own:], *grads)


def solution(mesh):
    shape = mesh.devices.shape
    fine = Mesh(
        mesh.devices.reshape(2, shape[0] // 2, shape[1], 2, shape[2] // 2),
        ("xl", "z", "gy", "xh", "core"),
    )
    return jax.shard_map(
        body,
        mesh=fine,
        in_specs=(P(("gy", *GX), DEV), P("gy", GX), P(GX, "gy"), P(("gy", *GX), DEV)),
        out_specs=(P(("gy", *GX), DEV), P(("gy", *GX), DEV), P(("gy", *DEV), GX), P((*GX, *DEV), "gy")),
        check_vma=False,
    )
```

time: 171 us -> 152 us (0.89)
  Pallas kernels: 0 us -> 20.7 us
  local copies, waits for them, and re-layouts: 14.7 us -> 0.69 us
  blocking collectives: 101 us -> 89.5 us
  matrix products: 9.54 us -> 0 us
  waiting for transfers between devices: 23 us -> 19.7 us
  other arithmetic: 3.07 us -> 0.96 us
    all_gather x1 -> x0, blocking collectives: 27.6 us -> none  [body(): lax.all_gather(jnp.concatenate([hidden, grad_pre], axis=0), 'gy', axis=0,...]
    pallas_call x0 -> x4, Pallas kernels: none -> 20.7 us  [call(): pl.pallas_call(kernel, out_shape=outs, in_specs=[pl.BlockSpec(memory_spac...]
    all_to_all x1 -> x2, blocking collectives: 21.7 us -> 38.2 us  [the longest x1 21.1 us: body(): parts = lax.all_to_all(parts, 'gy', 0, 0, tiled=True)]
    slice x9 -> x1, local copies, waits for them, and re-layouts: 10.6 us -> 0.61 us  [body(): return (sums[:own], sums[own:], *grads)]
    dot_general x6 -> x0, matrix products: 9.54 us -> none  [dot(): lax.dot_general(left, right, (contract, ((), ())), preferred_element_type...]
    all_to_all x1, waiting for transfers between devices: 23 us -> 19.6 us  [body(): sums = lax.all_to_all(sums, GX, 0, 0, tiled=True)]
    convert_element_type x4 -> x0, local copies, waits for them, and re-layouts: 2.21 us -> none  [the longest x1 0.89 us: body(): dot(weight_out, hidden_block, ((0,), (0,))).astype(BF16)]
    concatenate x2 -> x0, other arithmetic: 1.96 us -> none  [the longest x1 1.01 us: body(): jnp.concatenate([pre_part, grad_part], axis=1)]
  transfers between devices with their start and end apart: 3 -> 3, of which waited for: 1 -> 1; matrix products, arithmetic and copies ran while one was open for 12% -> 1% of each run, Pallas kernels for 0% -> 11%
where the time goes in v2:
time: 152 us; the launch traced here: 151 us
  blocking collectives  89.5 us (59%)
  Pallas kernels  20.7 us (14%)
  waiting for transfers between devices  19.7 us (13%)
  between operations  14.1 us (9%)
  starting transfers between devices  5.6 us (4%)
    all_gather x1, blocking collectives, body(): block = lax.all_gather(pair, 'z', axis=0, tiled=False)  43.8 us
    all_to_all x1, blocking collectives, body(): parts = lax.all_to_all(parts, 'gy', 0, 0, tiled=True)  21.1 us
    pallas_call x4, Pallas kernels, call(): pl.pallas_call(kernel, out_shape=outs, in_specs=[pl.BlockSpec(memory_spac...  20.7 us
    all_to_all x1, waiting for transfers between devices, body(): sums = lax.all_to_all(sums, GX, 0, 0, tiled=True)  19.6 us
    all_to_all x1, blocking collectives, spread(): return lax.all_to_all(copies, axes, 0, 0, tiled=True)  17.1 us
    all_gather x1, blocking collectives, body(): block = lax.all_gather(block, 'xl', axis=0, tiled=True)  7.49 us
    all_to_all x1, starting transfers between devices, body(): sums = lax.all_to_all(sums, GX, 0, 0, tiled=True)  5.52 us
  transfers between devices with their start and end apart: 3, of which 1 were waited for; matrix products, arithmetic and copies ran while one was open for 1% of the time, Pallas kernels for 11%

profile of v2, /device:TPU:6, one launch (start us, length us, event | category | flops | bytes accessed | tf_op | source)
XLA Modules:
  0.0 151.2 jit_solution(883074863203950911)
XLA Ops:
  7.2 0.0 all-gather.6.cloned.1.call-start
  7.2 0.7 pad_maximum_fusion.1
  7.9 43.8 %all-gather = bf16[1152,128]{1,0:T(8,128)(2,1)S(1)} all-gather(bf16[72,128]{1,0:T(8,128)(2,1)S(1)} %pad_maximum_fusion.1), channel_id=2, replica_groups=mesh['xl'=2,'z'=16,'gy'=8,'xh'=2,'core'=2] {'z'}, dimensions={0}, use_global_device_ids=true | all-gather | bytes 313344 | tf_op jit(solution)/shard_map/all_gather | solution.py:184
  51.7 7.5 %all_gather.23.block_ref = bf16[32,72,128]{2,1,0:T(8,128)(2,1)} all-gather(bf16[16,72,128]{2,1,0:T(8,128)(2,1)S(1)} %bitcast.4), channel_id=1, replica_groups=mesh['xl'=2,'z'=16,'gy'=8,'xh'=2,'core'=2] {'xl'}, dimensions={0}, use_global_device_ids=true | all-gather | bytes 884736 | tf_op jit(solution)/shard_map/all_gather | solution.py:185
  59.2 0.0 all-gather.6.cloned.1.call-update
  59.2 0.0 all-gather.8.cloned.1.call-start
  59.3 6.2 %unit_terms.1 = bf16[8,288,128]{2,1,0:T(8,128)(2,1)} custom-call(bf16[32,72,128]{2,1,0:T(8,128)(2,1)} %all_gather.23.block_ref, bf16[1152,1152]{1,0:T(8,128)(2,1)} %in_hbm.3, bf16[1152,1152]{1,0:T(8,128)(2,1)} %out_hbm.3), custom_call_target="tpu_custom_call" | custom-call | flops 679477248 | bytes 5898240 | tf_op jit(solution)/shard_map/unit_terms/pallas_call | solution.py:158
  65.5 21.1 %all_to_all.15 = bf16[8,288,128]{2,1,0:T(8,128)(2,1)S(1)} all-to-all(bf16[8,288,128]{2,1,0:T(8,128)(2,1)} %unit_terms.1), channel_id=1, replica_groups=mesh['xl'=2,'z'=16,'gy'=8,'xh'=2,'core'=2] {'gy'}, dimensions={0} | all-to-all | bytes 1179648 | tf_op jit(solution)/shard_map/all_to_all | solution.py:201
  86.6 0.1 convert_reduce_fusion
  86.8 0.1 broadcast_in_dim.2
  86.9 17.1 %all_to_all.16.both_ref = bf16[8,288,128]{2,1,0:T(8,128)(2,1)} all-to-all(bf16[8,288,128]{2,1,0:T(8,128)(2,1)S(1)} %broadcast_in_dim.2), channel_id=1, replica_groups=mesh['xl'=2,'z'=16,'gy'=8,'xh'=2,'core'=2] {'gy'}, dimensions={0} | all-to-all | bytes 1179648 | tf_op jit(solution)/shard_map/all_to_all | solution.py:172
  103.9 0.0 all-gather.8.cloned.1.call-update
  104.0 6.3 %feature_terms.1 = bf16[32,72,128]{2,1,0:T(8,128)(2,1)} custom-call(bf16[8,288,128]{2,1,0:T(8,128)(2,1)} %all_to_all.16.both_ref, bf16[1152,1152]{1,0:T(8,128)(2,1)} %in_hbm.3, bf16[1152,1152]{1,0:T(8,128)(2,1)} %out_hbm.3), custom_call_target="tpu_custom_call" | custom-call | flops 679477248 | bytes 5898240 | tf_op jit(solution)/shard_map/feature_terms/pallas_call | solution.py:158
  110.3 5.5 %all-to-all-start.2 = ((bf16[32,72,128]{2,1,0:T(8,128)(2,1)}), bf16[32,72,128]{2,1,0:T(8,128)(2,1)S(1)}, u32[]{:S(2)}, u32[]{:S(2)}) async-start(bf16[32,72,128]{2,1,0:T(8,128)(2,1)} %feature_terms.1), calls=%async_computation.2 | async-start | bytes 1179648 | tf_op jit(solution)/shard_map/all_to_all | solution.py:220
  115.8 0.0 all-gather.6.cloned.1.call-done
  115.8 3.4 %unpack.1 = (bf16[288,512]{1,0:T(8,128)(2,1)}, bf16[1152,512]{1,0:T(8,128)(2,1)}) custom-call(bf16[4,32,72,128]{3,2,1,0:T(8,128)(2,1)} %bitcast.5), custom_call_target="tpu_custom_call" | custom-call | flops 679477248 | bytes 2359296 | tf_op jit(solution)/shard_map/unpack/pallas_call | solution.py:158
  119.2 19.6 %all-to-all-done.2 = bf16[32,72,128]{2,1,0:T(8,128)(2,1)S(1)} async-done(((bf16[32,72,128]{2,1,0:T(8,128)(2,1)}), bf16[32,72,128]{2,1,0:T(8,128)(2,1)S(1)}, u32[]{:S(2)}, u32[]{:S(2)}) %all-to-all-start.2) | async-done | bytes 589856 | tf_op jit(solution)/shard_map/all_to_all | solution.py:220
  138.9 0.1 reduce_sum.22
  138.9 0.6 fusion.1
  139.6 0.0 all-gather.8.cloned.1.call-done
  139.6 4.8 %weight_grads.1 = (bf16[288,1152]{1,0:T(8,128)(2,1)}, bf16[288,1152]{1,0:T(8,128)(2,1)}) custom-call(bf16[288,512]{1,0:T(8,128)(2,1)} %get-tuple-element.8.acts_ref, bf16[1152,512]{1,0:T(8,128)(2,1)} %get-tuple-element.9.cots_ref, bf16[4,8,288,128]{3,2,1,0:T(8,128)(2,1)} %bitcast.3), custom_call_target="tpu_custom_call" | custom-call | flops 679477248 | bytes 3833856 | tf_op jit(solution)/shard_map/weight_grads/pallas_call | solution.py:158
  (2 shorter events, 0.1 us)
Async XLA Ops:
  7.2 108.7 %all-gather.6.cloned.1.call-start = ((), (), s32[]{:S(2)}) async-start(), calls=%async_computation.3 | async-start | bytes 2949120 | tf_op jit(solution)/shard_map/all_gather | solution.py:186
  59.2 80.3 %all-gather.8.cloned.1.call-start = ((), (), s32[]{:S(2)}) async-start(), calls=%async_computation.4 | async-start | bytes 2949120 | tf_op jit(solution)/shard_map/all_gather | solution.py:207
  110.3 28.6 %all-to-all-start.2 = ((bf16[32,72,128]{2,1,0:T(8,128)(2,1)}), bf16[32,72,128]{2,1,0:T(8,128)(2,1)S(1)}, u32[]{:S(2)}, u32[]{:S(2)}) async-start(bf16[32,72,128]{2,1,0:T(8,128)(2,1)} %feature_terms.1), calls=%async_computation.2 | async-start | bytes 1179648 | tf_op jit(solution)/shard_map/all_to_all | solution.py:220
Sparse Core Ops, SparseCore 0:
  59.4 30.0 all-gather.5
  104.1 29.7 all-gather.7

commit v3 on v2

v3 whole, which is shorter than its diff:
```python
import functools
import math

import jax
import jax.numpy as jnp
from jax import lax
from jax.experimental import pallas as pl
from jax.experimental.pallas import tpu as pltpu
from jax.sharding import Mesh, PartitionSpec as P

F32 = jnp.float32
BF16 = jnp.bfloat16
GX = ("xl", "z")
DEV = ("xh", "core")
VMEM = pl.BlockSpec(memory_space=pltpu.VMEM)


def silu_slope(pre):
    sig = jax.nn.sigmoid(pre)
    return sig * (1.0 + pre * (1.0 - sig))


def dot(left, right, contract):
    return lax.dot_general(left, right, (contract, ((), ())), preferred_element_type=F32)


def turned(right):
    return right.astype(F32).T.astype(BF16)


class Weights:
    def __init__(self, columns_hbm, rows_hbm, columns_ref, rows_ref, sems):
        n = sems.shape[1]
        self.columns_ref, self.rows_ref = columns_ref, rows_ref
        self.column_parts = [pl.ds(c * (columns_ref.shape[1] // 3), columns_ref.shape[1] // 3) for c in range(3)]
        self.row_parts = [pl.ds(c * (rows_ref.shape[0] // n), rows_ref.shape[0] // n) for c in range(n)]
        self.columns = [
            pltpu.make_async_copy(columns_hbm.at[:, part], columns_ref.at[:, part], sems.at[0, c])
            for c, part in enumerate(self.column_parts)
        ]
        self.rows = [
            pltpu.make_async_copy(rows_hbm.at[part], rows_ref.at[part], sems.at[1, c])
            for c, part in enumerate(self.row_parts)
        ]
        for copy in self.columns + self.rows:
            copy.start()

    def columns_dot(self, left, to_ref):
        for part, copy in zip(self.column_parts, self.columns):
            copy.wait()
            to_ref[part] = dot(left, self.columns_ref[:, part], ((1,), (0,))).T

    def rows_dot(self, right):
        for part, copy in zip(self.row_parts, self.rows):
            copy.wait()
            yield dot(self.rows_ref[part], right, ((1,), (0,)))


def unit_terms(block_ref, in_hbm, out_hbm, parts_ref, in_ref, out_ref, acts_ref, cots_ref, pair_ref, sems):
    weights = Weights(in_hbm, out_hbm, in_ref, out_ref, sems)
    own = block_ref.shape[1] // 2
    for g in range(block_ref.shape[0]):
        pair_ref[...] = block_ref[g].astype(F32)
        acts_ref[g * own : (g + 1) * own] = pair_ref[:own]
        cots_ref[g * own : (g + 1) * own] = pair_ref[own:]
    cots, acts = cots_ref[...].astype(BF16), turned(acts_ref[...])
    pre_ref = acts_ref
    weights.columns_dot(acts, pre_ref)
    shares, share = parts_ref.shape[0], parts_ref.shape[1] // 2
    for k in range(shares):
        parts_ref[k, :share] = pre_ref[k * share : (k + 1) * share].astype(BF16)
    each = shares // sems.shape[1]
    for c, grad in enumerate(weights.rows_dot(cots)):
        for j in range(each):
            parts_ref[c * each + j, share:] = grad[j * share : (j + 1) * share].astype(BF16)


def feature_terms(both_ref, in_hbm, out_hbm, sums_ref, out_ref, in_ref, out_rows_ref, in_rows_ref, pair_ref, sems):
    weights = Weights(out_hbm, in_hbm, out_ref, in_ref, sems)
    share = both_ref.shape[1] // 2
    shares = range(both_ref.shape[0])
    hidden = turned(jnp.concatenate([both_ref[k, :share] for k in shares], axis=0))
    grad = jnp.concatenate([both_ref[k, share:] for k in shares], axis=0)
    weights.columns_dot(hidden, out_rows_ref)
    members, own = sums_ref.shape[0], sums_ref.shape[1] // 2
    rows = in_ref.shape[0] // sems.shape[1]
    each = members // sems.shape[1]
    for c, part in enumerate(weights.rows_dot(grad)):
        in_rows_ref[c * rows : (c + 1) * rows] = part
        for g in range(c * each, (c + 1) * each):
            pair_ref[:own] = out_rows_ref[g * own : (g + 1) * own]
            pair_ref[own:] = in_rows_ref[g * own : (g + 1) * own]
            sums_ref[g] = pair_ref[...].astype(BF16)


def relative(step):
    xh, core = lax.axis_index("xh"), lax.axis_index("core")
    return 2 * (1 - xh if step & 2 else xh) + (1 - core if step & 1 else core)


def unpack(block_hbm, acts_out, cots_out, block_ref, acts_ref, cots_ref, pair_ref, sems):
    groups, members, rows, tokens = block_ref.shape
    own = rows // 2
    copies = [
        pltpu.make_async_copy(block_hbm.at[relative(t)], block_ref.at[t], sems.at[t])
        for t in range(groups)
    ]
    for copy in copies:
        copy.start()
    owner = relative(0)
    for t in range(groups):
        copies[t].wait()
        lanes = slice(t * tokens, (t + 1) * tokens)
        for g in range(members):
            pair_ref[...] = block_ref[t, g].astype(F32)
            cots_ref[g * own : (g + 1) * own] = pair_ref[own:]
        cots_out[:, lanes] = cots_ref[...].astype(BF16)
        for g in range(members // groups):
            pair_ref[...] = block_ref[t, owner * (members // groups) + g].astype(F32)
            acts_ref[g * own : (g + 1) * own] = pair_ref[:own]
        acts_out[:, lanes] = acts_ref[...].astype(BF16)


def weight_grads(factor, acts_ref, cots_ref, both_ref, core_ref, far_ref, far_core_ref, in_ref, out_ref):
    shares, share = both_ref.shape[0], both_ref.shape[1] // 2
    units = shares * share
    own = out_ref.shape[0]
    owner, core = relative(0), lax.axis_index("core")
    pieces = own // share
    acts = acts_ref[...]
    grads = jnp.concatenate(
        [jnp.concatenate([ref[k, share:] for k in range(shares)], axis=0) for ref in (both_ref, core_ref)]
        + [ref[:units] for ref in (far_ref, far_core_ref)],
        axis=1,
    )
    width = 384
    for at in range(0, in_ref.shape[1], width):
        part = grads[at : at + width]
        in_ref[:, at : at + width] = (dot(acts, part, ((1,), (1,))) * factor).astype(BF16)
    at = pl.multiple_of(units + core * own, share)
    hidden = jnp.concatenate(
        [
            jnp.concatenate([ref[owner * pieces + j, :share] for j in range(pieces)], axis=0)
            for ref in (both_ref, core_ref)
        ]
        + [ref[pl.ds(at, own)] for ref in (far_ref, far_core_ref)],
        axis=1,
    )
    for at in range(0, out_ref.shape[1], width):
        part = cots_ref[at : at + width]
        out_ref[:, at : at + width] = (dot(hidden, part, ((1,), (1,))) * factor).astype(BF16)


def call(kernel, name, outs, scratch, n_sems, args, in_hbm, flops, vmem):
    n_bytes = sum(a.size * a.dtype.itemsize for a in args)
    return pl.pallas_call(
        kernel,
        out_shape=outs,
        in_specs=[pl.BlockSpec(memory_space=pltpu.HBM) if i in in_hbm else VMEM for i in range(len(args))],
        out_specs=jax.tree.map(lambda _: VMEM, outs),
        scratch_shapes=[pltpu.VMEM(*s) for s in scratch]
        + ([pltpu.SemaphoreType.DMA(n_sems)] if n_sems else []),
        compiler_params=pltpu.CompilerParams(vmem_limit_bytes=vmem * 2**20),
        cost_estimate=pl.CostEstimate(flops=flops, bytes_accessed=n_bytes, transcendentals=0),
        name=name,
    )(*args)


def spread(local, axes):
    copies = jnp.broadcast_to(local[None], (lax.axis_size(axes), *local.shape))
    return lax.all_to_all(copies, axes, 0, 0, tiled=True)


def body(activations, weight_in, weight_out, cotangent):
    own, tokens = activations.shape
    feats, units = weight_in.shape
    n_gx, n_gy, n_dev = (lax.axis_size(a) for a in (GX, "gy", DEV))
    share = units // n_gy
    pair_rows = (2 * own, tokens)
    products = 4 * feats * units * tokens

    pair = jnp.concatenate([activations, cotangent], axis=0)
    block = lax.all_gather(pair, "z", axis=0, tiled=False)
    block = lax.all_gather(block, "xl", axis=0, tiled=True)
    block_all = lax.all_gather(block, DEV, axis=0, tiled=False)

    weight = (weight_in.shape, BF16)
    rows = ((feats, tokens), F32)
    parts = call(
        unit_terms,
        "unit_terms",
        jax.ShapeDtypeStruct((n_gy, 2 * share, tokens), BF16),
        [weight, weight, rows, rows, (pair_rows, F32)],
        (2, 4),
        (block, weight_in, weight_out),
        (1, 2),
        products,
        62,
    )
    parts = lax.all_to_all(parts, "gy", 0, 0, tiled=True)
    total = jnp.sum(parts.astype(F32), axis=0)
    pre, grad_hidden = total[:share], total[share:]
    hidden = jax.nn.silu(pre).astype(BF16)
    grad_pre = (grad_hidden * silu_slope(pre)).astype(BF16)
    both = spread(jnp.concatenate([hidden, grad_pre], axis=0), "gy").reshape(n_gy, 2 * share, tokens)
    swap = [(0, 1), (1, 0)]
    near = lax.axis_index("xh")
    half = lax.dynamic_slice_in_dim(both, (1 - near) * (n_gy // 2), n_gy // 2, 0)[:, :share]
    far = jnp.concatenate([both[:, share:].reshape(units, tokens), half.reshape(units // 2, tokens)])
    far = lax.ppermute(far, "xh", swap)
    both_core = lax.ppermute(both, "core", swap)
    far_core = lax.ppermute(far, "core", swap)

    sums = call(
        feature_terms,
        "feature_terms",
        jax.ShapeDtypeStruct((n_gx, *pair_rows), BF16),
        [weight, weight, rows, rows, (pair_rows, F32)],
        (2, 4),
        (both, weight_in, weight_out),
        (1, 2),
        products,
        62,
    )
    sums = lax.all_to_all(sums, GX, 0, 0, tiled=True)
    sums = jnp.sum(sums.astype(F32), axis=0).astype(BF16)

    acts_own, cots_all = call(
        unpack,
        "unpack",
        (
            jax.ShapeDtypeStruct((feats // n_dev, n_dev * tokens), BF16),
            jax.ShapeDtypeStruct((feats, n_dev * tokens), BF16),
        ),
        [
            (block_all.shape, BF16),
            ((feats // n_dev, tokens), F32),
            ((feats, tokens), F32),
            (pair_rows, F32),
        ],
        (n_dev,),
        (block_all,),
        (0,),
        products,
        62,
    )
    grads = call(
        functools.partial(weight_grads, 1.0 / math.sqrt(n_dev * tokens)),
        "weight_grads",
        (
            jax.ShapeDtypeStruct((feats // n_dev, units), BF16),
            jax.ShapeDtypeStruct((units // n_dev, feats), BF16),
        ),
        [],
        (),
        (acts_own, cots_all, both, both_core, far, far_core),
        (),
        products,
        32,
    )
    return (sums[:own], sums[own:], *grads)


def solution(mesh):
    shape = mesh.devices.shape
    fine = Mesh(
        mesh.devices.reshape(2, shape[0] // 2, shape[1], 2, shape[2] // 2),
        ("xl", "z", "gy", "xh", "core"),
    )
    return jax.shard_map(
        body,
        mesh=fine,
        in_specs=(P(("gy", *GX), DEV), P("gy", GX), P(GX, "gy"), P(("gy", *GX), DEV)),
        out_specs=(P(("gy", *GX), DEV), P(("gy", *GX), DEV), P(("gy", *DEV), GX), P((*GX, *DEV), "gy")),
        check_vma=False,
    )
```

time: 152 us -> 151 us (level); the launches traced: 151 us -> 148 us
  blocking collectives: 89.5 us -> 68.3 us
  starting transfers between devices: 5.6 us -> 19.9 us
  local copies, waits for them, and re-layouts: 0.69 us -> 2.94 us
  waiting for transfers between devices: 19.7 us -> 21.8 us
  Pallas kernels: 20.7 us -> 19.1 us
    all_to_all x1 -> x0, blocking collectives: 21.1 us -> none  [body(): parts = lax.all_to_all(parts, 'gy', 0, 0, tiled=True)]
    all_to_all x1, waiting for transfers between devices: 19.6 us -> 0.01 us  [body(): sums = lax.all_to_all(sums, GX, 0, 0, tiled=True)]
    all_to_all x0 -> x1, waiting for transfers between devices: none -> 13.4 us  [body(): parts = lax.all_to_all(parts, 'gy', 0, 0, tiled=True)]
    ppermute x0 -> x3, waiting for transfers between devices: none -> 7.71 us  [the longest x1 7.7 us: body(): far = lax.ppermute(far, 'xh', swap)]
    ppermute x0 -> x3, starting transfers between devices: none -> 7.14 us  [the longest x1 3.31 us: body(): far = lax.ppermute(far, 'xh', swap)]
    all_to_all x0 -> x1, starting transfers between devices: none -> 7.12 us  [body(): parts = lax.all_to_all(parts, 'gy', 0, 0, tiled=True)]
    unnamed x0 -> x6, local copies, waits for them, and re-layouts: none -> 2.23 us
    pallas_call x4, Pallas kernels: 20.7 us -> 19.1 us  [call(): pl.pallas_call(kernel, out_shape=outs, in_specs=[pl.BlockSpec(memory_spac...]
  transfers between devices with their start and end apart: 3 -> 6, of which waited for: 1 -> 2; matrix products, arithmetic and copies ran while one was open for 1% -> 0% of each run, Pallas kernels for 11% -> 9%
where the time goes in v3:
time: 151 us; the launch traced here: 148 us
  blocking collectives  68.3 us (45%)
  waiting for transfers between devices  21.8 us (14%)
  starting transfers between devices  19.9 us (13%)
  Pallas kernels  19.1 us (13%)
  between operations  14.2 us (9%)
  local copies, waits for them, and re-layouts  2.94 us (2%)
  other arithmetic  2.05 us (1%)
    all_gather x1, blocking collectives, body(): block = lax.all_gather(pair, 'z', axis=0, tiled=False)  43.8 us
    pallas_call x4, Pallas kernels, call(): pl.pallas_call(kernel, out_shape=outs, in_specs=[pl.BlockSpec(memory_spac...  19.1 us
    all_to_all x1, blocking collectives, spread(): return lax.all_to_all(copies, axes, 0, 0, tiled=True)  17.1 us
    all_to_all x1, waiting for transfers between devices, body(): parts = lax.all_to_all(parts, 'gy', 0, 0, tiled=True)  13.4 us
    ppermute x1, waiting for transfers between devices, body(): far = lax.ppermute(far, 'xh', swap)  7.7 us
    all_gather x1, blocking collectives, body(): block = lax.all_gather(block, 'xl', axis=0, tiled=True)  7.49 us
    all_to_all x1, starting transfers between devices, body(): parts = lax.all_to_all(parts, 'gy', 0, 0, tiled=True)  7.12 us
    all_to_all x1, starting transfers between devices, body(): sums = lax.all_to_all(sums, GX, 0, 0, tiled=True)  5.56 us
  transfers between devices with their start and end apart: 6, of which 2 were waited for; matrix products, arithmetic and copies ran while one was open for 0% of the time, Pallas kernels for 9%

profile of v3, /device:TPU:6, one launch (start us, length us, event | category | flops | bytes accessed | tf_op | source)
XLA Modules:
  0.0 148.3 jit_solution(8369617718560808406)
XLA Ops:
  7.2 0.7 pad_maximum_fusion.2
  7.9 43.8 %all-gather = bf16[1152,128]{1,0:T(8,128)(2,1)S(1)} all-gather(bf16[72,128]{1,0:T(8,128)(2,1)S(1)} %pad_maximum_fusion.2), channel_id=2, replica_groups=mesh['xl'=2,'z'=16,'gy'=8,'xh'=2,'core'=2] {'z'}, dimensions={0}, use_global_device_ids=true | all-gather | bytes 313344 | tf_op jit(solution)/shard_map/all_gather | solution.py:183
  51.7 7.5 %all_gather.17.block_ref = bf16[32,72,128]{2,1,0:T(8,128)(2,1)} all-gather(bf16[16,72,128]{2,1,0:T(8,128)(2,1)S(1)} %bitcast.5), channel_id=1, replica_groups=mesh['xl'=2,'z'=16,'gy'=8,'xh'=2,'core'=2] {'xl'}, dimensions={0}, use_global_device_ids=true | all-gather | bytes 884736 | tf_op jit(solution)/shard_map/all_gather | solution.py:184
  59.2 6.3 %unit_terms.1 = bf16[8,288,128]{2,1,0:T(8,128)(2,1)} custom-call(bf16[32,72,128]{2,1,0:T(8,128)(2,1)} %all_gather.17.block_ref, bf16[1152,1152]{1,0:T(8,128)(2,1)} %in_hbm.3, bf16[1152,1152]{1,0:T(8,128)(2,1)} %out_hbm.3), custom_call_target="tpu_custom_call" | custom-call | flops 679477248 | bytes 5898240 | tf_op jit(solution)/shard_map/unit_terms/pallas_call | solution.py:156
  65.4 7.1 %all-to-all-start = ((bf16[8,288,128]{2,1,0:T(8,128)(2,1)}), bf16[8,288,128]{2,1,0:T(8,128)(2,1)S(1)}, u32[]{:S(2)}, u32[]{:S(2)}) async-start(bf16[8,288,128]{2,1,0:T(8,128)(2,1)} %unit_terms.1), calls=%async_computation | async-start | bytes 1179648 | tf_op jit(solution)/shard_map/all_to_all | solution.py:200
  72.5 0.0 all-gather.4.cloned.1.call-start
  72.6 0.7 all-gather.4.cloned.1.call-update
  73.3 13.4 %all-to-all-done = bf16[8,288,128]{2,1,0:T(8,128)(2,1)S(1)} async-done(((bf16[8,288,128]{2,1,0:T(8,128)(2,1)}), bf16[8,288,128]{2,1,0:T(8,128)(2,1)S(1)}, u32[]{:S(2)}, u32[]{:S(2)}) %all-to-all-start) | async-done | bytes 589856 | tf_op jit(solution)/shard_map/all_to_all | solution.py:200
  86.6 0.1 convert_reduce_fusion
  86.8 0.1 broadcast_in_dim.2
  86.9 17.1 %all_to_all.15.both_ref = bf16[8,288,128]{2,1,0:T(8,128)(2,1)} all-to-all(bf16[8,288,128]{2,1,0:T(8,128)(2,1)S(1)} %broadcast_in_dim.2), channel_id=1, replica_groups=mesh['xl'=2,'z'=16,'gy'=8,'xh'=2,'core'=2] {'gy'}, dimensions={0} | all-to-all | bytes 1179648 | tf_op jit(solution)/shard_map/all_to_all | solution.py:171
  104.0 0.0 copy-start
  104.0 0.0 slice-start
  104.0 6.5 %feature_terms.1 = bf16[32,72,128]{2,1,0:T(8,128)(2,1)} custom-call(bf16[8,288,128]{2,1,0:T(8,128)(2,1)} %all_to_all.15.both_ref, bf16[1152,1152]{1,0:T(8,128)(2,1)} %in_hbm.3, bf16[1152,1152]{1,0:T(8,128)(2,1)} %out_hbm.3), custom_call_target="tpu_custom_call" | custom-call | flops 679477248 | bytes 5898240 | tf_op jit(solution)/shard_map/feature_terms/pallas_call | solution.py:156
  110.5 5.6 %all-to-all-start.2 = ((bf16[32,72,128]{2,1,0:T(8,128)(2,1)}), bf16[32,72,128]{2,1,0:T(8,128)(2,1)}, u32[]{:S(2)}, u32[]{:S(2)}) async-start(bf16[32,72,128]{2,1,0:T(8,128)(2,1)} %feature_terms.1), calls=%async_computation.2 | async-start | bytes 1179648 | tf_op jit(solution)/shard_map/all_to_all | solution.py:225
  116.1 0.0 copy-done
  116.1 0.0 slice-done
  116.2 3.3 %collective-permute-start.1 = (bf16[1728,128]{1,0:T(8,128)(2,1)S(1)}, bf16[1728,128]{1,0:T(8,128)(2,1)S(1)}, u32[]{:S(2)}, u32[]{:S(2)}) collective-permute-start(bf16[1728,128]{1,0:T(8,128)(2,1)S(1)} %pad_maximum_fusion), channel_id=1, source_target_pairs={{0,2},{2,0},{1,3},{3,1},{4,6},{6,4},{5,7},{7,5},{8,10},{10,8},{9,1... | collective-permute-start | bytes 1327112 | tf_op jit(solution)/shard_map/ppermute | solution.py:210
  119.5 1.9 %collective-permute-start = (bf16[8,288,128]{2,1,0:T(8,128)(2,1)S(1)}, bf16[8,288,128]{2,1,0:T(8,128)(2,1)S(1)}, u32[]{:S(2)}, u32[]{:S(2)}) collective-permute-start(bf16[8,288,128]{2,1,0:T(8,128)(2,1)S(1)} %copy-done), channel_id=1, source_target_pairs={{0,1},{1,0},{2,3},{3,2},{4,5},{5,4},{6,7},{7,6},{8,9},{9,8},{10,11... | collective-permute-start | bytes 1769480 | tf_op jit(solution)/shard_map/ppermute | solution.py:211
  121.4 7.7 %collective-permute-done.1.far_ref = bf16[1728,128]{1,0:T(8,128)(2,1)S(1)} collective-permute-done((bf16[1728,128]{1,0:T(8,128)(2,1)S(1)}, bf16[1728,128]{1,0:T(8,128)(2,1)S(1)}, u32[]{:S(2)}, u32[]{:S(2)}) %collective-permute-start.1) | collective-permute-done | bytes 442400 | tf_op jit(solution)/shard_map/ppermute | solution.py:210
  129.1 1.9 %collective-permute-start.2 = (bf16[1728,128]{1,0:T(8,128)(2,1)S(1)}, bf16[1728,128]{1,0:T(8,128)(2,1)}, u32[]{:S(2)}, u32[]{:S(2)}) collective-permute-start(bf16[1728,128]{1,0:T(8,128)(2,1)S(1)} %collective-permute-done.1.far_ref), channel_id=1, source_target_pairs={{0,1},{1,0},{2,3},{3,2},{4,5},{5,4},{6,7},{7,6},{8,9},{9,8},{10,11... | collective-permute-start | bytes 1327112 | tf_op jit(solution)/shard_map/ppermute | solution.py:212
  131.0 0.0 all-gather.4.cloned.1.call-done
  131.1 3.3 %unpack.1 = (bf16[288,512]{1,0:T(8,128)(2,1)}, bf16[1152,512]{1,0:T(8,128)(2,1)}) custom-call(bf16[4,32,72,128]{3,2,1,0:T(8,128)(2,1)} %bitcast.7), custom_call_target="tpu_custom_call" | custom-call | flops 679477248 | bytes 2359296 | tf_op jit(solution)/shard_map/unpack/pallas_call | solution.py:156
  134.4 0.0 collective-permute-done.core_ref
  134.4 0.0 collective-permute-done.2.far_core_ref
  134.4 0.0 copy-start.1
  134.5 1.3 copy-done.1
  135.7 1.0 copy-done.2
  136.7 3.0 %weight_grads.1 = (bf16[288,1152]{1,0:T(8,128)(2,1)}, bf16[288,1152]{1,0:T(8,128)(2,1)}) custom-call(bf16[288,512]{1,0:T(8,128)(2,1)S(1)} %copy-done.2, bf16[1152,512]{1,0:T(8,128)(2,1)S(1)} %copy-done.1, bf16[8,288,128]{2,1,0:T(8,128)(2,1)S(1)} %copy-done, bf16[8,288,128]{2,1,0:T(8,128)(2,1)S(1)} %collective-permute-done.core_ref, ...), custom_call_target="tpu_custom_call" | custom-call | flops 679477248 | bytes 3538944 | tf_op jit(solution)/shard_map/weight_grads/pallas_call | solution.py:156
  139.7 0.0 all-to-all-done.2
  139.7 1.2 reduce_sum.22
  140.8 0.6 fusion.1
  (5 shorter events, 0.1 us)
Async XLA Ops:
  65.4 21.2 %all-to-all-start = ((bf16[8,288,128]{2,1,0:T(8,128)(2,1)}), bf16[8,288,128]{2,1,0:T(8,128)(2,1)S(1)}, u32[]{:S(2)}, u32[]{:S(2)}) async-start(bf16[8,288,128]{2,1,0:T(8,128)(2,1)} %unit_terms.1), calls=%async_computation | async-start | bytes 1179648 | tf_op jit(solution)/shard_map/all_to_all | solution.py:200
  72.5 58.5 %all-gather.4.cloned.1.call-start = ((), (), s32[]{:S(2)}) async-start(), calls=%async_computation.3 | async-start | bytes 2949120 | tf_op jit(solution)/shard_map/all_gather | solution.py:185
  104.0 12.1 %copy-start = (bf16[8,288,128]{2,1,0:T(8,128)(2,1)S(1)}, bf16[8,288,128]{2,1,0:T(8,128)(2,1)}, u32[]{:S(2)}) copy-start(bf16[8,288,128]{2,1,0:T(8,128)(2,1)} %all_to_all.15.both_ref) | copy-start | bytes 1769476
  104.0 12.2 %slice-start = ((bf16[8,288,128]{2,1,0:T(8,128)(2,1)}), bf16[8,144,128]{2,1,0:T(8,128)(2,1)S(1)}, s32[]{:S(2)}) async-start(bf16[8,288,128]{2,1,0:T(8,128)(2,1)} %all_to_all.15.both_ref), calls=%async_computation.4 | async-start | bytes 589824 | tf_op jit(solution)/shard_map/slice | solution.py:209
  110.5 29.2 %all-to-all-start.2 = ((bf16[32,72,128]{2,1,0:T(8,128)(2,1)}), bf16[32,72,128]{2,1,0:T(8,128)(2,1)}, u32[]{:S(2)}, u32[]{:S(2)}) async-start(bf16[32,72,128]{2,1,0:T(8,128)(2,1)} %feature_terms.1), calls=%async_computation.2 | async-start | bytes 1179648 | tf_op jit(solution)/shard_map/all_to_all | solution.py:225
  116.2 13.0 %collective-permute-start.1 = (bf16[1728,128]{1,0:T(8,128)(2,1)S(1)}, bf16[1728,128]{1,0:T(8,128)(2,1)S(1)}, u32[]{:S(2)}, u32[]{:S(2)}) collective-permute-start(bf16[1728,128]{1,0:T(8,128)(2,1)S(1)} %pad_maximum_fusion), channel_id=1, source_target_pairs={{0,2},{2,0},{1,3},{3,1},{4,6},{6,4},{5,7},{7,5},{8,10},{10,8},{9,1... | collective-permute-start | bytes 1327112 | tf_op jit(solution)/shard_map/ppermute | solution.py:210
  119.5 14.9 %collective-permute-start = (bf16[8,288,128]{2,1,0:T(8,128)(2,1)S(1)}, bf16[8,288,128]{2,1,0:T(8,128)(2,1)S(1)}, u32[]{:S(2)}, u32[]{:S(2)}) collective-permute-start(bf16[8,288,128]{2,1,0:T(8,128)(2,1)S(1)} %copy-done), channel_id=1, source_target_pairs={{0,1},{1,0},{2,3},{3,2},{4,5},{5,4},{6,7},{7,6},{8,9},{9,8},{10,11... | collective-permute-start | bytes 1769480 | tf_op jit(solution)/shard_map/ppermute | solution.py:211
  129.1 5.3 %collective-permute-start.2 = (bf16[1728,128]{1,0:T(8,128)(2,1)S(1)}, bf16[1728,128]{1,0:T(8,128)(2,1)}, u32[]{:S(2)}, u32[]{:S(2)}) collective-permute-start(bf16[1728,128]{1,0:T(8,128)(2,1)S(1)} %collective-permute-done.1.far_ref), channel_id=1, source_target_pairs={{0,1},{1,0},{2,3},{3,2},{4,5},{5,4},{6,7},{7,6},{8,9},{9,8},{10,11... | collective-permute-start | bytes 1327112 | tf_op jit(solution)/shard_map/ppermute | solution.py:212
  134.4 1.3 copy-start.1
  135.7 1.0 copy-start.2
Sparse Core Ops, SparseCore 0:
  76.1 30.1 all-gather.3

commit v4 on v3

--- a/solution.py
+++ b/solution.py
@@ -34,31 +34,44 @@
         self.columns_ref, self.rows_ref = columns_ref, rows_ref
         self.column_parts = [pl.ds(c * (columns_ref.shape[1] // 3), columns_ref.shape[1] // 3) for c in range(3)]
         self.row_parts = [pl.ds(c * (rows_ref.shape[0] // n), rows_ref.shape[0] // n) for c in range(n)]
-        self.columns = [
+        self.coming = [
             pltpu.make_async_copy(columns_hbm.at[:, part], columns_ref.at[:, part], sems.at[0, c])
             for c, part in enumerate(self.column_parts)
-        ]
-        self.rows = [
+        ] + [
             pltpu.make_async_copy(rows_hbm.at[part], rows_ref.at[part], sems.at[1, c])
             for c, part in enumerate(self.row_parts)
         ]
-        for copy in self.columns + self.rows:
+        self.ahead = 2
+        self.taken = 0
+        for copy in self.coming[: self.ahead]:
             copy.start()
 
+    def take(self):
+        self.coming[self.taken].wait()
+        if self.taken + self.ahead < len(self.coming):
+            self.coming[self.taken + self.ahead].start()
+        self.taken += 1
+
     def columns_dot(self, left, to_ref):
-        for part, copy in zip(self.column_parts, self.columns):
-            copy.wait()
+        for part in self.column_parts:
+            self.take()
             to_ref[part] = dot(left, self.columns_ref[:, part], ((1,), (0,))).T
 
     def rows_dot(self, right):
-        for part, copy in zip(self.row_parts, self.rows):
-            copy.wait()
+        for part in self.row_parts:
+            self.take()
             yield dot(self.rows_ref[part], right, ((1,), (0,)))
 
 
-def unit_terms(block_ref, in_hbm, out_hbm, parts_ref, in_ref, out_ref, acts_ref, cots_ref, pair_ref, sems):
+def unit_terms(
+    block_hbm, in_hbm, out_hbm, parts_hbm,
+    block_ref, parts_ref, in_ref, out_ref, acts_ref, cots_ref, pair_ref, sems, own_sems,
+):
+    load = pltpu.make_async_copy(block_hbm, block_ref, own_sems.at[0])
+    load.start()
     weights = Weights(in_hbm, out_hbm, in_ref, out_ref, sems)
     own = block_ref.shape[1] // 2
+    load.wait()
     for g in range(block_ref.shape[0]):
         pair_ref[...] = block_ref[g].astype(F32)
         acts_ref[g * own : (g + 1) * own] = pair_ref[:own]
@@ -70,27 +83,45 @@
     for k in range(shares):
         parts_ref[k, :share] = pre_ref[k * share : (k + 1) * share].astype(BF16)
     each = shares // sems.shape[1]
+    stores = []
     for c, grad in enumerate(weights.rows_dot(cots)):
         for j in range(each):
             parts_ref[c * each + j, share:] = grad[j * share : (j + 1) * share].astype(BF16)
-
-
-def feature_terms(both_ref, in_hbm, out_hbm, sums_ref, out_ref, in_ref, out_rows_ref, in_rows_ref, pair_ref, sems):
+        part = pl.ds(c * each, each)
+        stores.append(pltpu.make_async_copy(parts_ref.at[part], parts_hbm.at[part], own_sems.at[1 + c]))
+        stores[-1].start()
+    for store in stores:
+        store.wait()
+
+
+def feature_terms(
+    both_hbm, in_hbm, out_hbm, sums_hbm,
+    both_ref, sums_ref, out_ref, in_ref, out_rows_ref, in_rows_ref, pair_ref, sems, own_sems,
+):
+    load = pltpu.make_async_copy(both_hbm, both_ref, own_sems.at[0])
+    load.start()
     weights = Weights(out_hbm, in_hbm, out_ref, in_ref, sems)
     share = both_ref.shape[1] // 2
     shares = range(both_ref.shape[0])
+    load.wait()
     hidden = turned(jnp.concatenate([both_ref[k, :share] for k in shares], axis=0))
     grad = jnp.concatenate([both_ref[k, share:] for k in shares], axis=0)
     weights.columns_dot(hidden, out_rows_ref)
     members, own = sums_ref.shape[0], sums_ref.shape[1] // 2
     rows = in_ref.shape[0] // sems.shape[1]
     each = members // sems.shape[1]
+    stores = []
     for c, part in enumerate(weights.rows_dot(grad)):
         in_rows_ref[c * rows : (c + 1) * rows] = part
         for g in range(c * each, (c + 1) * each):
             pair_ref[:own] = out_rows_ref[g * own : (g + 1) * own]
             pair_ref[own:] = in_rows_ref[g * own : (g + 1) * own]
             sums_ref[g] = pair_ref[...].astype(BF16)
+        span = pl.ds(c * each, each)
+        stores.append(pltpu.make_async_copy(sums_ref.at[span], sums_hbm.at[span], own_sems.at[1 + c]))
+        stores[-1].start()
+    for store in stores:
+        store.wait()
 
 
 def relative(step):
@@ -98,7 +129,7 @@
     return 2 * (1 - xh if step & 2 else xh) + (1 - core if step & 1 else core)
 
 
-def unpack(block_hbm, acts_out, cots_out, block_ref, acts_ref, cots_ref, pair_ref, sems):
+def unpack(block_hbm, unused_hbm, acts_out, cots_out, block_ref, acts_ref, cots_ref, pair_ref, sems):
     groups, members, rows, tokens = block_ref.shape
     own = rows // 2
     copies = [
@@ -151,15 +182,14 @@
         out_ref[:, at : at + width] = (dot(hidden, part, ((1,), (1,))) * factor).astype(BF16)
 
 
-def call(kernel, name, outs, scratch, n_sems, args, in_hbm, flops, vmem):
+def call(kernel, name, outs, scratch, sems, args, in_hbm, flops, vmem, out_space=pltpu.VMEM):
     n_bytes = sum(a.size * a.dtype.itemsize for a in args)
     return pl.pallas_call(
         kernel,
         out_shape=outs,
         in_specs=[pl.BlockSpec(memory_space=pltpu.HBM) if i in in_hbm else VMEM for i in range(len(args))],
-        out_specs=jax.tree.map(lambda _: VMEM, outs),
-        scratch_shapes=[pltpu.VMEM(*s) for s in scratch]
-        + ([pltpu.SemaphoreType.DMA(n_sems)] if n_sems else []),
+        out_specs=jax.tree.map(lambda _: pl.BlockSpec(memory_space=out_space), outs),
+        scratch_shapes=[pltpu.VMEM(*s) for s in scratch] + [pltpu.SemaphoreType.DMA(s) for s in sems],
         compiler_params=pltpu.CompilerParams(vmem_limit_bytes=vmem * 2**20),
         cost_estimate=pl.CostEstimate(flops=flops, bytes_accessed=n_bytes, transcendentals=0),
         name=name,
@@ -190,12 +220,13 @@
         unit_terms,
         "unit_terms",
         jax.ShapeDtypeStruct((n_gy, 2 * share, tokens), BF16),
-        [weight, weight, rows, rows, (pair_rows, F32)],
-        (2, 4),
+        [((n_gx, *pair_rows), BF16), ((n_gy, 2 * share, tokens), BF16), weight, weight, rows, rows, (pair_rows, F32)],
+        [(2, 4), (5,)],
         (block, weight_in, weight_out),
-        (1, 2),
+        (0, 1, 2),
         products,
         62,
+        pltpu.HBM,
     )
     parts = lax.all_to_all(parts, "gy", 0, 0, tiled=True)
     total = jnp.sum(parts.astype(F32), axis=0)
@@ -215,12 +246,13 @@
         feature_terms,
         "feature_terms",
         jax.ShapeDtypeStruct((n_gx, *pair_rows), BF16),
-        [weight, weight, rows, rows, (pair_rows, F32)],
-        (2, 4),
+        [((n_gy, 2 * share, tokens), BF16), ((n_gx, *pair_rows), BF16), weight, weight, rows, rows, (pair_rows, F32)],
+        [(2, 4), (5,)],
         (both, weight_in, weight_out),
-        (1, 2),
+        (0, 1, 2),
         products,
         62,
+        pltpu.HBM,
     )
     sums = lax.all_to_all(sums, GX, 0, 0, tiled=True)
     sums = jnp.sum(sums.astype(F32), axis=0).astype(BF16)
@@ -238,10 +270,10 @@
             ((feats, tokens), F32),
             (pair_rows, F32),
         ],
-        (n_dev,),
-        (block_all,),
-        (0,),
-        products,
+        [(n_dev,)],
+        (block_all, both_core),
+        (0, 1),
+        32 * products,
         62,
     )
     grads = call(
@@ -252,7 +284,7 @@
             jax.ShapeDtypeStruct((units // n_dev, feats), BF16),
         ),
         [],
-        (),
+        [],
         (acts_own, cots_all, both, both_core, far, far_core),
         (),
         products,

time: 151 us -> 168 us (1.11)
  the two profiles are of different devices: /device:TPU:6 before, /device:TPU:65 now
where the time goes in v4:
time: 168 us; the launch traced here: 167 us
  blocking collectives  59.5 us (35%)
  waiting for transfers between devices  35 us (21%)
  starting transfers between devices  30.8 us (18%)
  Pallas kernels  19 us (11%)
  between operations  14.2 us (8%)
  local copies, waits for them, and re-layouts  5.62 us (3%)
  other arithmetic  2.81 us (2%)
    all_gather x1, blocking collectives, body(): block = lax.all_gather(pair, 'z', axis=0, tiled=False)  33.5 us
    all_to_all x1, waiting for transfers between devices, body(): sums = lax.all_to_all(sums, GX, 0, 0, tiled=True)  22.3 us
    all_to_all x1, blocking collectives, body(): parts = lax.all_to_all(parts, 'gy', 0, 0, tiled=True)  19.7 us
    pallas_call x4, Pallas kernels, call(): pl.pallas_call(kernel, out_shape=outs, in_specs=[pl.BlockSpec(memory_spac...  19 us
    ppermute x1, starting transfers between devices, body(): both_core = lax.ppermute(both, 'core', swap)  13.5 us
    all_to_all x1, waiting for transfers between devices, spread(): return lax.all_to_all(copies, axes, 0, 0, tiled=True)  12.8 us
    all_to_all x1, starting transfers between devices, body(): sums = lax.all_to_all(sums, GX, 0, 0, tiled=True)  6.62 us
    all_gather x1, blocking collectives, body(): block = lax.all_gather(block, 'xl', axis=0, tiled=True)  6.34 us
  transfers between devices with their start and end apart: 6, of which 2 were waited for; matrix products, arithmetic and copies ran while one was open for 1% of the time, Pallas kernels for 11%

profile of v4, /device:TPU:65, one launch (start us, length us, event | category | flops | bytes accessed | tf_op | source)
XLA Modules:
  0.0 167.1 jit_solution(1382610286857294286)
XLA Ops:
  7.2 0.0 all-gather.4.cloned.1.call-start
  7.2 0.7 pad_maximum_fusion.2
  7.9 33.5 %all-gather = bf16[1152,128]{1,0:T(8,128)(2,1)S(1)} all-gather(bf16[72,128]{1,0:T(8,128)(2,1)S(1)} %pad_maximum_fusion.2), channel_id=2, replica_groups=mesh['xl'=2,'z'=16,'gy'=8,'xh'=2,'core'=2] {'z'}, dimensions={0}, use_global_device_ids=true | all-gather | bytes 313344 | tf_op jit(solution)/shard_map/all_gather | solution.py:213
  41.5 6.3 %all_gather.17.block_hbm = bf16[32,72,128]{2,1,0:T(8,128)(2,1)} all-gather(bf16[16,72,128]{2,1,0:T(8,128)(2,1)S(1)} %bitcast.5), channel_id=1, replica_groups=mesh['xl'=2,'z'=16,'gy'=8,'xh'=2,'core'=2] {'xl'}, dimensions={0}, use_global_device_ids=true | all-gather | bytes 884736 | tf_op jit(solution)/shard_map/all_gather | solution.py:214
  47.8 0.0 all-gather.4.cloned.1.call-update
  47.8 6.3 %unit_terms.1 = bf16[8,288,128]{2,1,0:T(8,128)(2,1)} custom-call(bf16[32,72,128]{2,1,0:T(8,128)(2,1)} %all_gather.17.block_hbm, bf16[1152,1152]{1,0:T(8,128)(2,1)} %in_hbm.3, bf16[1152,1152]{1,0:T(8,128)(2,1)} %out_hbm.3), custom_call_target="tpu_custom_call" | custom-call | flops 679477248 | bytes 5898240 | tf_op jit(solution)/shard_map/unit_terms/pallas_call | solution.py:187
  54.2 19.7 %all_to_all.15 = bf16[8,288,128]{2,1,0:T(8,128)(2,1)S(1)} all-to-all(bf16[8,288,128]{2,1,0:T(8,128)(2,1)} %unit_terms.1), channel_id=1, replica_groups=mesh['xl'=2,'z'=16,'gy'=8,'xh'=2,'core'=2] {'gy'}, dimensions={0} | all-to-all | bytes 1179648 | tf_op jit(solution)/shard_map/all_to_all | solution.py:231
  73.8 0.1 convert_reduce_fusion
  74.0 0.9 broadcast_in_dim.2
  74.9 3.5 %all-to-all-start.1 = ((bf16[8,288,128]{2,1,0:T(8,128)(2,1)}), bf16[8,288,128]{2,1,0:T(8,128)(2,1)S(1)}, u32[]{:S(2)}, u32[]{:S(2)}) async-start(bf16[8,288,128]{2,1,0:T(8,128)(2,1)} %broadcast_in_dim.2), calls=%async_computation.1 | async-start | bytes 1179648 | tf_op jit(solution)/shard_map/all_to_all | solution.py:201
  78.4 12.8 %all-to-all-done.1.both_hbm.both_ref = bf16[8,288,128]{2,1,0:T(8,128)(2,1)S(1)} async-done(((bf16[8,288,128]{2,1,0:T(8,128)(2,1)}), bf16[8,288,128]{2,1,0:T(8,128)(2,1)S(1)}, u32[]{:S(2)}, u32[]{:S(2)}) %all-to-all-start.1) | async-done | bytes 589856 | tf_op jit(solution)/shard_map/all_to_all | solution.py:201
  91.2 13.5 %collective-permute-start = (bf16[8,288,128]{2,1,0:T(8,128)(2,1)S(1)}, bf16[8,288,128]{2,1,0:T(8,128)(2,1)S(1)}, u32[]{:S(2)}, u32[]{:S(2)}) collective-permute-start(bf16[8,288,128]{2,1,0:T(8,128)(2,1)S(1)} %all-to-all-done.1.both_hbm.both_ref), channel_id=1, source_target_pairs={{0,1},{1,0},{2,3},{3,2},{4,5},{5,4},{6,7},{7,6},{8,9},{9,8},{10,11... | collective-permute-start | bytes 1769480 | tf_op jit(solution)/shard_map/ppermute | solution.py:242
  104.8 0.8 pad_maximum_fusion
  105.6 4.6 %collective-permute-start.1 = (bf16[1728,128]{1,0:T(8,128)(2,1)}, bf16[1728,128]{1,0:T(8,128)(2,1)S(1)}, u32[]{:S(2)}, u32[]{:S(2)}) collective-permute-start(bf16[1728,128]{1,0:T(8,128)(2,1)} %pad_maximum_fusion), channel_id=1, source_target_pairs={{0,2},{2,0},{1,3},{3,1},{4,6},{6,4},{5,7},{7,5},{8,10},{10,8},{9,1... | collective-permute-start | bytes 1327112 | tf_op jit(solution)/shard_map/ppermute | solution.py:241
  110.2 6.3 %feature_terms.1 = bf16[32,72,128]{2,1,0:T(8,128)(2,1)} custom-call(bf16[8,288,128]{2,1,0:T(8,128)(2,1)} %copy-done, bf16[1152,1152]{1,0:T(8,128)(2,1)} %in_hbm.3, bf16[1152,1152]{1,0:T(8,128)(2,1)} %out_hbm.3), custom_call_target="tpu_custom_call" | custom-call | flops 679477248 | bytes 5898240 | tf_op jit(solution)/shard_map/feature_terms/pallas_call | solution.py:187
  116.5 6.6 %all-to-all-start.2 = ((bf16[32,72,128]{2,1,0:T(8,128)(2,1)}), bf16[32,72,128]{2,1,0:T(8,128)(2,1)}, u32[]{:S(2)}, u32[]{:S(2)}) async-start(bf16[32,72,128]{2,1,0:T(8,128)(2,1)} %feature_terms.1), calls=%async_computation.2 | async-start | bytes 1179648 | tf_op jit(solution)/shard_map/all_to_all | solution.py:257
  123.1 0.0 collective-permute-done.1.far_ref
  123.2 2.5 %collective-permute-start.2 = (bf16[1728,128]{1,0:T(8,128)(2,1)S(1)}, bf16[1728,128]{1,0:T(8,128)(2,1)}, u32[]{:S(2)}, u32[]{:S(2)}) collective-permute-start(bf16[1728,128]{1,0:T(8,128)(2,1)S(1)} %collective-permute-done.1.far_ref), channel_id=1, source_target_pairs={{0,1},{1,0},{2,3},{3,2},{4,5},{5,4},{6,7},{7,6},{8,9},{9,8},{10,11... | collective-permute-start | bytes 1327112 | tf_op jit(solution)/shard_map/ppermute | solution.py:243
  125.6 0.0 collective-permute-done.unused_hbm.core_ref
  125.7 0.0 copy-start.3
  125.7 0.0 all-gather.4.cloned.1.call-done
  125.7 0.8 copy-done.3
  126.5 3.4 %unpack.1 = (bf16[288,512]{1,0:T(8,128)(2,1)}, bf16[1152,512]{1,0:T(8,128)(2,1)}) custom-call(bf16[4,32,72,128]{3,2,1,0:T(8,128)(2,1)} %bitcast.7, bf16[8,288,128]{2,1,0:T(8,128)(2,1)} %copy-done.3), custom_call_target="tpu_custom_call" | custom-call | flops 21743271936 | bytes 2949120 | tf_op jit(solution)/shard_map/unpack/pallas_call | solution.py:187
  129.9 0.0 collective-permute-done.2.far_core_ref
  129.9 0.0 copy-done.1
  129.9 1.3 copy-done.2
  131.2 1.1 copy-done.4
  132.3 1.0 copy-done.5
  133.2 3.0 %weight_grads.1 = (bf16[288,1152]{1,0:T(8,128)(2,1)}, bf16[288,1152]{1,0:T(8,128)(2,1)}) custom-call(bf16[288,512]{1,0:T(8,128)(2,1)S(1)} %copy-done.5, bf16[1152,512]{1,0:T(8,128)(2,1)S(1)} %copy-done.2, bf16[8,288,128]{2,1,0:T(8,128)(2,1)S(1)} %copy-done.1, bf16[8,288,128]{2,1,0:T(8,128)(2,1)S(1)} %copy-done.4, ...), custom_call_target="tpu_custom_call" | custom-call | flops 679477248 | bytes 3538944 | tf_op jit(solution)/shard_map/weight_grads/pallas_call | solution.py:187
  136.2 22.3 %all-to-all-done.2 = bf16[32,72,128]{2,1,0:T(8,128)(2,1)} async-done(((bf16[32,72,128]{2,1,0:T(8,128)(2,1)}), bf16[32,72,128]{2,1,0:T(8,128)(2,1)}, u32[]{:S(2)}, u32[]{:S(2)}) %all-to-all-start.2) | async-done | bytes 589856 | tf_op jit(solution)/shard_map/all_to_all | solution.py:257
  158.5 1.2 reduce_sum.22
  159.6 0.6 fusion.1
  (10 shorter events, 0.1 us)
Async XLA Ops:
  7.2 118.5 %all-gather.4.cloned.1.call-start = ((), (), s32[]{:S(2)}) async-start(), calls=%async_computation.3 | async-start | bytes 2949120 | tf_op jit(solution)/shard_map/all_gather | solution.py:215
  74.9 16.3 %all-to-all-start.1 = ((bf16[8,288,128]{2,1,0:T(8,128)(2,1)}), bf16[8,288,128]{2,1,0:T(8,128)(2,1)S(1)}, u32[]{:S(2)}, u32[]{:S(2)}) async-start(bf16[8,288,128]{2,1,0:T(8,128)(2,1)} %broadcast_in_dim.2), calls=%async_computation.1 | async-start | bytes 1179648 | tf_op jit(solution)/shard_map/all_to_all | solution.py:201
  91.2 19.0 %copy-start = (bf16[8,288,128]{2,1,0:T(8,128)(2,1)}, bf16[8,288,128]{2,1,0:T(8,128)(2,1)S(1)}, u32[]{:S(2)}) copy-start(bf16[8,288,128]{2,1,0:T(8,128)(2,1)S(1)} %all-to-all-done.1.both_hbm.both_ref) | copy-start | bytes 1769476
  91.2 34.5 %collective-permute-start = (bf16[8,288,128]{2,1,0:T(8,128)(2,1)S(1)}, bf16[8,288,128]{2,1,0:T(8,128)(2,1)S(1)}, u32[]{:S(2)}, u32[]{:S(2)}) collective-permute-start(bf16[8,288,128]{2,1,0:T(8,128)(2,1)S(1)} %all-to-all-done.1.both_hbm.both_ref), channel_id=1, source_target_pairs={{0,1},{1,0},{2,3},{3,2},{4,5},{5,4},{6,7},{7,6},{8,9},{9,8},{10,11... | collective-permute-start | bytes 1769480 | tf_op jit(solution)/shard_map/ppermute | solution.py:242
  105.6 17.6 %collective-permute-start.1 = (bf16[1728,128]{1,0:T(8,128)(2,1)}, bf16[1728,128]{1,0:T(8,128)(2,1)S(1)}, u32[]{:S(2)}, u32[]{:S(2)}) collective-permute-start(bf16[1728,128]{1,0:T(8,128)(2,1)} %pad_maximum_fusion), channel_id=1, source_target_pairs={{0,2},{2,0},{1,3},{3,1},{4,6},{6,4},{5,7},{7,5},{8,10},{10,8},{9,1... | collective-permute-start | bytes 1327112 | tf_op jit(solution)/shard_map/ppermute | solution.py:241
  116.5 42.0 %all-to-all-start.2 = ((bf16[32,72,128]{2,1,0:T(8,128)(2,1)}), bf16[32,72,128]{2,1,0:T(8,128)(2,1)}, u32[]{:S(2)}, u32[]{:S(2)}) async-start(bf16[32,72,128]{2,1,0:T(8,128)(2,1)} %feature_terms.1), calls=%async_computation.2 | async-start | bytes 1179648 | tf_op jit(solution)/shard_map/all_to_all | solution.py:257
  123.2 6.7 %collective-permute-start.2 = (bf16[1728,128]{1,0:T(8,128)(2,1)S(1)}, bf16[1728,128]{1,0:T(8,128)(2,1)}, u32[]{:S(2)}, u32[]{:S(2)}) collective-permute-start(bf16[1728,128]{1,0:T(8,128)(2,1)S(1)} %collective-permute-done.1.far_ref), channel_id=1, source_target_pairs={{0,1},{1,0},{2,3},{3,2},{4,5},{5,4},{6,7},{7,6},{8,9},{9,8},{10,11... | collective-permute-start | bytes 1327112 | tf_op jit(solution)/shard_map/ppermute | solution.py:243
  125.7 0.8 copy-start.3
  126.5 3.4 %copy-start.1 = (bf16[8,288,128]{2,1,0:T(8,128)(2,1)S(1)}, bf16[8,288,128]{2,1,0:T(8,128)(2,1)}, u32[]{:S(2)}) copy-start(bf16[8,288,128]{2,1,0:T(8,128)(2,1)} %copy-done) | copy-start | bytes 1769476
  129.9 1.3 copy-start.2
  131.2 1.1 copy-start.4
  132.3 1.0 copy-start.5
Sparse Core Ops, SparseCore 0:
  48.0 42.7 all-gather.3

commit v5 on v4

v5 whole, which is shorter than its diff:
```python
import functools
import math

import jax
import jax.numpy as jnp
from jax import lax
from jax.experimental import pallas as pl
from jax.experimental.pallas import tpu as pltpu
from jax.sharding import Mesh, PartitionSpec as P

F32 = jnp.float32
BF16 = jnp.bfloat16
GX = ("xl", "z")
DEV = ("xh", "core")
VMEM = pl.BlockSpec(memory_space=pltpu.VMEM)


def silu_slope(pre):
    sig = jax.nn.sigmoid(pre)
    return sig * (1.0 + pre * (1.0 - sig))


def dot(left, right, contract):
    return lax.dot_general(left, right, (contract, ((), ())), preferred_element_type=F32)


def turned(right):
    return right.astype(F32).T.astype(BF16)


def columns_dot(left, columns_ref, to_ref):
    width = 384
    for at in range(0, columns_ref.shape[1], width):
        to_ref[at : at + width] = dot(left, columns_ref[:, at : at + width], ((1,), (0,))).T


def unit_terms(
    block_hbm, in_hbm, out_hbm, parts_hbm,
    block_ref, parts_ref, in_ref, out_ref, acts_ref, cots_ref, pair_ref, sems,
):
    load = pltpu.make_async_copy(block_hbm, block_ref, sems.at[0])
    load_in = pltpu.make_async_copy(in_hbm, in_ref, sems.at[1])
    load_out = pltpu.make_async_copy(out_hbm, out_ref, sems.at[2])
    load.start()
    load_in.start()
    own = block_ref.shape[1] // 2
    load.wait()
    load_out.start()
    for g in range(block_ref.shape[0]):
        pair_ref[...] = block_ref[g].astype(F32)
        acts_ref[g * own : (g + 1) * own] = pair_ref[:own]
        cots_ref[g * own : (g + 1) * own] = pair_ref[own:]
    cots, acts = cots_ref[...].astype(BF16), turned(acts_ref[...])
    pre_ref = acts_ref
    load_in.wait()
    columns_dot(acts, in_ref, pre_ref)
    shares, share = parts_ref.shape[0], parts_ref.shape[1] // 2
    for k in range(shares):
        parts_ref[k, :share] = pre_ref[k * share : (k + 1) * share].astype(BF16)
    load_out.wait()
    each = 2
    stores = []
    for k in range(0, shares, each):
        grad = dot(out_ref[k * share : (k + each) * share], cots, ((1,), (0,))).astype(BF16)
        for j in range(each):
            parts_ref[k + j, share:] = grad[j * share : (j + 1) * share]
        part = pl.ds(k, each)
        stores.append(pltpu.make_async_copy(parts_ref.at[part], parts_hbm.at[part], sems.at[3 + k // each]))
        stores[-1].start()
    for store in stores:
        store.wait()


def feature_terms(
    both_hbm, in_hbm, out_hbm, sums_hbm, near_hbm, far_hbm,
    both_ref, sums_ref, in_ref, out_ref, out_rows_ref, in_rows_ref, pair_ref, sems,
):
    shares, share = both_ref.shape[0], both_ref.shape[1] // 2
    load = pltpu.make_async_copy(both_hbm, both_ref, sems.at[0])
    load_in = pltpu.make_async_copy(in_hbm, in_ref, sems.at[10])
    load_out = pltpu.make_async_copy(out_hbm, out_ref, sems.at[1])
    load.start()
    load_in.start()
    quarter, half = near_hbm.shape[0] - shares, far_hbm.shape[0] - shares
    load.wait()
    stores = [
        pltpu.make_async_copy(source, target, sems.at[2 + i])
        for i, (source, target) in enumerate(
            [
                (both_ref.at[:, pl.ds(share, share)], near_hbm.at[pl.ds(0, shares)]),
                (both_ref.at[pl.ds(relative(1) * quarter, quarter), pl.ds(0, share)], near_hbm.at[pl.ds(shares, quarter)]),
                (both_ref.at[:, pl.ds(share, share)], far_hbm.at[pl.ds(0, shares)]),
                (both_ref.at[pl.ds((1 - lax.axis_index("xh")) * half, half), pl.ds(0, share)], far_hbm.at[pl.ds(shares, half)]),
            ]
        )
    ]
    load_out.start()
    for store in stores:
        store.start()
    grad = jnp.concatenate([both_ref[k, share:] for k in range(shares)], axis=0)
    load_in.wait()
    in_rows_ref[...] = dot(in_ref[...], grad, ((1,), (0,)))
    hidden = turned(jnp.concatenate([both_ref[k, :share] for k in range(shares)], axis=0))
    load_out.wait()
    columns_dot(hidden, out_ref, out_rows_ref)
    members, own = sums_ref.shape[0], sums_ref.shape[1] // 2
    each = members // 4
    for c in range(4):
        for g in range(c * each, (c + 1) * each):
            pair_ref[:own] = out_rows_ref[g * own : (g + 1) * own]
            pair_ref[own:] = in_rows_ref[g * own : (g + 1) * own]
            sums_ref[g] = pair_ref[...].astype(BF16)
        span = pl.ds(c * each, each)
        stores.append(pltpu.make_async_copy(sums_ref.at[span], sums_hbm.at[span], sems.at[6 + c]))
        stores[-1].start()
    for store in stores:
        store.wait()


def relative(step):
    xh, core = lax.axis_index("xh"), lax.axis_index("core")
    return 2 * (1 - xh if step & 2 else xh) + (1 - core if step & 1 else core)


def unpack(block_hbm, acts_out, cots_out, block_ref, acts_ref, cots_ref, pair_ref, sems):
    groups, members, rows, tokens = block_ref.shape
    own = rows // 2
    copies = [
        pltpu.make_async_copy(block_hbm.at[relative(t)], block_ref.at[t], sems.at[t])
        for t in range(groups)
    ]
    for copy in copies:
        copy.start()
    owner = relative(0)
    for t in range(groups):
        copies[t].wait()
        lanes = slice(t * tokens, (t + 1) * tokens)
        for g in range(members):
            pair_ref[...] = block_ref[t, g].astype(F32)
            cots_ref[g * own : (g + 1) * own] = pair_ref[own:]
        cots_out[:, lanes] = cots_ref[...].astype(BF16)
        for g in range(members // groups):
            pair_ref[...] = block_ref[t, owner * (members // groups) + g].astype(F32)
            acts_ref[g * own : (g + 1) * own] = pair_ref[:own]
        acts_out[:, lanes] = acts_ref[...].astype(BF16)


def weight_grads(factor, acts_ref, cots_ref, both_ref, near_ref, far_ref, far_near_ref, in_ref, out_ref):
    shares, share = both_ref.shape[0], both_ref.shape[1] // 2
    pieces = out_ref.shape[0] // share
    owner, core = relative(0), lax.axis_index("core")
    others = (near_ref, far_ref, far_near_ref)
    acts = acts_ref[...]
    own_grads = jnp.concatenate([both_ref[k, share:] for k in range(shares)], axis=0)
    grads = jnp.concatenate(
        [own_grads] + [jnp.concatenate([ref[k] for k in range(shares)], axis=0) for ref in others], axis=1
    )
    width = 384
    for at in range(0, in_ref.shape[1], width):
        part = grads[at : at + width]
        in_ref[:, at : at + width] = (dot(acts, part, ((1,), (1,))) * factor).astype(BF16)
    places = (shares, shares + core * pieces, shares + core * pieces)
    own_hidden = jnp.concatenate([both_ref[owner * pieces + j, :share] for j in range(pieces)], axis=0)
    hidden = jnp.concatenate(
        [own_hidden]
        + [
            jnp.concatenate([ref[place + j] for j in range(pieces)], axis=0)
            for ref, place in zip(others, places)
        ],
        axis=1,
    )
    for at in range(0, out_ref.shape[1], width):
        part = cots_ref[at : at + width]
        out_ref[:, at : at + width] = (dot(hidden, part, ((1,), (1,))) * factor).astype(BF16)


def call(kernel, name, outs, scratch, sems, args, in_hbm, flops, vmem, out_hbm=()):
    n_bytes = sum(a.size * a.dtype.itemsize for a in args)
    return pl.pallas_call(
        kernel,
        out_shape=outs,
        in_specs=[pl.BlockSpec(memory_space=pltpu.HBM) if i in in_hbm else VMEM for i in range(len(args))],
        out_specs=tuple(pl.BlockSpec(memory_space=pltpu.HBM) if i in out_hbm else VMEM for i in range(len(outs))),
        scratch_shapes=[pltpu.VMEM(*s) for s in scratch] + [pltpu.SemaphoreType.DMA(s) for s in sems],
        compiler_params=pltpu.CompilerParams(vmem_limit_bytes=vmem * 2**20),
        cost_estimate=pl.CostEstimate(flops=flops, bytes_accessed=n_bytes, transcendentals=0),
        name=name,
    )(*args)


def spread(local, axes):
    copies = jnp.broadcast_to(local[None], (lax.axis_size(axes), *local.shape))
    return lax.all_to_all(copies, axes, 0, 0, tiled=True)


def body(activations, weight_in, weight_out, cotangent):
    own, tokens = activations.shape
    feats, units = weight_in.shape
    n_gx, n_gy, n_dev = (lax.axis_size(a) for a in (GX, "gy", DEV))
    share = units // n_gy
    pair_rows = (2 * own, tokens)
    products = 4 * feats * units * tokens

    pair = jnp.concatenate([activations, cotangent], axis=0)
    block = lax.all_gather(pair, "z", axis=0, tiled=False)
    block = lax.all_gather(block, "xl", axis=0, tiled=True)
    block_all = lax.all_gather(block, DEV, axis=0, tiled=False)

    weight = (weight_in.shape, BF16)
    rows = ((feats, tokens), F32)
    (parts,) = call(
        unit_terms,
        "unit_terms",
        (jax.ShapeDtypeStruct((n_gy, 2 * share, tokens), BF16),),
        [((n_gx, *pair_rows), BF16), ((n_gy, 2 * share, tokens), BF16), weight, weight, rows, rows, (pair_rows, F32)],
        [(3 + n_gy // 2,)],
        (block, weight_in, weight_out),
        (0, 1, 2),
        products,
        62,
        (0,),
    )
    parts = lax.all_to_all(parts, "gy", 0, 0, tiled=True)
    total = jnp.sum(parts.astype(F32), axis=0)
    pre, grad_hidden = total[:share], total[share:]
    hidden = jax.nn.silu(pre).astype(BF16)
    grad_pre = (grad_hidden * silu_slope(pre)).astype(BF16)
    both = spread(jnp.concatenate([hidden, grad_pre], axis=0), "gy").reshape(n_gy, 2 * share, tokens)
    sums, near, far = call(
        feature_terms,
        "feature_terms",
        (
            jax.ShapeDtypeStruct((n_gx, *pair_rows), BF16),
            jax.ShapeDtypeStruct((n_gy + n_gy // n_dev, share, tokens), BF16),
            jax.ShapeDtypeStruct((n_gy + n_gy // 2, share, tokens), BF16),
        ),
        [((n_gy, 2 * share, tokens), BF16), ((n_gx, *pair_rows), BF16), weight, weight, rows, rows, (pair_rows, F32)],
        [(11,)],
        (both, weight_in, weight_out),
        (0, 1, 2),
        products,
        62,
        (0, 1, 2),
    )
    swap = [(0, 1), (1, 0)]
    far = lax.ppermute(far, "xh", swap)
    near = lax.ppermute(near, "core", swap)
    far_near = lax.ppermute(far, "core", swap)
    sums = lax.all_to_all(sums, GX, 0, 0, tiled=True)
    sums = jnp.sum(sums.astype(F32), axis=0).astype(BF16)

    acts_own, cots_all = call(
        unpack,
        "unpack",
        (
            jax.ShapeDtypeStruct((feats // n_dev, n_dev * tokens), BF16),
            jax.ShapeDtypeStruct((feats, n_dev * tokens), BF16),
        ),
        [
            (block_all.shape, BF16),
            ((feats // n_dev, tokens), F32),
            ((feats, tokens), F32),
            (pair_rows, F32),
        ],
        [(n_dev,)],
        (block_all,),
        (0,),
        products,
        62,
    )
    grads = call(
        functools.partial(weight_grads, 1.0 / math.sqrt(n_dev * tokens)),
        "weight_grads",
        (
            jax.ShapeDtypeStruct((feats // n_dev, units), BF16),
            jax.ShapeDtypeStruct((units // n_dev, feats), BF16),
        ),
        [],
        [],
        (acts_own, cots_all, both, near, far, far_near),
        (),
        products,
        32,
    )
    return (sums[:own], sums[own:], *grads)


def solution(mesh):
    shape = mesh.devices.shape
    fine = Mesh(
        mesh.devices.reshape(2, shape[0] // 2, shape[1], 2, shape[2] // 2),
        ("xl", "z", "gy", "xh", "core"),
    )
    return jax.shard_map(
        body,
        mesh=fine,
        in_specs=(P(("gy", *GX), DEV), P("gy", GX), P(GX, "gy"), P(("gy", *GX), DEV)),
        out_specs=(P(("gy", *GX), DEV), P(("gy", *GX), DEV), P(("gy", *DEV), GX), P((*GX, *DEV), "gy")),
        check_vma=False,
    )
```

time: 168 us -> 149 us (0.89)
  the two profiles are of different devices: /device:TPU:65 before, /device:TPU:6 now
where the time goes in v5:
time: 149 us; the launch traced here: 147 us
  blocking collectives  68.3 us (46%)
  waiting for transfers between devices  23.8 us (16%)
  starting transfers between devices  20.5 us (14%)
  Pallas kernels  15.3 us (10%)
  between operations  14.2 us (10%)
  local copies, waits for them, and re-layouts  2.92 us (2%)
  other arithmetic  2.02 us (1%)
    all_gather x1, blocking collectives, body(): block = lax.all_gather(pair, 'z', axis=0, tiled=False)  43.8 us
    all_to_all x1, blocking collectives, spread(): return lax.all_to_all(copies, axes, 0, 0, tiled=True)  17.1 us
    pallas_call x4, Pallas kernels, call(): pl.pallas_call(kernel, out_shape=outs, in_specs=[pl.BlockSpec(memory_spac...  15.3 us
    all_to_all x1, waiting for transfers between devices, body(): parts = lax.all_to_all(parts, 'gy', 0, 0, tiled=True)  13.4 us
    ppermute x1, waiting for transfers between devices, body(): far = lax.ppermute(far, 'xh', swap)  9.74 us
    all_gather x1, blocking collectives, body(): block = lax.all_gather(block, 'xl', axis=0, tiled=True)  7.49 us
    all_to_all x1, starting transfers between devices, body(): parts = lax.all_to_all(parts, 'gy', 0, 0, tiled=True)  7.11 us
    all_to_all x1, starting transfers between devices, body(): sums = lax.all_to_all(sums, GX, 0, 0, tiled=True)  5.7 us
  transfers between devices with their start and end apart: 6, of which 2 were waited for; matrix products, arithmetic and copies ran while one was open for 0% of the time, Pallas kernels for 7%

profile of v5, /device:TPU:6, one launch (start us, length us, event | category | flops | bytes accessed | tf_op | source)
XLA Modules:
  0.0 147.1 jit_solution(121641812679757247)
XLA Ops:
  7.2 0.7 pad_maximum_fusion.1
  7.9 43.8 %all-gather = bf16[1152,128]{1,0:T(8,128)(2,1)S(1)} all-gather(bf16[72,128]{1,0:T(8,128)(2,1)S(1)} %pad_maximum_fusion.1), channel_id=2, replica_groups=mesh['xl'=2,'z'=16,'gy'=8,'xh'=2,'core'=2] {'z'}, dimensions={0}, use_global_device_ids=true | all-gather | bytes 313344 | tf_op jit(solution)/shard_map/all_gather | solution.py:205
  51.7 7.5 %all_gather.17.block_hbm = bf16[32,72,128]{2,1,0:T(8,128)(2,1)} all-gather(bf16[16,72,128]{2,1,0:T(8,128)(2,1)S(1)} %bitcast.2), channel_id=1, replica_groups=mesh['xl'=2,'z'=16,'gy'=8,'xh'=2,'core'=2] {'xl'}, dimensions={0}, use_global_device_ids=true | all-gather | bytes 884736 | tf_op jit(solution)/shard_map/all_gather | solution.py:206
  59.2 4.6 %unit_terms.1 = bf16[8,288,128]{2,1,0:T(8,128)(2,1)} custom-call(bf16[32,72,128]{2,1,0:T(8,128)(2,1)} %all_gather.17.block_hbm, bf16[1152,1152]{1,0:T(8,128)(2,1)} %in_hbm.3, bf16[1152,1152]{1,0:T(8,128)(2,1)} %out_hbm.3), custom_call_target="tpu_custom_call" | custom-call | flops 679477248 | bytes 5898240 | tf_op jit(solution)/shard_map/unit_terms/pallas_call | solution.py:179
  63.8 7.1 %all-to-all-start = ((bf16[8,288,128]{2,1,0:T(8,128)(2,1)}), bf16[8,288,128]{2,1,0:T(8,128)(2,1)S(1)}, u32[]{:S(2)}, u32[]{:S(2)}) async-start(bf16[8,288,128]{2,1,0:T(8,128)(2,1)} %unit_terms.1), calls=%async_computation | async-start | bytes 1179648 | tf_op jit(solution)/shard_map/all_to_all | solution.py:223
  70.9 0.0 all-gather.4.cloned.1.call-start
  70.9 0.7 all-gather.4.cloned.1.call-update
  71.6 13.4 %all-to-all-done = bf16[8,288,128]{2,1,0:T(8,128)(2,1)S(1)} async-done(((bf16[8,288,128]{2,1,0:T(8,128)(2,1)}), bf16[8,288,128]{2,1,0:T(8,128)(2,1)S(1)}, u32[]{:S(2)}, u32[]{:S(2)}) %all-to-all-start) | async-done | bytes 589856 | tf_op jit(solution)/shard_map/all_to_all | solution.py:223
  85.0 0.1 convert_reduce_fusion
  85.1 0.1 broadcast_in_dim.2
  85.2 17.1 %all_to_all.15.both_hbm.both_ref = bf16[8,288,128]{2,1,0:T(8,128)(2,1)} all-to-all(bf16[8,288,128]{2,1,0:T(8,128)(2,1)S(1)} %broadcast_in_dim.2), channel_id=1, replica_groups=mesh['xl'=2,'z'=16,'gy'=8,'xh'=2,'core'=2] {'gy'}, dimensions={0} | all-to-all | bytes 1179648 | tf_op jit(solution)/shard_map/all_to_all | solution.py:193
  102.3 5.4 %feature_terms.1 = (bf16[32,72,128]{2,1,0:T(8,128)(2,1)}, bf16[10,144,128]{2,1,0:T(8,128)(2,1)}, bf16[12,144,128]{2,1,0:T(8,128)(2,1)}) custom-call(bf16[8,288,128]{2,1,0:T(8,128)(2,1)} %all_to_all.15.both_hbm.both_ref, bf16[1152,1152]{1,0:T(8,128)(2,1)} %in_hbm.3, bf16[1152,1152]{1,0:T(8,128)(2,1)} %out_hbm.3), custom_call_target="tpu_custom_call" | custom-call | flops 679477248 | bytes 5898240 | tf_op jit(solution)/shard_map/feature_terms/pallas_call | solution.py:179
  107.7 0.0 copy-start
  107.7 5.7 %all-to-all-start.2 = ((bf16[32,72,128]{2,1,0:T(8,128)(2,1)}), bf16[32,72,128]{2,1,0:T(8,128)(2,1)}, u32[]{:S(2)}, u32[]{:S(2)}) async-start(bf16[32,72,128]{2,1,0:T(8,128)(2,1)} %get-tuple-element.11), calls=%async_computation.2 | async-start | bytes 1179648 | tf_op jit(solution)/shard_map/all_to_all | solution.py:249
  113.4 3.4 %collective-permute-start.1 = (bf16[12,144,128]{2,1,0:T(8,128)(2,1)}, bf16[12,144,128]{2,1,0:T(8,128)(2,1)S(1)}, u32[]{:S(2)}, u32[]{:S(2)}) collective-permute-start(bf16[12,144,128]{2,1,0:T(8,128)(2,1)} %get-tuple-element.15), channel_id=1, source_target_pairs={{0,2},{2,0},{1,3},{3,1},{4,6},{6,4},{5,7},{7,5},{8,10},{10,8},{9,1... | collective-permute-start | bytes 1327112 | tf_op jit(solution)/shard_map/ppermute | solution.py:246
  116.8 9.7 %collective-permute-done.1.far_ref = bf16[12,144,128]{2,1,0:T(8,128)(2,1)S(1)} collective-permute-done((bf16[12,144,128]{2,1,0:T(8,128)(2,1)}, bf16[12,144,128]{2,1,0:T(8,128)(2,1)S(1)}, u32[]{:S(2)}, u32[]{:S(2)}) %collective-permute-start.1) | collective-permute-done | bytes 442400 | tf_op jit(solution)/shard_map/ppermute | solution.py:246
  126.5 1.9 %collective-permute-start.2 = (bf16[12,144,128]{2,1,0:T(8,128)(2,1)S(1)}, bf16[12,144,128]{2,1,0:T(8,128)(2,1)S(1)}, u32[]{:S(2)}, u32[]{:S(2)}) collective-permute-start(bf16[12,144,128]{2,1,0:T(8,128)(2,1)S(1)} %collective-permute-done.1.far_ref), channel_id=1, source_target_pairs={{0,1},{1,0},{2,3},{3,2},{4,5},{5,4},{6,7},{7,6},{8,9},{9,8},{10,11... | collective-permute-start | bytes 1327112 | tf_op jit(solution)/shard_map/ppermute | solution.py:248
  128.4 2.4 %collective-permute-start = (bf16[10,144,128]{2,1,0:T(8,128)(2,1)}, bf16[10,144,128]{2,1,0:T(8,128)(2,1)S(1)}, u32[]{:S(2)}, u32[]{:S(2)}) collective-permute-start(bf16[10,144,128]{2,1,0:T(8,128)(2,1)} %get-tuple-element.14), channel_id=1, source_target_pairs={{0,1},{1,0},{2,3},{3,2},{4,5},{5,4},{6,7},{7,6},{8,9},{9,8},{10,11... | collective-permute-start | bytes 1105928 | tf_op jit(solution)/shard_map/ppermute | solution.py:247
  130.9 0.0 all-gather.4.cloned.1.call-done
  130.9 3.3 %unpack.1 = (bf16[288,512]{1,0:T(8,128)(2,1)}, bf16[1152,512]{1,0:T(8,128)(2,1)}) custom-call(bf16[4,32,72,128]{3,2,1,0:T(8,128)(2,1)} %bitcast.3), custom_call_target="tpu_custom_call" | custom-call | flops 679477248 | bytes 2359296 | tf_op jit(solution)/shard_map/unpack/pallas_call | solution.py:179
  134.2 0.0 collective-permute-done.near_ref
  134.2 0.0 collective-permute-done.2.far_near_ref
  134.3 0.0 copy-done
  134.3 0.0 copy-start.1
  134.3 1.3 copy-done.1
  135.5 0.0 copy-start.2
  135.5 1.0 copy-done.2
  136.5 2.0 %weight_grads.1 = (bf16[288,1152]{1,0:T(8,128)(2,1)}, bf16[288,1152]{1,0:T(8,128)(2,1)}) custom-call(bf16[288,512]{1,0:T(8,128)(2,1)S(1)} %copy-done.2, bf16[1152,512]{1,0:T(8,128)(2,1)S(1)} %copy-done.1, bf16[8,288,128]{2,1,0:T(8,128)(2,1)S(1)} %copy-done, bf16[10,144,128]{2,1,0:T(8,128)(2,1)S(1)} %collective-permute-done.near_ref, ...), custom_call_target="tpu_custom_call" | custom-call | flops 679477248 | bytes 3317760 | tf_op jit(solution)/shard_map/weight_grads/pallas_call | solution.py:179
  138.5 0.0 all-to-all-done.2
  138.5 1.2 reduce_sum.22
  139.6 0.6 fusion.1
  (2 shorter events, 0.1 us)
Async XLA Ops:
  63.8 21.2 %all-to-all-start = ((bf16[8,288,128]{2,1,0:T(8,128)(2,1)}), bf16[8,288,128]{2,1,0:T(8,128)(2,1)S(1)}, u32[]{:S(2)}, u32[]{:S(2)}) async-start(bf16[8,288,128]{2,1,0:T(8,128)(2,1)} %unit_terms.1), calls=%async_computation | async-start | bytes 1179648 | tf_op jit(solution)/shard_map/all_to_all | solution.py:223
  70.9 60.0 %all-gather.4.cloned.1.call-start = ((), (), s32[]{:S(2)}) async-start(), calls=%async_computation.3 | async-start | bytes 2949120 | tf_op jit(solution)/shard_map/all_gather | solution.py:207
  107.7 26.6 %copy-start = (bf16[8,288,128]{2,1,0:T(8,128)(2,1)S(1)}, bf16[8,288,128]{2,1,0:T(8,128)(2,1)}, u32[]{:S(2)}) copy-start(bf16[8,288,128]{2,1,0:T(8,128)(2,1)} %all_to_all.15.both_hbm.both_ref) | copy-start | bytes 1769476
  107.7 30.8 %all-to-all-start.2 = ((bf16[32,72,128]{2,1,0:T(8,128)(2,1)}), bf16[32,72,128]{2,1,0:T(8,128)(2,1)}, u32[]{:S(2)}, u32[]{:S(2)}) async-start(bf16[32,72,128]{2,1,0:T(8,128)(2,1)} %get-tuple-element.11), calls=%async_computation.2 | async-start | bytes 1179648 | tf_op jit(solution)/shard_map/all_to_all | solution.py:249
  113.4 13.1 %collective-permute-start.1 = (bf16[12,144,128]{2,1,0:T(8,128)(2,1)}, bf16[12,144,128]{2,1,0:T(8,128)(2,1)S(1)}, u32[]{:S(2)}, u32[]{:S(2)}) collective-permute-start(bf16[12,144,128]{2,1,0:T(8,128)(2,1)} %get-tuple-element.15), channel_id=1, source_target_pairs={{0,2},{2,0},{1,3},{3,1},{4,6},{6,4},{5,7},{7,5},{8,10},{10,8},{9,1... | collective-permute-start | bytes 1327112 | tf_op jit(solution)/shard_map/ppermute | solution.py:246
  126.5 7.7 %collective-permute-start.2 = (bf16[12,144,128]{2,1,0:T(8,128)(2,1)S(1)}, bf16[12,144,128]{2,1,0:T(8,128)(2,1)S(1)}, u32[]{:S(2)}, u32[]{:S(2)}) collective-permute-start(bf16[12,144,128]{2,1,0:T(8,128)(2,1)S(1)} %collective-permute-done.1.far_ref), channel_id=1, source_target_pairs={{0,1},{1,0},{2,3},{3,2},{4,5},{5,4},{6,7},{7,6},{8,9},{9,8},{10,11... | collective-permute-start | bytes 1327112 | tf_op jit(solution)/shard_map/ppermute | solution.py:248
  128.4 5.8 %collective-permute-start = (bf16[10,144,128]{2,1,0:T(8,128)(2,1)}, bf16[10,144,128]{2,1,0:T(8,128)(2,1)S(1)}, u32[]{:S(2)}, u32[]{:S(2)}) collective-permute-start(bf16[10,144,128]{2,1,0:T(8,128)(2,1)} %get-tuple-element.14), channel_id=1, source_target_pairs={{0,1},{1,0},{2,3},{3,2},{4,5},{5,4},{6,7},{7,6},{8,9},{9,8},{10,11... | collective-permute-start | bytes 1105928 | tf_op jit(solution)/shard_map/ppermute | solution.py:247
  134.3 1.3 copy-start.1
  135.5 1.0 copy-start.2
Sparse Core Ops, SparseCore 0:
  74.4 30.1 all-gather.3

commit v6 on v5

--- a/solution.py
+++ b/solution.py
@@ -145,6 +145,20 @@
         acts_out[:, lanes] = acts_ref[...].astype(BF16)
 
 
+def forward(far_ref, after_hbm, out_ref, sems):
+    pieces = far_ref.shape[0] - out_ref.shape[0]
+    shares = out_ref.shape[0] - pieces
+    other = shares + (1 - lax.axis_index("core")) * pieces
+    copies = [
+        pltpu.make_async_copy(far_ref.at[pl.ds(0, shares)], out_ref.at[pl.ds(0, shares)], sems.at[0]),
+        pltpu.make_async_copy(far_ref.at[pl.ds(other, pieces)], out_ref.at[pl.ds(shares, pieces)], sems.at[1]),
+    ]
+    for copy in copies:
+        copy.start()
+    for copy in copies:
+        copy.wait()
+
+
 def weight_grads(factor, acts_ref, cots_ref, both_ref, near_ref, far_ref, far_near_ref, in_ref, out_ref):
     shares, share = both_ref.shape[0], both_ref.shape[1] // 2
     pieces = out_ref.shape[0] // share
@@ -159,7 +173,7 @@
     for at in range(0, in_ref.shape[1], width):
         part = grads[at : at + width]
         in_ref[:, at : at + width] = (dot(acts, part, ((1,), (1,))) * factor).astype(BF16)
-    places = (shares, shares + core * pieces, shares + core * pieces)
+    places = (shares, shares + core * pieces, shares)
     own_hidden = jnp.concatenate([both_ref[owner * pieces + j, :share] for j in range(pieces)], axis=0)
     hidden = jnp.concatenate(
         [own_hidden]
@@ -245,7 +259,10 @@
     swap = [(0, 1), (1, 0)]
     far = lax.ppermute(far, "xh", swap)
     near = lax.ppermute(near, "core", swap)
-    far_near = lax.ppermute(far, "core", swap)
+    (far_near,) = call(
+        forward, "forward", (jax.ShapeDtypeStruct(near.shape, BF16),), [], [(2,)], (far, near), (1,), 0, 32
+    )
+    far_near = lax.ppermute(far_near, "core", swap)
     sums = lax.all_to_all(sums, GX, 0, 0, tiled=True)
     sums = jnp.sum(sums.astype(F32), axis=0).astype(BF16)
 
@@ -266,7 +283,7 @@
         (block_all,),
         (0,),
         products,
-        62,
+        40,
     )
     grads = call(
         functools.partial(weight_grads, 1.0 / math.sqrt(n_dev * tokens)),

time: 149 us -> 145 us (0.973)
  Pallas kernels: 15.3 us -> 13.8 us
    ppermute x1, waiting for transfers between devices: 9.74 us -> 5.94 us  [body(): far = lax.ppermute(far, 'xh', swap)]
    all_to_all x1, waiting for transfers between devices: 0.01 us -> 2.31 us  [body(): sums = lax.all_to_all(sums, GX, 0, 0, tiled=True)]
    ppermute x1, waiting for transfers between devices: 0.01 us -> 1.86 us  [body(): near = lax.ppermute(near, 'core', swap)]
    pallas_call x4 -> x5, Pallas kernels: 15.3 us -> 13.8 us  [call(): pl.pallas_call(kernel, out_shape=outs, in_specs=[pl.BlockSpec(memory_spac...]
  transfers between devices with their start and end apart: 6 -> 6, of which waited for: 2 -> 4; matrix products, arithmetic and copies ran while one was open for 0% -> 0% of each run, Pallas kernels for 7% -> 6%
where the time goes in v6:
time: 145 us; the launch traced here: 144 us
  blocking collectives  68.4 us (47%)
  waiting for transfers between devices  24.2 us (17%)
  starting transfers between devices  20 us (14%)
  between operations  14.2 us (10%)
  Pallas kernels  13.8 us (10%)
  local copies, waits for them, and re-layouts  2.35 us (2%)
    all_gather x1, blocking collectives, body(): block = lax.all_gather(pair, 'z', axis=0, tiled=False)  43.8 us
    all_to_all x1, blocking collectives, spread(): return lax.all_to_all(copies, axes, 0, 0, tiled=True)  17.1 us
    pallas_call x5, Pallas kernels, call(): pl.pallas_call(kernel, out_shape=outs, in_specs=[pl.BlockSpec(memory_spac...  13.8 us
    all_to_all x1, waiting for transfers between devices, body(): parts = lax.all_to_all(parts, 'gy', 0, 0, tiled=True)  13.4 us
    all_gather x1, blocking collectives, body(): block = lax.all_gather(block, 'xl', axis=0, tiled=True)  7.49 us
    all_to_all x1, starting transfers between devices, body(): parts = lax.all_to_all(parts, 'gy', 0, 0, tiled=True)  7.11 us
    ppermute x1, waiting for transfers between devices, body(): far = lax.ppermute(far, 'xh', swap)  5.94 us
    all_to_all x1, starting transfers between devices, body(): sums = lax.all_to_all(sums, GX, 0, 0, tiled=True)  5.64 us
  transfers between devices with their start and end apart: 6, of which 4 were waited for; matrix products, arithmetic and copies ran while one was open for 0% of the time, Pallas kernels for 6%

profile of v6, /device:TPU:6, one launch (start us, length us, event | category | flops | bytes accessed | tf_op | source)
XLA Modules:
  0.0 143.9 jit_solution(5791284611176146787)
XLA Ops:
  7.2 0.7 pad_maximum_fusion.1
  7.9 43.8 %all-gather = bf16[1152,128]{1,0:T(8,128)(2,1)S(1)} all-gather(bf16[72,128]{1,0:T(8,128)(2,1)S(1)} %pad_maximum_fusion.1), channel_id=2, replica_groups=mesh['xl'=2,'z'=16,'gy'=8,'xh'=2,'core'=2] {'z'}, dimensions={0}, use_global_device_ids=true | all-gather | bytes 313344 | tf_op jit(solution)/shard_map/all_gather | solution.py:219
  51.7 7.5 %all_gather.17.block_hbm = bf16[32,72,128]{2,1,0:T(8,128)(2,1)} all-gather(bf16[16,72,128]{2,1,0:T(8,128)(2,1)S(1)} %bitcast.3), channel_id=1, replica_groups=mesh['xl'=2,'z'=16,'gy'=8,'xh'=2,'core'=2] {'xl'}, dimensions={0}, use_global_device_ids=true | all-gather | bytes 884736 | tf_op jit(solution)/shard_map/all_gather | solution.py:220
  59.2 4.6 %unit_terms.1 = bf16[8,288,128]{2,1,0:T(8,128)(2,1)} custom-call(bf16[32,72,128]{2,1,0:T(8,128)(2,1)} %all_gather.17.block_hbm, bf16[1152,1152]{1,0:T(8,128)(2,1)} %in_hbm.3, bf16[1152,1152]{1,0:T(8,128)(2,1)} %out_hbm.3), custom_call_target="tpu_custom_call" | custom-call | flops 679477248 | bytes 5898240 | tf_op jit(solution)/shard_map/unit_terms/pallas_call | solution.py:193
  63.8 7.1 %all-to-all-start = ((bf16[8,288,128]{2,1,0:T(8,128)(2,1)}), bf16[8,288,128]{2,1,0:T(8,128)(2,1)S(1)}, u32[]{:S(2)}, u32[]{:S(2)}) async-start(bf16[8,288,128]{2,1,0:T(8,128)(2,1)} %unit_terms.1), calls=%async_computation | async-start | bytes 1179648 | tf_op jit(solution)/shard_map/all_to_all | solution.py:237
  70.9 0.0 all-gather.4.cloned.1.call-start
  70.9 0.7 all-gather.4.cloned.1.call-update
  71.6 13.4 %all-to-all-done = bf16[8,288,128]{2,1,0:T(8,128)(2,1)S(1)} async-done(((bf16[8,288,128]{2,1,0:T(8,128)(2,1)}), bf16[8,288,128]{2,1,0:T(8,128)(2,1)S(1)}, u32[]{:S(2)}, u32[]{:S(2)}) %all-to-all-start) | async-done | bytes 589856 | tf_op jit(solution)/shard_map/all_to_all | solution.py:237
  85.0 0.1 convert_reduce_fusion
  85.1 0.1 broadcast_in_dim.2
  85.2 17.1 %all_to_all.15.both_hbm.both_ref = bf16[8,288,128]{2,1,0:T(8,128)(2,1)} all-to-all(bf16[8,288,128]{2,1,0:T(8,128)(2,1)S(1)} %broadcast_in_dim.2), channel_id=1, replica_groups=mesh['xl'=2,'z'=16,'gy'=8,'xh'=2,'core'=2] {'gy'}, dimensions={0} | all-to-all | bytes 1179648 | tf_op jit(solution)/shard_map/all_to_all | solution.py:207
  102.3 5.4 %feature_terms.1 = (bf16[32,72,128]{2,1,0:T(8,128)(2,1)}, bf16[10,144,128]{2,1,0:T(8,128)(2,1)}, bf16[12,144,128]{2,1,0:T(8,128)(2,1)}) custom-call(bf16[8,288,128]{2,1,0:T(8,128)(2,1)} %all_to_all.15.both_hbm.both_ref, bf16[1152,1152]{1,0:T(8,128)(2,1)} %in_hbm.3, bf16[1152,1152]{1,0:T(8,128)(2,1)} %out_hbm.3), custom_call_target="tpu_custom_call" | custom-call | flops 679477248 | bytes 5898240 | tf_op jit(solution)/shard_map/feature_terms/pallas_call | solution.py:193
  107.7 0.0 copy-start
  107.7 5.6 %all-to-all-start.2 = ((bf16[32,72,128]{2,1,0:T(8,128)(2,1)}), bf16[32,72,128]{2,1,0:T(8,128)(2,1)S(1)}, u32[]{:S(2)}, u32[]{:S(2)}) async-start(bf16[32,72,128]{2,1,0:T(8,128)(2,1)} %get-tuple-element.11), calls=%async_computation.2 | async-start | bytes 1179648 | tf_op jit(solution)/shard_map/all_to_all | solution.py:266
  113.4 3.4 %collective-permute-start.1 = (bf16[12,144,128]{2,1,0:T(8,128)(2,1)}, bf16[12,144,128]{2,1,0:T(8,128)(2,1)S(1)}, u32[]{:S(2)}, u32[]{:S(2)}) collective-permute-start(bf16[12,144,128]{2,1,0:T(8,128)(2,1)} %get-tuple-element.15), channel_id=1, source_target_pairs={{0,2},{2,0},{1,3},{3,1},{4,6},{6,4},{5,7},{7,5},{8,10},{10,8},{9,1... | collective-permute-start | bytes 1327112 | tf_op jit(solution)/shard_map/ppermute | solution.py:260
  116.7 1.9 %collective-permute-start = (bf16[10,144,128]{2,1,0:T(8,128)(2,1)}, bf16[10,144,128]{2,1,0:T(8,128)(2,1)S(1)}, u32[]{:S(2)}, u32[]{:S(2)}) collective-permute-start(bf16[10,144,128]{2,1,0:T(8,128)(2,1)} %get-tuple-element.14), channel_id=1, source_target_pairs={{0,1},{1,0},{2,3},{3,2},{4,5},{5,4},{6,7},{7,6},{8,9},{9,8},{10,11... | collective-permute-start | bytes 1105928 | tf_op jit(solution)/shard_map/ppermute | solution.py:261
  118.7 1.9 %collective-permute-done.after_hbm.near_ref = bf16[10,144,128]{2,1,0:T(8,128)(2,1)S(1)} collective-permute-done((bf16[10,144,128]{2,1,0:T(8,128)(2,1)}, bf16[10,144,128]{2,1,0:T(8,128)(2,1)S(1)}, u32[]{:S(2)}, u32[]{:S(2)}) %collective-permute-start) | collective-permute-done | bytes 368672 | tf_op jit(solution)/shard_map/ppermute | solution.py:261
  120.5 5.9 %collective-permute-done.1.far_ref = bf16[12,144,128]{2,1,0:T(8,128)(2,1)S(1)} collective-permute-done((bf16[12,144,128]{2,1,0:T(8,128)(2,1)}, bf16[12,144,128]{2,1,0:T(8,128)(2,1)S(1)}, u32[]{:S(2)}, u32[]{:S(2)}) %collective-permute-start.1) | collective-permute-done | bytes 442400 | tf_op jit(solution)/shard_map/ppermute | solution.py:260
  126.5 0.2 forward.1
  126.6 1.9 %collective-permute-start.2 = (bf16[10,144,128]{2,1,0:T(8,128)(2,1)S(1)}, bf16[10,144,128]{2,1,0:T(8,128)(2,1)S(1)}, u32[]{:S(2)}, u32[]{:S(2)}) collective-permute-start(bf16[10,144,128]{2,1,0:T(8,128)(2,1)S(1)} %forward.1), channel_id=1, source_target_pairs={{0,1},{1,0},{2,3},{3,2},{4,5},{5,4},{6,7},{7,6},{8,9},{9,8},{10,11... | collective-permute-start | bytes 1105928 | tf_op jit(solution)/shard_map/ppermute | solution.py:265
  128.6 0.0 all-gather.4.cloned.1.call-done
  128.6 0.0 copy-start.1
  128.6 1.7 %copy-done.1 = bf16[128,72,128]{2,1,0:T(8,128)(2,1)S(1)} copy-done((bf16[128,72,128]{2,1,0:T(8,128)(2,1)S(1)}, bf16[128,72,128]{2,1,0:T(8,128)(2,1)}, u32[]{:S(2)}) %copy-start.1) | copy-done | bytes 2359320
  130.3 1.7 %unpack.1 = (bf16[288,512]{1,0:T(8,128)(2,1)S(1)}, bf16[1152,512]{1,0:T(8,128)(2,1)S(1)}) custom-call(bf16[4,32,72,128]{3,2,1,0:T(8,128)(2,1)S(1)} %bitcast.2), custom_call_target="tpu_custom_call" | custom-call | flops 679477248 | bytes 2359296 | tf_op jit(solution)/shard_map/unpack/pallas_call | solution.py:193
  132.0 0.0 collective-permute-done.2.far_near_ref
  132.0 0.0 copy-done
  132.0 2.0 %weight_grads.1 = (bf16[288,1152]{1,0:T(8,128)(2,1)}, bf16[288,1152]{1,0:T(8,128)(2,1)}) custom-call(bf16[288,512]{1,0:T(8,128)(2,1)S(1)} %get-tuple-element.12.acts_ref, bf16[1152,512]{1,0:T(8,128)(2,1)S(1)} %get-tuple-element.13.cots_ref, bf16[8,288,128]{2,1,0:T(8,128)(2,1)S(1)} %copy-done, ...), custom_call_target="tpu_custom_call" | custom-call | flops 679477248 | bytes 3244032 | tf_op jit(solution)/shard_map/weight_grads/pallas_call | solution.py:193
  134.0 2.3 %all-to-all-done.2 = bf16[32,72,128]{2,1,0:T(8,128)(2,1)S(1)} async-done(((bf16[32,72,128]{2,1,0:T(8,128)(2,1)}), bf16[32,72,128]{2,1,0:T(8,128)(2,1)S(1)}, u32[]{:S(2)}, u32[]{:S(2)}) %all-to-all-start.2) | async-done | bytes 589856 | tf_op jit(solution)/shard_map/all_to_all | solution.py:266
  136.3 0.1 reduce_sum.22
  136.4 0.6 fusion.1
  (2 shorter events, 0.1 us)
Async XLA Ops:
  63.8 21.2 %all-to-all-start = ((bf16[8,288,128]{2,1,0:T(8,128)(2,1)}), bf16[8,288,128]{2,1,0:T(8,128)(2,1)S(1)}, u32[]{:S(2)}, u32[]{:S(2)}) async-start(bf16[8,288,128]{2,1,0:T(8,128)(2,1)} %unit_terms.1), calls=%async_computation | async-start | bytes 1179648 | tf_op jit(solution)/shard_map/all_to_all | solution.py:237
  70.9 57.7 %all-gather.4.cloned.1.call-start = ((), (), s32[]{:S(2)}) async-start(), calls=%async_computation.3 | async-start | bytes 2949120 | tf_op jit(solution)/shard_map/all_gather | solution.py:221
  107.7 24.3 %copy-start = (bf16[8,288,128]{2,1,0:T(8,128)(2,1)S(1)}, bf16[8,288,128]{2,1,0:T(8,128)(2,1)}, u32[]{:S(2)}) copy-start(bf16[8,288,128]{2,1,0:T(8,128)(2,1)} %all_to_all.15.both_hbm.both_ref) | copy-start | bytes 1769476
  107.7 28.6 %all-to-all-start.2 = ((bf16[32,72,128]{2,1,0:T(8,128)(2,1)}), bf16[32,72,128]{2,1,0:T(8,128)(2,1)S(1)}, u32[]{:S(2)}, u32[]{:S(2)}) async-start(bf16[32,72,128]{2,1,0:T(8,128)(2,1)} %get-tuple-element.11), calls=%async_computation.2 | async-start | bytes 1179648 | tf_op jit(solution)/shard_map/all_to_all | solution.py:266
  113.4 13.1 %collective-permute-start.1 = (bf16[12,144,128]{2,1,0:T(8,128)(2,1)}, bf16[12,144,128]{2,1,0:T(8,128)(2,1)S(1)}, u32[]{:S(2)}, u32[]{:S(2)}) collective-permute-start(bf16[12,144,128]{2,1,0:T(8,128)(2,1)} %get-tuple-element.15), channel_id=1, source_target_pairs={{0,2},{2,0},{1,3},{3,1},{4,6},{6,4},{5,7},{7,5},{8,10},{10,8},{9,1... | collective-permute-start | bytes 1327112 | tf_op jit(solution)/shard_map/ppermute | solution.py:260
  116.7 3.8 %collective-permute-start = (bf16[10,144,128]{2,1,0:T(8,128)(2,1)}, bf16[10,144,128]{2,1,0:T(8,128)(2,1)S(1)}, u32[]{:S(2)}, u32[]{:S(2)}) collective-permute-start(bf16[10,144,128]{2,1,0:T(8,128)(2,1)} %get-tuple-element.14), channel_id=1, source_target_pairs={{0,1},{1,0},{2,3},{3,2},{4,5},{5,4},{6,7},{7,6},{8,9},{9,8},{10,11... | collective-permute-start | bytes 1105928 | tf_op jit(solution)/shard_map/ppermute | solution.py:261
  126.6 5.3 %collective-permute-start.2 = (bf16[10,144,128]{2,1,0:T(8,128)(2,1)S(1)}, bf16[10,144,128]{2,1,0:T(8,128)(2,1)S(1)}, u32[]{:S(2)}, u32[]{:S(2)}) collective-permute-start(bf16[10,144,128]{2,1,0:T(8,128)(2,1)S(1)} %forward.1), channel_id=1, source_target_pairs={{0,1},{1,0},{2,3},{3,2},{4,5},{5,4},{6,7},{7,6},{8,9},{9,8},{10,11... | collective-permute-start | bytes 1105928 | tf_op jit(solution)/shard_map/ppermute | solution.py:265
  128.6 1.7 %copy-start.1 = (bf16[128,72,128]{2,1,0:T(8,128)(2,1)S(1)}, bf16[128,72,128]{2,1,0:T(8,128)(2,1)}, u32[]{:S(2)}) copy-start(bf16[128,72,128]{2,1,0:T(8,128)(2,1)} %all-gather.4.cloned.1.call-done) | copy-start | bytes 7077892
Sparse Core Ops, SparseCore 0:
  74.4 30.1 all-gather.3

commit v7 on v6

--- a/solution.py
+++ b/solution.py
@@ -35,8 +35,8 @@
 
 
 def unit_terms(
-    block_hbm, in_hbm, out_hbm, parts_hbm,
-    block_ref, parts_ref, in_ref, out_ref, acts_ref, cots_ref, pair_ref, sems,
+    block_hbm, in_hbm, out_hbm, parts_hbm, own_hbm, near_hbm, far_hbm,
+    block_ref, parts_ref, features_ref, in_ref, out_ref, acts_ref, cots_ref, pair_ref, sems, feature_sems,
 ):
     load = pltpu.make_async_copy(block_hbm, block_ref, sems.at[0])
     load_in = pltpu.make_async_copy(in_hbm, in_ref, sems.at[1])
@@ -51,15 +51,38 @@
         acts_ref[g * own : (g + 1) * own] = pair_ref[:own]
         cots_ref[g * own : (g + 1) * own] = pair_ref[own:]
     cots, acts = cots_ref[...].astype(BF16), turned(acts_ref[...])
+    pieces = features_ref.shape[0] // 2
+    rows = features_ref.shape[1]
+    for k in range(pieces):
+        features_ref[k] = cots_ref[k * rows : (k + 1) * rows].astype(BF16)
+        features_ref[pieces + k] = acts_ref[k * rows : (k + 1) * rows].astype(BF16)
+    quarter, half = near_hbm.shape[0] - pieces, far_hbm.shape[0] - pieces
+    stores = []
+    for i, (target, start, count) in enumerate(
+        [
+            (near_hbm, relative(1) * quarter, quarter),
+            (far_hbm, (1 - lax.axis_index("xh")) * half, half),
+            (own_hbm, relative(0) * quarter, quarter),
+        ]
+    ):
+        stores.append(
+            pltpu.make_async_copy(features_ref.at[pl.ds(0, pieces)], target.at[pl.ds(0, pieces)], feature_sems.at[2 * i])
+        )
+        stores.append(
+            pltpu.make_async_copy(
+                features_ref.at[pl.ds(pieces + start, count)], target.at[pl.ds(pieces, count)], feature_sems.at[2 * i + 1]
+            )
+        )
     pre_ref = acts_ref
     load_in.wait()
+    for store in stores:
+        store.start()
     columns_dot(acts, in_ref, pre_ref)
     shares, share = parts_ref.shape[0], parts_ref.shape[1] // 2
     for k in range(shares):
         parts_ref[k, :share] = pre_ref[k * share : (k + 1) * share].astype(BF16)
     load_out.wait()
     each = 2
-    stores = []
     for k in range(0, shares, each):
         grad = dot(out_ref[k * share : (k + each) * share], cots, ((1,), (0,))).astype(BF16)
         for j in range(each):
@@ -71,8 +94,21 @@
         store.wait()
 
 
+def activate(parts_ref, near_hbm, far_hbm, copies_ref):
+    shares, share = parts_ref.shape[0], parts_ref.shape[1] // 2
+    total = parts_ref[0].astype(F32)
+    for k in range(1, shares):
+        total = total + parts_ref[k].astype(F32)
+    pre, grad_hidden = total[:share], total[share:]
+    hidden = jax.nn.silu(pre).astype(BF16)
+    grad_pre = (grad_hidden * silu_slope(pre)).astype(BF16)
+    for k in range(shares):
+        copies_ref[k, :share] = hidden
+        copies_ref[k, share:] = grad_pre
+
+
 def feature_terms(
-    both_hbm, in_hbm, out_hbm, sums_hbm, near_hbm, far_hbm,
+    both_hbm, in_hbm, out_hbm, after_hbm, sums_hbm, near_hbm, far_hbm,
     both_ref, sums_ref, in_ref, out_ref, out_rows_ref, in_rows_ref, pair_ref, sems,
 ):
     shares, share = both_ref.shape[0], both_ref.shape[1] // 2
@@ -122,29 +158,6 @@
     return 2 * (1 - xh if step & 2 else xh) + (1 - core if step & 1 else core)
 
 
-def unpack(block_hbm, acts_out, cots_out, block_ref, acts_ref, cots_ref, pair_ref, sems):
-    groups, members, rows, tokens = block_ref.shape
-    own = rows // 2
-    copies = [
-        pltpu.make_async_copy(block_hbm.at[relative(t)], block_ref.at[t], sems.at[t])
-        for t in range(groups)
-    ]
-    for copy in copies:
-        copy.start()
-    owner = relative(0)
-    for t in range(groups):
-        copies[t].wait()
-        lanes = slice(t * tokens, (t + 1) * tokens)
-        for g in range(members):
-            pair_ref[...] = block_ref[t, g].astype(F32)
-            cots_ref[g * own : (g + 1) * own] = pair_ref[own:]
-        cots_out[:, lanes] = cots_ref[...].astype(BF16)
-        for g in range(members // groups):
-            pair_ref[...] = block_ref[t, owner * (members // groups) + g].astype(F32)
-            acts_ref[g * own : (g + 1) * own] = pair_ref[:own]
-        acts_out[:, lanes] = acts_ref[...].astype(BF16)
-
-
 def forward(far_ref, after_hbm, out_ref, sems):
     pieces = far_ref.shape[0] - out_ref.shape[0]
     shares = out_ref.shape[0] - pieces
@@ -159,33 +172,37 @@
         copy.wait()
 
 
-def weight_grads(factor, acts_ref, cots_ref, both_ref, near_ref, far_ref, far_near_ref, in_ref, out_ref):
+def weight_grads(
+    factor, own_features_ref, near_features_ref, far_features_ref, far_near_features_ref,
+    both_ref, near_ref, far_ref, far_near_ref, in_ref, out_ref,
+):
     shares, share = both_ref.shape[0], both_ref.shape[1] // 2
     pieces = out_ref.shape[0] // share
     owner, core = relative(0), lax.axis_index("core")
+    far_place = shares + core * pieces
+
+    def chunks(ref, place, count):
+        return jnp.concatenate([ref[place + k] for k in range(count)], axis=0)
+
+    def quarters(refs, places):
+        return [chunks(ref, place, pieces) for ref, place in zip(refs, places)]
+
+    def products(left, right, to_ref):
+        width = 384
+        for at in range(0, to_ref.shape[1], width):
+            part = dot(left, right[at : at + width], ((1,), (1,))) * factor
+            to_ref[:, at : at + width] = part.astype(BF16)
+
+    features = (own_features_ref, near_features_ref, far_features_ref, far_near_features_ref)
     others = (near_ref, far_ref, far_near_ref)
-    acts = acts_ref[...]
+    acts = jnp.concatenate(quarters(features, (shares, shares, far_place, shares)), axis=1)
     own_grads = jnp.concatenate([both_ref[k, share:] for k in range(shares)], axis=0)
-    grads = jnp.concatenate(
-        [own_grads] + [jnp.concatenate([ref[k] for k in range(shares)], axis=0) for ref in others], axis=1
-    )
-    width = 384
-    for at in range(0, in_ref.shape[1], width):
-        part = grads[at : at + width]
-        in_ref[:, at : at + width] = (dot(acts, part, ((1,), (1,))) * factor).astype(BF16)
-    places = (shares, shares + core * pieces, shares)
+    grads = jnp.concatenate([own_grads] + [chunks(ref, 0, shares) for ref in others], axis=1)
+    products(acts, grads, in_ref)
     own_hidden = jnp.concatenate([both_ref[owner * pieces + j, :share] for j in range(pieces)], axis=0)
-    hidden = jnp.concatenate(
-        [own_hidden]
-        + [
-            jnp.concatenate([ref[place + j] for j in range(pieces)], axis=0)
-            for ref, place in zip(others, places)
-        ],
-        axis=1,
-    )
-    for at in range(0, out_ref.shape[1], width):
-        part = cots_ref[at : at + width]
-        out_ref[:, at : at + width] = (dot(hidden, part, ((1,), (1,))) * factor).astype(BF16)
+    hidden = jnp.concatenate([own_hidden] + quarters(others, (shares, far_place, shares)), axis=1)
+    cots = jnp.concatenate([chunks(ref, 0, shares) for ref in features], axis=1)
+    products(hidden, cots, out_ref)
 
 
 def call(kernel, name, outs, scratch, sems, args, in_hbm, flops, vmem, out_hbm=()):
@@ -202,9 +219,14 @@
     )(*args)
 
 
-def spread(local, axes):
-    copies = jnp.broadcast_to(local[None], (lax.axis_size(axes), *local.shape))
-    return lax.all_to_all(copies, axes, 0, 0, tiled=True)
+def exchange(near, far):
+    swap = [(0, 1), (1, 0)]
+    far = lax.ppermute(far, "xh", swap)
+    near = lax.ppermute(near, "core", swap)
+    (far_near,) = call(
+        forward, "forward", (jax.ShapeDtypeStruct(near.shape, BF16),), [], [(2,)], (far, near), (1,), 0, 32
+    )
+    return near, far, lax.ppermute(far_near, "core", swap)
 
 
 def body(activations, weight_in, weight_out, cotangent):
@@ -218,73 +240,53 @@
     pair = jnp.concatenate([activations, cotangent], axis=0)
     block = lax.all_gather(pair, "z", axis=0, tiled=False)
     block = lax.all_gather(block, "xl", axis=0, tiled=True)
-    block_all = lax.all_gather(block, DEV, axis=0, tiled=False)
-
     weight = (weight_in.shape, BF16)
     rows = ((feats, tokens), F32)
-    (parts,) = call(
+    near_shape = jax.ShapeDtypeStruct((n_gy + n_gy // n_dev, share, tokens), BF16)
+    far_shape = jax.ShapeDtypeStruct((n_gy + n_gy // 2, share, tokens), BF16)
+    parts, own_features, near, far = call(
         unit_terms,
         "unit_terms",
-        (jax.ShapeDtypeStruct((n_gy, 2 * share, tokens), BF16),),
-        [((n_gx, *pair_rows), BF16), ((n_gy, 2 * share, tokens), BF16), weight, weight, rows, rows, (pair_rows, F32)],
-        [(3 + n_gy // 2,)],
+        (jax.ShapeDtypeStruct((n_gy, 2 * share, tokens), BF16), near_shape, near_shape, far_shape),
+        [((n_gx, *pair_rows), BF16), ((n_gy, 2 * share, tokens), BF16), ((2 * n_gy, feats // n_gy, tokens), BF16), weight, weight, rows, rows, (pair_rows, F32)],
+        [(3 + n_gy // 2,), (6,)],
         (block, weight_in, weight_out),
         (0, 1, 2),
         products,
         62,
-        (0,),
-    )
+        (0, 1, 2, 3),
+    )
+    near_features, far_features, far_near_features = exchange(near, far)
     parts = lax.all_to_all(parts, "gy", 0, 0, tiled=True)
-    total = jnp.sum(parts.astype(F32), axis=0)
-    pre, grad_hidden = total[:share], total[share:]
-    hidden = jax.nn.silu(pre).astype(BF16)
-    grad_pre = (grad_hidden * silu_slope(pre)).astype(BF16)
-    both = spread(jnp.concatenate([hidden, grad_pre], axis=0), "gy").reshape(n_gy, 2 * share, tokens)
+    (both,) = call(
+        activate,
+        "activate",
+        (jax.ShapeDtypeStruct(parts.shape, BF16),),
+        [],
+        [],
+        (parts, near_features, far_features),
+        (1, 2),
+        0,
+        32,
+    )
+    both = lax.all_to_all(both, "gy", 0, 0, tiled=True)
+
     sums, near, far = call(
         feature_terms,
         "feature_terms",
-        (
-            jax.ShapeDtypeStruct((n_gx, *pair_rows), BF16),
-            jax.ShapeDtypeStruct((n_gy + n_gy // n_dev, share, tokens), BF16),
-            jax.ShapeDtypeStruct((n_gy + n_gy // 2, share, tokens), BF16),
-        ),
+        (jax.ShapeDtypeStruct((n_gx, *pair_rows), BF16), near_shape, far_shape),
         [((n_gy, 2 * share, tokens), BF16), ((n_gx, *pair_rows), BF16), weight, weight, rows, rows, (pair_rows, F32)],
         [(11,)],
-        (both, weight_in, weight_out),
-        (0, 1, 2),
+        (both, weight_in, weight_out, far_near_features),
+        (0, 1, 2, 3),
         products,
         62,
         (0, 1, 2),
     )
-    swap = [(0, 1), (1, 0)]
-    far = lax.ppermute(far, "xh", swap)
-    near = lax.ppermute(near, "core", swap)
-    (far_near,) = call(
-        forward, "forward", (jax.ShapeDtypeStruct(near.shape, BF16),), [], [(2,)], (far, near), (1,), 0, 32
-    )
-    far_near = lax.ppermute(far_near, "core", swap)
+    near, far, far_near = exchange(near, far)
     sums = lax.all_to_all(sums, GX, 0, 0, tiled=True)
     sums = jnp.sum(sums.astype(F32), axis=0).astype(BF16)
 
-    acts_own, cots_all = call(
-        unpack,
-        "unpack",
-        (
-            jax.ShapeDtypeStruct((feats // n_dev, n_dev * tokens), BF16),
-            jax.ShapeDtypeStruct((feats, n_dev * tokens), BF16),
-        ),
-        [
-            (block_all.shape, BF16),
-            ((feats // n_dev, tokens), F32),
-            ((feats, tokens), F32),
-            (pair_rows, F32),
-        ],
-        [(n_dev,)],
-        (block_all,),
-        (0,),
-        products,
-        40,
-    )
     grads = call(
         functools.partial(weight_grads, 1.0 / math.sqrt(n_dev * tokens)),
         "weight_grads",
@@ -294,7 +296,7 @@
         ),
         [],
         [],
-        (acts_own, cots_all, both, near, far, far_near),
+        (own_features, near_features, far_features, far_near_features, both, near, far, far_near),
         (),
         products,
         32,

time: 145 us -> 144 us (level)
  the two profiles are of different devices: /device:TPU:6 before, /device:TPU:64 now
where the time goes in v7:
time: 144 us; the launch traced here: 143 us
  blocking collectives  48.2 us (33%)
  waiting for transfers between devices  41.2 us (29%)
  starting transfers between devices  35.7 us (25%)
  Pallas kernels  13.3 us (9%)
  local copies, waits for them, and re-layouts  3.41 us (2%)
    all_gather x1, blocking collectives, body(): block = lax.all_gather(pair, 'z', axis=0, tiled=False)  40.8 us
    pallas_call x6, Pallas kernels, call(): pl.pallas_call(kernel, out_shape=outs, in_specs=[pl.BlockSpec(memory_spac...  13.3 us
    all_to_all x1, waiting for transfers between devices, body(): both = lax.all_to_all(both, 'gy', 0, 0, tiled=True)  12.3 us
    ppermute x2, waiting for transfers between devices, exchange(): far = lax.ppermute(far, 'xh', swap)  10.3 us
    all_to_all x1, waiting for transfers between devices, body(): sums = lax.all_to_all(sums, GX, 0, 0, tiled=True)  9.55 us
    ppermute x2, starting transfers between devices, exchange(): far = lax.ppermute(far, 'xh', swap)  8.89 us
    all_gather x1, blocking collectives, body(): block = lax.all_gather(block, 'xl', axis=0, tiled=True)  7.49 us
    all_to_all x1, starting transfers between devices, body(): parts = lax.all_to_all(parts, 'gy', 0, 0, tiled=True)  7.11 us
  transfers between devices with their start and end apart: 9, of which 9 were waited for; matrix products, arithmetic and copies ran while one was open for 0% of the time, Pallas kernels for 2%

profile of v7, /device:TPU:64, one launch (start us, length us, event | category | flops | bytes accessed | tf_op | source)
XLA Modules:
  0.0 143.4 jit_solution(9619252815537287510)
XLA Ops:
  0.6 0.7 pad_maximum_fusion
  1.4 40.8 %all-gather = bf16[1152,128]{1,0:T(8,128)(2,1)S(1)} all-gather(bf16[72,128]{1,0:T(8,128)(2,1)S(1)} %pad_maximum_fusion), channel_id=2, replica_groups=mesh['xl'=2,'z'=16,'gy'=8,'xh'=2,'core'=2] {'z'}, dimensions={0}, use_global_device_ids=true | all-gather | bytes 313344 | tf_op jit(solution)/shard_map/all_gather | solution.py:241
  42.1 7.5 %all_gather.11.block_hbm = bf16[32,72,128]{2,1,0:T(8,128)(2,1)} all-gather(bf16[16,72,128]{2,1,0:T(8,128)(2,1)S(1)} %bitcast.1), channel_id=1, replica_groups=mesh['xl'=2,'z'=16,'gy'=8,'xh'=2,'core'=2] {'xl'}, dimensions={0}, use_global_device_ids=true | all-gather | bytes 884736 | tf_op jit(solution)/shard_map/all_gather | solution.py:242
  49.6 4.6 %unit_terms.1 = (bf16[8,288,128]{2,1,0:T(8,128)(2,1)}, bf16[10,144,128]{2,1,0:T(8,128)(2,1)}, bf16[10,144,128]{2,1,0:T(8,128)(2,1)}, bf16[12,144,128]{2,1,0:T(8,128)(2,1)}) custom-call(bf16[32,72,128]{2,1,0:T(8,128)(2,1)} %all_gather.11.block_hbm, bf16[1152,1152]{1,0:T(8,128)(2,1)} %in_hbm.3, bf16[1152,1152]{1,0:T(8,128)(2,1)} %out_hbm.3), custom_call_target="tpu_custom_call" | custom-call | flops 679477248 | bytes 5898240 | tf_op jit(solution)/shard_map/unit_terms/pallas_call | solution.py:210
  54.3 7.1 %all-to-all-start = ((bf16[8,288,128]{2,1,0:T(8,128)(2,1)}), bf16[8,288,128]{2,1,0:T(8,128)(2,1)S(1)}, u32[]{:S(2)}, u32[]{:S(2)}) async-start(bf16[8,288,128]{2,1,0:T(8,128)(2,1)} %get-tuple-element.13), calls=%async_computation | async-start | bytes 1179648 | tf_op jit(solution)/shard_map/all_to_all | solution.py:260
  61.4 4.9 %collective-permute-start.1 = (bf16[12,144,128]{2,1,0:T(8,128)(2,1)}, bf16[12,144,128]{2,1,0:T(8,128)(2,1)S(1)}, u32[]{:S(2)}, u32[]{:S(2)}) collective-permute-start(bf16[12,144,128]{2,1,0:T(8,128)(2,1)} %get-tuple-element.15), channel_id=1, source_target_pairs={{0,2},{2,0},{1,3},{3,1},{4,6},{6,4},{5,7},{7,5},{8,10},{10,8},{9,1... | collective-permute-start | bytes 1327112 | tf_op jit(solution)/shard_map/ppermute | solution.py:224
  66.3 1.9 %collective-permute-start = (bf16[10,144,128]{2,1,0:T(8,128)(2,1)}, bf16[10,144,128]{2,1,0:T(8,128)(2,1)S(1)}, u32[]{:S(2)}, u32[]{:S(2)}) collective-permute-start(bf16[10,144,128]{2,1,0:T(8,128)(2,1)} %get-tuple-element.14), channel_id=1, source_target_pairs={{0,1},{1,0},{2,3},{3,2},{4,5},{5,4},{6,7},{7,6},{8,9},{9,8},{10,11... | collective-permute-start | bytes 1105928 | tf_op jit(solution)/shard_map/ppermute | solution.py:225
  68.2 1.9 %collective-permute-done.near_hbm.after_hbm.near_features_ref = bf16[10,144,128]{2,1,0:T(8,128)(2,1)S(1)} collective-permute-done((bf16[10,144,128]{2,1,0:T(8,128)(2,1)}, bf16[10,144,128]{2,1,0:T(8,128)(2,1)S(1)}, u32[]{:S(2)}, u32[]{:S(2)}) %collective-permute-start) | collective-permute-done | bytes 368672 | tf_op jit(solution)/shard_map/ppermute | solution.py:225
  70.1 3.2 %collective-permute-done.1.far_hbm.far_ref.far_features_ref = bf16[12,144,128]{2,1,0:T(8,128)(2,1)S(1)} collective-permute-done((bf16[12,144,128]{2,1,0:T(8,128)(2,1)}, bf16[12,144,128]{2,1,0:T(8,128)(2,1)S(1)}, u32[]{:S(2)}, u32[]{:S(2)}) %collective-permute-start.1) | collective-permute-done | bytes 442400 | tf_op jit(solution)/shard_map/ppermute | solution.py:224
  73.3 2.1 %all-to-all-done.parts_ref = bf16[8,288,128]{2,1,0:T(8,128)(2,1)S(1)} async-done(((bf16[8,288,128]{2,1,0:T(8,128)(2,1)}), bf16[8,288,128]{2,1,0:T(8,128)(2,1)S(1)}, u32[]{:S(2)}, u32[]{:S(2)}) %all-to-all-start) | async-done | bytes 589856 | tf_op jit(solution)/shard_map/all_to_all | solution.py:260
  75.4 0.9 activate.1
  76.3 5.1 %all-to-all-start.1 = ((bf16[8,288,128]{2,1,0:T(8,128)(2,1)}), bf16[8,288,128]{2,1,0:T(8,128)(2,1)S(1)}, u32[]{:S(2)}, u32[]{:S(2)}) async-start(bf16[8,288,128]{2,1,0:T(8,128)(2,1)} %activate.1), calls=%async_computation.1 | async-start | bytes 1179648 | tf_op jit(solution)/shard_map/all_to_all | solution.py:272
  81.4 0.2 forward.2
  81.6 1.9 %collective-permute-start.2 = (bf16[10,144,128]{2,1,0:T(8,128)(2,1)S(1)}, bf16[10,144,128]{2,1,0:T(8,128)(2,1)S(1)}, u32[]{:S(2)}, u32[]{:S(2)}) collective-permute-start(bf16[10,144,128]{2,1,0:T(8,128)(2,1)S(1)} %forward.2), channel_id=1, source_target_pairs={{0,1},{1,0},{2,3},{3,2},{4,5},{5,4},{6,7},{7,6},{8,9},{9,8},{10,11... | collective-permute-start | bytes 1105928 | tf_op jit(solution)/shard_map/ppermute | solution.py:229
  83.5 1.7 %collective-permute-done.2.after_hbm.far_near_features_ref = bf16[10,144,128]{2,1,0:T(8,128)(2,1)S(1)} collective-permute-done((bf16[10,144,128]{2,1,0:T(8,128)(2,1)S(1)}, bf16[10,144,128]{2,1,0:T(8,128)(2,1)S(1)}, u32[]{:S(2)}, u32[]{:S(2)}) %collective-permute-start.2) | collective-permute-done | bytes 368672 | tf_op jit(solution)/shard_map/ppermute | solution.py:229
  85.2 12.3 %all-to-all-done.1.both_hbm.both_ref = bf16[8,288,128]{2,1,0:T(8,128)(2,1)S(1)} async-done(((bf16[8,288,128]{2,1,0:T(8,128)(2,1)}), bf16[8,288,128]{2,1,0:T(8,128)(2,1)S(1)}, u32[]{:S(2)}, u32[]{:S(2)}) %all-to-all-start.1) | async-done | bytes 589856 | tf_op jit(solution)/shard_map/all_to_all | solution.py:272
  97.4 0.8 copy-done
  98.2 5.4 %feature_terms.1 = (bf16[32,72,128]{2,1,0:T(8,128)(2,1)}, bf16[10,144,128]{2,1,0:T(8,128)(2,1)}, bf16[12,144,128]{2,1,0:T(8,128)(2,1)}) custom-call(bf16[8,288,128]{2,1,0:T(8,128)(2,1)} %copy-done, bf16[1152,1152]{1,0:T(8,128)(2,1)} %in_hbm.3, bf16[1152,1152]{1,0:T(8,128)(2,1)} %out_hbm.3, bf16[10,144,128]{2,1,0:T(8,128)(2,1)} %copy-done.2), custom_call_target="tpu_custom_call" | custom-call | flops 679477248 | bytes 6266880 | tf_op jit(solution)/shard_map/feature_terms/pallas_call | solution.py:210
  103.7 6.9 %all-to-all-start.2 = ((bf16[32,72,128]{2,1,0:T(8,128)(2,1)}), bf16[32,72,128]{2,1,0:T(8,128)(2,1)S(1)}, u32[]{:S(2)}, u32[]{:S(2)}) async-start(bf16[32,72,128]{2,1,0:T(8,128)(2,1)} %get-tuple-element.16), calls=%async_computation.2 | async-start | bytes 1179648 | tf_op jit(solution)/shard_map/all_to_all | solution.py:287
  110.6 4.0 %collective-permute-start.4 = (bf16[12,144,128]{2,1,0:T(8,128)(2,1)}, bf16[12,144,128]{2,1,0:T(8,128)(2,1)S(1)}, u32[]{:S(2)}, u32[]{:S(2)}) collective-permute-start(bf16[12,144,128]{2,1,0:T(8,128)(2,1)} %get-tuple-element.19), channel_id=1, source_target_pairs={{0,2},{2,0},{1,3},{3,1},{4,6},{6,4},{5,7},{7,5},{8,10},{10,8},{9,1... | collective-permute-start | bytes 1327112 | tf_op jit(solution)/shard_map/ppermute | solution.py:224
  114.5 1.9 %collective-permute-start.3 = (bf16[10,144,128]{2,1,0:T(8,128)(2,1)}, bf16[10,144,128]{2,1,0:T(8,128)(2,1)S(1)}, u32[]{:S(2)}, u32[]{:S(2)}) collective-permute-start(bf16[10,144,128]{2,1,0:T(8,128)(2,1)} %get-tuple-element.18), channel_id=1, source_target_pairs={{0,1},{1,0},{2,3},{3,2},{4,5},{5,4},{6,7},{7,6},{8,9},{9,8},{10,11... | collective-permute-start | bytes 1105928 | tf_op jit(solution)/shard_map/ppermute | solution.py:225
  116.5 1.9 %collective-permute-done.3.after_hbm.near_ref = bf16[10,144,128]{2,1,0:T(8,128)(2,1)S(1)} collective-permute-done((bf16[10,144,128]{2,1,0:T(8,128)(2,1)}, bf16[10,144,128]{2,1,0:T(8,128)(2,1)S(1)}, u32[]{:S(2)}, u32[]{:S(2)}) %collective-permute-start.3) | collective-permute-done | bytes 368672 | tf_op jit(solution)/shard_map/ppermute | solution.py:225
  118.3 7.1 %collective-permute-done.4.far_ref = bf16[12,144,128]{2,1,0:T(8,128)(2,1)S(1)} collective-permute-done((bf16[12,144,128]{2,1,0:T(8,128)(2,1)}, bf16[12,144,128]{2,1,0:T(8,128)(2,1)S(1)}, u32[]{:S(2)}, u32[]{:S(2)}) %collective-permute-start.4) | collective-permute-done | bytes 442400 | tf_op jit(solution)/shard_map/ppermute | solution.py:224
  125.4 0.2 forward.3
  125.6 1.9 %collective-permute-start.5 = (bf16[10,144,128]{2,1,0:T(8,128)(2,1)S(1)}, bf16[10,144,128]{2,1,0:T(8,128)(2,1)S(1)}, u32[]{:S(2)}, u32[]{:S(2)}) collective-permute-start(bf16[10,144,128]{2,1,0:T(8,128)(2,1)S(1)} %forward.3), channel_id=1, source_target_pairs={{0,1},{1,0},{2,3},{3,2},{4,5},{5,4},{6,7},{7,6},{8,9},{9,8},{10,11... | collective-permute-start | bytes 1105928 | tf_op jit(solution)/shard_map/ppermute | solution.py:229
  127.5 1.7 %collective-permute-done.5.far_near_ref = bf16[10,144,128]{2,1,0:T(8,128)(2,1)S(1)} collective-permute-done((bf16[10,144,128]{2,1,0:T(8,128)(2,1)S(1)}, bf16[10,144,128]{2,1,0:T(8,128)(2,1)S(1)}, u32[]{:S(2)}, u32[]{:S(2)}) %collective-permute-start.5) | collective-permute-done | bytes 368672 | tf_op jit(solution)/shard_map/ppermute | solution.py:229
  129.2 1.0 copy-done.3
  130.2 1.0 copy-done.4
  131.1 2.0 %weight_grads.1 = (bf16[288,1152]{1,0:T(8,128)(2,1)}, bf16[288,1152]{1,0:T(8,128)(2,1)}) custom-call(bf16[10,144,128]{2,1,0:T(8,128)(2,1)S(1)} %copy-done.4, bf16[10,144,128]{2,1,0:T(8,128)(2,1)S(1)} %collective-permute-done.near_hbm.after_hbm.near_features_ref, bf16[12,144,128]{2,1,0:T(8,128)(2,1)S(1)} %collective-permute-done.1.far_hbm.far_ref.far_features_ref, ...), custom_call_target="tpu_custom_call" | custom-call | flops 679477248 | bytes 3317760 | tf_op jit(solution)/shard_map/weight_grads/pallas_call | solution.py:210
  133.1 9.6 %all-to-all-done.2 = bf16[32,72,128]{2,1,0:T(8,128)(2,1)S(1)} async-done(((bf16[32,72,128]{2,1,0:T(8,128)(2,1)}), bf16[32,72,128]{2,1,0:T(8,128)(2,1)S(1)}, u32[]{:S(2)}, u32[]{:S(2)}) %all-to-all-start.2) | async-done | bytes 589856 | tf_op jit(solution)/shard_map/all_to_all | solution.py:287
  142.7 0.1 reduce_sum.12
  142.8 0.6 fusion
  (7 shorter events, 0.0 us)
Async XLA Ops:
  54.3 21.1 %all-to-all-start = ((bf16[8,288,128]{2,1,0:T(8,128)(2,1)}), bf16[8,288,128]{2,1,0:T(8,128)(2,1)S(1)}, u32[]{:S(2)}, u32[]{:S(2)}) async-start(bf16[8,288,128]{2,1,0:T(8,128)(2,1)} %get-tuple-element.13), calls=%async_computation | async-start | bytes 1179648 | tf_op jit(solution)/shard_map/all_to_all | solution.py:260
  61.4 11.9 %collective-permute-start.1 = (bf16[12,144,128]{2,1,0:T(8,128)(2,1)}, bf16[12,144,128]{2,1,0:T(8,128)(2,1)S(1)}, u32[]{:S(2)}, u32[]{:S(2)}) collective-permute-start(bf16[12,144,128]{2,1,0:T(8,128)(2,1)} %get-tuple-element.15), channel_id=1, source_target_pairs={{0,2},{2,0},{1,3},{3,1},{4,6},{6,4},{5,7},{7,5},{8,10},{10,8},{9,1... | collective-permute-start | bytes 1327112 | tf_op jit(solution)/shard_map/ppermute | solution.py:224
  66.3 3.8 %collective-permute-start = (bf16[10,144,128]{2,1,0:T(8,128)(2,1)}, bf16[10,144,128]{2,1,0:T(8,128)(2,1)S(1)}, u32[]{:S(2)}, u32[]{:S(2)}) collective-permute-start(bf16[10,144,128]{2,1,0:T(8,128)(2,1)} %get-tuple-element.14), channel_id=1, source_target_pairs={{0,1},{1,0},{2,3},{3,2},{4,5},{5,4},{6,7},{7,6},{8,9},{9,8},{10,11... | collective-permute-start | bytes 1105928 | tf_op jit(solution)/shard_map/ppermute | solution.py:225
  76.3 21.1 %all-to-all-start.1 = ((bf16[8,288,128]{2,1,0:T(8,128)(2,1)}), bf16[8,288,128]{2,1,0:T(8,128)(2,1)S(1)}, u32[]{:S(2)}, u32[]{:S(2)}) async-start(bf16[8,288,128]{2,1,0:T(8,128)(2,1)} %activate.1), calls=%async_computation.1 | async-start | bytes 1179648 | tf_op jit(solution)/shard_map/all_to_all | solution.py:272
  81.6 3.6 %collective-permute-start.2 = (bf16[10,144,128]{2,1,0:T(8,128)(2,1)S(1)}, bf16[10,144,128]{2,1,0:T(8,128)(2,1)S(1)}, u32[]{:S(2)}, u32[]{:S(2)}) collective-permute-start(bf16[10,144,128]{2,1,0:T(8,128)(2,1)S(1)} %forward.2), channel_id=1, source_target_pairs={{0,1},{1,0},{2,3},{3,2},{4,5},{5,4},{6,7},{7,6},{8,9},{9,8},{10,11... | collective-permute-start | bytes 1105928 | tf_op jit(solution)/shard_map/ppermute | solution.py:229
  85.2 12.3 %copy-start.2 = (bf16[10,144,128]{2,1,0:T(8,128)(2,1)}, bf16[10,144,128]{2,1,0:T(8,128)(2,1)S(1)}, u32[]{:S(2)}) copy-start(bf16[10,144,128]{2,1,0:T(8,128)(2,1)S(1)} %collective-permute-done.2.after_hbm.far_near_features_ref) | copy-start | bytes 1105924
  97.4 0.8 copy-start
  103.6 25.5 %copy-start.1 = (bf16[8,288,128]{2,1,0:T(8,128)(2,1)S(1)}, bf16[8,288,128]{2,1,0:T(8,128)(2,1)}, u32[]{:S(2)}) copy-start(bf16[8,288,128]{2,1,0:T(8,128)(2,1)} %copy-done) | copy-start | bytes 1769476
  103.7 39.0 %all-to-all-start.2 = ((bf16[32,72,128]{2,1,0:T(8,128)(2,1)}), bf16[32,72,128]{2,1,0:T(8,128)(2,1)S(1)}, u32[]{:S(2)}, u32[]{:S(2)}) async-start(bf16[32,72,128]{2,1,0:T(8,128)(2,1)} %get-tuple-element.16), calls=%async_computation.2 | async-start | bytes 1179648 | tf_op jit(solution)/shard_map/all_to_all | solution.py:287
  110.6 14.8 %collective-permute-start.4 = (bf16[12,144,128]{2,1,0:T(8,128)(2,1)}, bf16[12,144,128]{2,1,0:T(8,128)(2,1)S(1)}, u32[]{:S(2)}, u32[]{:S(2)}) collective-permute-start(bf16[12,144,128]{2,1,0:T(8,128)(2,1)} %get-tuple-element.19), channel_id=1, source_target_pairs={{0,2},{2,0},{1,3},{3,1},{4,6},{6,4},{5,7},{7,5},{8,10},{10,8},{9,1... | collective-permute-start | bytes 1327112 | tf_op jit(solution)/shard_map/ppermute | solution.py:224
  114.5 3.8 %collective-permute-start.3 = (bf16[10,144,128]{2,1,0:T(8,128)(2,1)}, bf16[10,144,128]{2,1,0:T(8,128)(2,1)S(1)}, u32[]{:S(2)}, u32[]{:S(2)}) collective-permute-start(bf16[10,144,128]{2,1,0:T(8,128)(2,1)} %get-tuple-element.18), channel_id=1, source_target_pairs={{0,1},{1,0},{2,3},{3,2},{4,5},{5,4},{6,7},{7,6},{8,9},{9,8},{10,11... | collective-permute-start | bytes 1105928 | tf_op jit(solution)/shard_map/ppermute | solution.py:225
  125.6 3.6 %collective-permute-start.5 = (bf16[10,144,128]{2,1,0:T(8,128)(2,1)S(1)}, bf16[10,144,128]{2,1,0:T(8,128)(2,1)S(1)}, u32[]{:S(2)}, u32[]{:S(2)}) collective-permute-start(bf16[10,144,128]{2,1,0:T(8,128)(2,1)S(1)} %forward.3), channel_id=1, source_target_pairs={{0,1},{1,0},{2,3},{3,2},{4,5},{5,4},{6,7},{7,6},{8,9},{9,8},{10,11... | collective-permute-start | bytes 1105928 | tf_op jit(solution)/shard_map/ppermute | solution.py:229
  129.2 1.0 copy-start.3
  130.2 1.0 copy-start.4

commit v8 on v7

--- a/solution.py
+++ b/solution.py
@@ -94,7 +94,7 @@
         store.wait()
 
 
-def activate(parts_ref, near_hbm, far_hbm, copies_ref):
+def activate(parts_ref, far_hbm, copies_ref):
     shares, share = parts_ref.shape[0], parts_ref.shape[1] // 2
     total = parts_ref[0].astype(F32)
     for k in range(1, shares):
@@ -264,8 +264,8 @@
         (jax.ShapeDtypeStruct(parts.shape, BF16),),
         [],
         [],
-        (parts, near_features, far_features),
-        (1, 2),
+        (parts, far_features),
+        (1,),
         0,
         32,
     )

time: 144 us -> 141 us (0.979)
  the two profiles are of different devices: /device:TPU:64 before, /device:TPU:6 now
where the time goes in v8:
time: 141 us; the launch traced here: 139 us
  blocking collectives  51.3 us (36%)
  waiting for transfers between devices  37 us (26%)
  starting transfers between devices  32.4 us (23%)
  Pallas kernels  13.3 us (9%)
  local copies, waits for them, and re-layouts  3.41 us (2%)
    all_gather x1, blocking collectives, body(): block = lax.all_gather(pair, 'z', axis=0, tiled=False)  43.8 us
    ppermute x2, waiting for transfers between devices, exchange(): far = lax.ppermute(far, 'xh', swap)  14.6 us
    pallas_call x6, Pallas kernels, call(): pl.pallas_call(kernel, out_shape=outs, in_specs=[pl.BlockSpec(memory_spac...  13.3 us
    all_gather x1, blocking collectives, body(): block = lax.all_gather(block, 'xl', axis=0, tiled=True)  7.49 us
    all_to_all x1, starting transfers between devices, body(): parts = lax.all_to_all(parts, 'gy', 0, 0, tiled=True)  7.24 us
    all_to_all x1, waiting for transfers between devices, body(): sums = lax.all_to_all(sums, GX, 0, 0, tiled=True)  6.93 us
    all_to_all x1, waiting for transfers between devices, body(): both = lax.all_to_all(both, 'gy', 0, 0, tiled=True)  6.64 us
    ppermute x2, starting transfers between devices, exchange(): far = lax.ppermute(far, 'xh', swap)  6.61 us
  transfers between devices with their start and end apart: 9, of which 9 were waited for; matrix products, arithmetic and copies ran while one was open for 0% of the time, Pallas kernels for 2%

profile of v8, /device:TPU:6, one launch (start us, length us, event | category | flops | bytes accessed | tf_op | source)
XLA Modules:
  0.0 139.0 jit_solution(16831064773621394047)
XLA Ops:
  0.6 0.7 pad_maximum_fusion
  1.4 43.8 %all-gather = bf16[1152,128]{1,0:T(8,128)(2,1)S(1)} all-gather(bf16[72,128]{1,0:T(8,128)(2,1)S(1)} %pad_maximum_fusion), channel_id=2, replica_groups=mesh['xl'=2,'z'=16,'gy'=8,'xh'=2,'core'=2] {'z'}, dimensions={0}, use_global_device_ids=true | all-gather | bytes 313344 | tf_op jit(solution)/shard_map/all_gather | solution.py:241
  45.1 7.5 %all_gather.11.block_hbm = bf16[32,72,128]{2,1,0:T(8,128)(2,1)} all-gather(bf16[16,72,128]{2,1,0:T(8,128)(2,1)S(1)} %bitcast.1), channel_id=1, replica_groups=mesh['xl'=2,'z'=16,'gy'=8,'xh'=2,'core'=2] {'xl'}, dimensions={0}, use_global_device_ids=true | all-gather | bytes 884736 | tf_op jit(solution)/shard_map/all_gather | solution.py:242
  52.6 4.6 %unit_terms.1 = (bf16[8,288,128]{2,1,0:T(8,128)(2,1)}, bf16[10,144,128]{2,1,0:T(8,128)(2,1)}, bf16[10,144,128]{2,1,0:T(8,128)(2,1)}, bf16[12,144,128]{2,1,0:T(8,128)(2,1)}) custom-call(bf16[32,72,128]{2,1,0:T(8,128)(2,1)} %all_gather.11.block_hbm, bf16[1152,1152]{1,0:T(8,128)(2,1)} %in_hbm.3, bf16[1152,1152]{1,0:T(8,128)(2,1)} %out_hbm.3), custom_call_target="tpu_custom_call" | custom-call | flops 679477248 | bytes 5898240 | tf_op jit(solution)/shard_map/unit_terms/pallas_call | solution.py:210
  57.3 7.2 %all-to-all-start = ((bf16[8,288,128]{2,1,0:T(8,128)(2,1)}), bf16[8,288,128]{2,1,0:T(8,128)(2,1)S(1)}, u32[]{:S(2)}, u32[]{:S(2)}) async-start(bf16[8,288,128]{2,1,0:T(8,128)(2,1)} %get-tuple-element.13), calls=%async_computation | async-start | bytes 1179648 | tf_op jit(solution)/shard_map/all_to_all | solution.py:260
  64.5 3.3 %collective-permute-start = (bf16[12,144,128]{2,1,0:T(8,128)(2,1)}, bf16[12,144,128]{2,1,0:T(8,128)(2,1)S(1)}, u32[]{:S(2)}, u32[]{:S(2)}) collective-permute-start(bf16[12,144,128]{2,1,0:T(8,128)(2,1)} %get-tuple-element.14), channel_id=1, source_target_pairs={{0,2},{2,0},{1,3},{3,1},{4,6},{6,4},{5,7},{7,5},{8,10},{10,8},{9,1... | collective-permute-start | bytes 1327112 | tf_op jit(solution)/shard_map/ppermute | solution.py:224
  67.9 8.6 %collective-permute-done.far_hbm.far_ref.far_features_ref = bf16[12,144,128]{2,1,0:T(8,128)(2,1)S(1)} collective-permute-done((bf16[12,144,128]{2,1,0:T(8,128)(2,1)}, bf16[12,144,128]{2,1,0:T(8,128)(2,1)S(1)}, u32[]{:S(2)}, u32[]{:S(2)}) %collective-permute-start) | collective-permute-done | bytes 442400 | tf_op jit(solution)/shard_map/ppermute | solution.py:224
  76.4 2.1 %all-to-all-done.parts_ref = bf16[8,288,128]{2,1,0:T(8,128)(2,1)S(1)} async-done(((bf16[8,288,128]{2,1,0:T(8,128)(2,1)}), bf16[8,288,128]{2,1,0:T(8,128)(2,1)S(1)}, u32[]{:S(2)}, u32[]{:S(2)}) %all-to-all-start) | async-done | bytes 589856 | tf_op jit(solution)/shard_map/all_to_all | solution.py:260
  78.5 0.9 activate.1
  79.5 5.1 %all-to-all-start.1 = ((bf16[8,288,128]{2,1,0:T(8,128)(2,1)}), bf16[8,288,128]{2,1,0:T(8,128)(2,1)S(1)}, u32[]{:S(2)}, u32[]{:S(2)}) async-start(bf16[8,288,128]{2,1,0:T(8,128)(2,1)} %activate.1), calls=%async_computation.1 | async-start | bytes 1179648 | tf_op jit(solution)/shard_map/all_to_all | solution.py:272
  84.6 1.9 %collective-permute-start.1 = (bf16[10,144,128]{2,1,0:T(8,128)(2,1)S(1)}, bf16[10,144,128]{2,1,0:T(8,128)(2,1)S(1)}, u32[]{:S(2)}, u32[]{:S(2)}) collective-permute-start(bf16[10,144,128]{2,1,0:T(8,128)(2,1)S(1)} %copy-done.5), channel_id=1, source_target_pairs={{0,1},{1,0},{2,3},{3,2},{4,5},{5,4},{6,7},{7,6},{8,9},{9,8},{10,11... | collective-permute-start | bytes 1105928 | tf_op jit(solution)/shard_map/ppermute | solution.py:225
  86.5 1.7 %collective-permute-done.1.after_hbm.near_features_ref = bf16[10,144,128]{2,1,0:T(8,128)(2,1)S(1)} collective-permute-done((bf16[10,144,128]{2,1,0:T(8,128)(2,1)S(1)}, bf16[10,144,128]{2,1,0:T(8,128)(2,1)S(1)}, u32[]{:S(2)}, u32[]{:S(2)}) %collective-permute-start.1) | collective-permute-done | bytes 368672 | tf_op jit(solution)/shard_map/ppermute | solution.py:225
  88.2 0.2 forward.2
  88.3 2.0 %collective-permute-start.2 = (bf16[10,144,128]{2,1,0:T(8,128)(2,1)S(1)}, bf16[10,144,128]{2,1,0:T(8,128)(2,1)S(1)}, u32[]{:S(2)}, u32[]{:S(2)}) collective-permute-start(bf16[10,144,128]{2,1,0:T(8,128)(2,1)S(1)} %forward.2), channel_id=1, source_target_pairs={{0,1},{1,0},{2,3},{3,2},{4,5},{5,4},{6,7},{7,6},{8,9},{9,8},{10,11... | collective-permute-start | bytes 1105928 | tf_op jit(solution)/shard_map/ppermute | solution.py:229
  90.4 1.5 %collective-permute-done.2.after_hbm.far_near_features_ref = bf16[10,144,128]{2,1,0:T(8,128)(2,1)S(1)} collective-permute-done((bf16[10,144,128]{2,1,0:T(8,128)(2,1)S(1)}, bf16[10,144,128]{2,1,0:T(8,128)(2,1)S(1)}, u32[]{:S(2)}, u32[]{:S(2)}) %collective-permute-start.2) | collective-permute-done | bytes 368672 | tf_op jit(solution)/shard_map/ppermute | solution.py:229
  91.9 6.6 %all-to-all-done.1.both_hbm.both_ref = bf16[8,288,128]{2,1,0:T(8,128)(2,1)S(1)} async-done(((bf16[8,288,128]{2,1,0:T(8,128)(2,1)}), bf16[8,288,128]{2,1,0:T(8,128)(2,1)S(1)}, u32[]{:S(2)}, u32[]{:S(2)}) %all-to-all-start.1) | async-done | bytes 589856 | tf_op jit(solution)/shard_map/all_to_all | solution.py:272
  98.6 0.8 copy-done
  99.4 5.4 %feature_terms.1 = (bf16[32,72,128]{2,1,0:T(8,128)(2,1)}, bf16[10,144,128]{2,1,0:T(8,128)(2,1)}, bf16[12,144,128]{2,1,0:T(8,128)(2,1)}) custom-call(bf16[8,288,128]{2,1,0:T(8,128)(2,1)} %copy-done, bf16[1152,1152]{1,0:T(8,128)(2,1)} %in_hbm.3, bf16[1152,1152]{1,0:T(8,128)(2,1)} %out_hbm.3, bf16[10,144,128]{2,1,0:T(8,128)(2,1)} %copy-done.2), custom_call_target="tpu_custom_call" | custom-call | flops 679477248 | bytes 6266880 | tf_op jit(solution)/shard_map/feature_terms/pallas_call | solution.py:210
  104.8 5.7 %all-to-all-start.2 = ((bf16[32,72,128]{2,1,0:T(8,128)(2,1)}), bf16[32,72,128]{2,1,0:T(8,128)(2,1)S(1)}, u32[]{:S(2)}, u32[]{:S(2)}) async-start(bf16[32,72,128]{2,1,0:T(8,128)(2,1)} %get-tuple-element.16), calls=%async_computation.2 | async-start | bytes 1179648 | tf_op jit(solution)/shard_map/all_to_all | solution.py:287
  110.5 3.3 %collective-permute-start.4 = (bf16[12,144,128]{2,1,0:T(8,128)(2,1)}, bf16[12,144,128]{2,1,0:T(8,128)(2,1)S(1)}, u32[]{:S(2)}, u32[]{:S(2)}) collective-permute-start(bf16[12,144,128]{2,1,0:T(8,128)(2,1)} %get-tuple-element.19), channel_id=1, source_target_pairs={{0,2},{2,0},{1,3},{3,1},{4,6},{6,4},{5,7},{7,5},{8,10},{10,8},{9,1... | collective-permute-start | bytes 1327112 | tf_op jit(solution)/shard_map/ppermute | solution.py:224
  113.8 1.9 %collective-permute-start.3 = (bf16[10,144,128]{2,1,0:T(8,128)(2,1)}, bf16[10,144,128]{2,1,0:T(8,128)(2,1)S(1)}, u32[]{:S(2)}, u32[]{:S(2)}) collective-permute-start(bf16[10,144,128]{2,1,0:T(8,128)(2,1)} %get-tuple-element.18), channel_id=1, source_target_pairs={{0,1},{1,0},{2,3},{3,2},{4,5},{5,4},{6,7},{7,6},{8,9},{9,8},{10,11... | collective-permute-start | bytes 1105928 | tf_op jit(solution)/shard_map/ppermute | solution.py:225
  115.7 1.9 %collective-permute-done.3.after_hbm.near_ref = bf16[10,144,128]{2,1,0:T(8,128)(2,1)S(1)} collective-permute-done((bf16[10,144,128]{2,1,0:T(8,128)(2,1)}, bf16[10,144,128]{2,1,0:T(8,128)(2,1)S(1)}, u32[]{:S(2)}, u32[]{:S(2)}) %collective-permute-start.3) | collective-permute-done | bytes 368672 | tf_op jit(solution)/shard_map/ppermute | solution.py:225
  117.6 6.0 %collective-permute-done.4.far_ref = bf16[12,144,128]{2,1,0:T(8,128)(2,1)S(1)} collective-permute-done((bf16[12,144,128]{2,1,0:T(8,128)(2,1)}, bf16[12,144,128]{2,1,0:T(8,128)(2,1)S(1)}, u32[]{:S(2)}, u32[]{:S(2)}) %collective-permute-start.4) | collective-permute-done | bytes 442400 | tf_op jit(solution)/shard_map/ppermute | solution.py:224
  123.6 0.2 forward.3
  123.8 1.9 %collective-permute-start.5 = (bf16[10,144,128]{2,1,0:T(8,128)(2,1)S(1)}, bf16[10,144,128]{2,1,0:T(8,128)(2,1)S(1)}, u32[]{:S(2)}, u32[]{:S(2)}) collective-permute-start(bf16[10,144,128]{2,1,0:T(8,128)(2,1)S(1)} %forward.3), channel_id=1, source_target_pairs={{0,1},{1,0},{2,3},{3,2},{4,5},{5,4},{6,7},{7,6},{8,9},{9,8},{10,11... | collective-permute-start | bytes 1105928 | tf_op jit(solution)/shard_map/ppermute | solution.py:229
  125.7 1.7 %collective-permute-done.5.far_near_ref = bf16[10,144,128]{2,1,0:T(8,128)(2,1)S(1)} collective-permute-done((bf16[10,144,128]{2,1,0:T(8,128)(2,1)S(1)}, bf16[10,144,128]{2,1,0:T(8,128)(2,1)S(1)}, u32[]{:S(2)}, u32[]{:S(2)}) %collective-permute-start.5) | collective-permute-done | bytes 368672 | tf_op jit(solution)/shard_map/ppermute | solution.py:229
  127.4 1.0 copy-done.3
  128.4 1.0 copy-done.4
  129.3 2.0 %weight_grads.1 = (bf16[288,1152]{1,0:T(8,128)(2,1)}, bf16[288,1152]{1,0:T(8,128)(2,1)}) custom-call(bf16[10,144,128]{2,1,0:T(8,128)(2,1)S(1)} %copy-done.4, bf16[10,144,128]{2,1,0:T(8,128)(2,1)S(1)} %collective-permute-done.1.after_hbm.near_features_ref, bf16[12,144,128]{2,1,0:T(8,128)(2,1)S(1)} %collective-permute-done.far_hbm.far_ref.far_features_ref, ...), custom_call_target="tpu_custom_call" | custom-call | flops 679477248 | bytes 3317760 | tf_op jit(solution)/shard_map/weight_grads/pallas_call | solution.py:210
  131.3 6.9 %all-to-all-done.2 = bf16[32,72,128]{2,1,0:T(8,128)(2,1)S(1)} async-done(((bf16[32,72,128]{2,1,0:T(8,128)(2,1)}), bf16[32,72,128]{2,1,0:T(8,128)(2,1)S(1)}, u32[]{:S(2)}, u32[]{:S(2)}) %all-to-all-start.2) | async-done | bytes 589856 | tf_op jit(solution)/shard_map/all_to_all | solution.py:287
  138.3 0.1 reduce_sum.12
  138.4 0.6 fusion
  (9 shorter events, 0.0 us)
Async XLA Ops:
  57.3 27.3 %copy-start.5 = (bf16[10,144,128]{2,1,0:T(8,128)(2,1)S(1)}, bf16[10,144,128]{2,1,0:T(8,128)(2,1)}, u32[]{:S(2)}) copy-start(bf16[10,144,128]{2,1,0:T(8,128)(2,1)} %get-tuple-element.15) | copy-start | bytes 1105924
  57.3 21.2 %all-to-all-start = ((bf16[8,288,128]{2,1,0:T(8,128)(2,1)}), bf16[8,288,128]{2,1,0:T(8,128)(2,1)S(1)}, u32[]{:S(2)}, u32[]{:S(2)}) async-start(bf16[8,288,128]{2,1,0:T(8,128)(2,1)} %get-tuple-element.13), calls=%async_computation | async-start | bytes 1179648 | tf_op jit(solution)/shard_map/all_to_all | solution.py:260
  64.5 11.9 %collective-permute-start = (bf16[12,144,128]{2,1,0:T(8,128)(2,1)}, bf16[12,144,128]{2,1,0:T(8,128)(2,1)S(1)}, u32[]{:S(2)}, u32[]{:S(2)}) collective-permute-start(bf16[12,144,128]{2,1,0:T(8,128)(2,1)} %get-tuple-element.14), channel_id=1, source_target_pairs={{0,2},{2,0},{1,3},{3,1},{4,6},{6,4},{5,7},{7,5},{8,10},{10,8},{9,1... | collective-permute-start | bytes 1327112 | tf_op jit(solution)/shard_map/ppermute | solution.py:224
  79.5 19.1 %all-to-all-start.1 = ((bf16[8,288,128]{2,1,0:T(8,128)(2,1)}), bf16[8,288,128]{2,1,0:T(8,128)(2,1)S(1)}, u32[]{:S(2)}, u32[]{:S(2)}) async-start(bf16[8,288,128]{2,1,0:T(8,128)(2,1)} %activate.1), calls=%async_computation.1 | async-start | bytes 1179648 | tf_op jit(solution)/shard_map/all_to_all | solution.py:272
  84.6 3.6 %collective-permute-start.1 = (bf16[10,144,128]{2,1,0:T(8,128)(2,1)S(1)}, bf16[10,144,128]{2,1,0:T(8,128)(2,1)S(1)}, u32[]{:S(2)}, u32[]{:S(2)}) collective-permute-start(bf16[10,144,128]{2,1,0:T(8,128)(2,1)S(1)} %copy-done.5), channel_id=1, source_target_pairs={{0,1},{1,0},{2,3},{3,2},{4,5},{5,4},{6,7},{7,6},{8,9},{9,8},{10,11... | collective-permute-start | bytes 1105928 | tf_op jit(solution)/shard_map/ppermute | solution.py:225
  88.3 3.6 %collective-permute-start.2 = (bf16[10,144,128]{2,1,0:T(8,128)(2,1)S(1)}, bf16[10,144,128]{2,1,0:T(8,128)(2,1)S(1)}, u32[]{:S(2)}, u32[]{:S(2)}) collective-permute-start(bf16[10,144,128]{2,1,0:T(8,128)(2,1)S(1)} %forward.2), channel_id=1, source_target_pairs={{0,1},{1,0},{2,3},{3,2},{4,5},{5,4},{6,7},{7,6},{8,9},{9,8},{10,11... | collective-permute-start | bytes 1105928 | tf_op jit(solution)/shard_map/ppermute | solution.py:229
  91.9 6.6 %copy-start.2 = (bf16[10,144,128]{2,1,0:T(8,128)(2,1)}, bf16[10,144,128]{2,1,0:T(8,128)(2,1)S(1)}, u32[]{:S(2)}) copy-start(bf16[10,144,128]{2,1,0:T(8,128)(2,1)S(1)} %collective-permute-done.2.after_hbm.far_near_features_ref) | copy-start | bytes 1105924
  98.6 0.8 copy-start
  104.8 22.6 %copy-start.1 = (bf16[8,288,128]{2,1,0:T(8,128)(2,1)S(1)}, bf16[8,288,128]{2,1,0:T(8,128)(2,1)}, u32[]{:S(2)}) copy-start(bf16[8,288,128]{2,1,0:T(8,128)(2,1)} %copy-done) | copy-start | bytes 1769476
  104.8 33.5 %all-to-all-start.2 = ((bf16[32,72,128]{2,1,0:T(8,128)(2,1)}), bf16[32,72,128]{2,1,0:T(8,128)(2,1)S(1)}, u32[]{:S(2)}, u32[]{:S(2)}) async-start(bf16[32,72,128]{2,1,0:T(8,128)(2,1)} %get-tuple-element.16), calls=%async_computation.2 | async-start | bytes 1179648 | tf_op jit(solution)/shard_map/all_to_all | solution.py:287
  110.5 13.1 %collective-permute-start.4 = (bf16[12,144,128]{2,1,0:T(8,128)(2,1)}, bf16[12,144,128]{2,1,0:T(8,128)(2,1)S(1)}, u32[]{:S(2)}, u32[]{:S(2)}) collective-permute-start(bf16[12,144,128]{2,1,0:T(8,128)(2,1)} %get-tuple-element.19), channel_id=1, source_target_pairs={{0,2},{2,0},{1,3},{3,1},{4,6},{6,4},{5,7},{7,5},{8,10},{10,8},{9,1... | collective-permute-start | bytes 1327112 | tf_op jit(solution)/shard_map/ppermute | solution.py:224
  113.8 3.8 %collective-permute-start.3 = (bf16[10,144,128]{2,1,0:T(8,128)(2,1)}, bf16[10,144,128]{2,1,0:T(8,128)(2,1)S(1)}, u32[]{:S(2)}, u32[]{:S(2)}) collective-permute-start(bf16[10,144,128]{2,1,0:T(8,128)(2,1)} %get-tuple-element.18), channel_id=1, source_target_pairs={{0,1},{1,0},{2,3},{3,2},{4,5},{5,4},{6,7},{7,6},{8,9},{9,8},{10,11... | collective-permute-start | bytes 1105928 | tf_op jit(solution)/shard_map/ppermute | solution.py:225
  123.8 3.6 %collective-permute-start.5 = (bf16[10,144,128]{2,1,0:T(8,128)(2,1)S(1)}, bf16[10,144,128]{2,1,0:T(8,128)(2,1)S(1)}, u32[]{:S(2)}, u32[]{:S(2)}) collective-permute-start(bf16[10,144,128]{2,1,0:T(8,128)(2,1)S(1)} %forward.3), channel_id=1, source_target_pairs={{0,1},{1,0},{2,3},{3,2},{4,5},{5,4},{6,7},{7,6},{8,9},{9,8},{10,11... | collective-permute-start | bytes 1105928 | tf_op jit(solution)/shard_map/ppermute | solution.py:229
  127.4 1.0 copy-start.3
  128.4 1.0 copy-start.4
